TPU v7x, 32 devices: a whole 2x2x4 slice. The times are simulated.
32 devices in a mesh: seq: 8 (over y, x, core), dp: 4 (over z).
Axes of the slice: x: 2, y: 2, z: 4, core: 2. Of those that a mesh axis runs over, the one named last changes fastest.
Arguments:
- tokens: bfloat16 [4096, 1024], P(('dp', 'seq')), parts along dimension 0, may hold values from -6 to 6
- norm_gain: float32 [1024], replicated, may hold values from 0.1 to 1.9
- filters: float32 [12, 1024], P(None, 'seq'), may hold values from -0.1875 to 0.1875
- mixing: bfloat16 [12, 1024, 1024], P(None, 'seq'), may hold values from -0.0546875 to 0.0546875
Outputs:
- mixed: bfloat16 [4096, 1024], P(('dp', 'seq')), parts along dimension 0
There are 4 independent parts, one for each index of `dp`. A program takes and returns all parts, laid end to end along the dimension named above; an argument that names none is the same for every part. Nothing has to cross between parts.
All inputs are finite; a program needn't handle non-finite values.
Results may differ from a plain program's by a relative error of at most 0.0044.
Values may be sent and summed in bfloat16 or wider, within the bound.
No kernel may reach another device: no remote copies, remote signals or barrier semaphores. Data moves between devices by JAX's collectives and lax.ppermute only.
A program may use at most 192 MiB of HBM per device.

v0:
```python
import math

import jax
import jax.numpy as jnp
from jax import lax
from jax.sharding import PartitionSpec as P

radix = 128
highest = lax.Precision.HIGHEST


def cos_sin(rows, cols, total):
    left = lax.broadcasted_iota(jnp.int32, (rows, cols), 0)
    right = lax.broadcasted_iota(jnp.int32, (rows, cols), 1)
    angle = (left * right % total).astype(jnp.float32) * (2.0 * math.pi / total)
    return (jnp.cos(angle), jnp.sin(angle))


def make_tables(blocks):
    total = blocks * radix
    half = blocks // 2
    cos_outer, sin_outer = cos_sin(blocks, half, blocks)
    cos_twid, sin_twid = cos_sin(blocks, radix, total)
    cos_inner, sin_inner = cos_sin(radix, radix, radix)
    cos_back, sin_back = cos_sin(half, blocks, blocks)
    return (
        cos_outer,
        sin_outer,
        cos_twid,
        sin_twid,
        cos_inner,
        sin_inner,
        cos_back,
        sin_back,
        total,
    )


def forward(signal, tables):
    cos_outer, sin_outer, cos_twid, sin_twid, cos_inner, sin_inner, cos_back, sin_back, total = (
        tables
    )
    first_re = jnp.einsum("kn,cna->cka", cos_outer, signal, precision=highest)
    first_im = -jnp.einsum("kn,cna->cka", sin_outer, signal, precision=highest)
    twist_re = first_re * cos_twid + first_im * sin_twid
    twist_im = first_im * cos_twid - first_re * sin_twid
    out_re = jnp.einsum("cka,aj->ckj", twist_re, cos_inner, precision=highest) + jnp.einsum(
        "cka,aj->ckj", twist_im, sin_inner, precision=highest
    )
    out_im = jnp.einsum("cka,aj->ckj", twist_im, cos_inner, precision=highest) - jnp.einsum(
        "cka,aj->ckj", twist_re, sin_inner, precision=highest
    )
    return (out_re, out_im)


def inverse(spec_re, spec_im, tables):
    cos_outer, sin_outer, cos_twid, sin_twid, cos_inner, sin_inner, cos_back, sin_back, total = (
        tables
    )
    inner_re = jnp.einsum("ckj,aj->cka", spec_re, cos_inner, precision=highest) - jnp.einsum(
        "ckj,aj->cka", spec_im, sin_inner, precision=highest
    )
    inner_im = jnp.einsum("ckj,aj->cka", spec_im, cos_inner, precision=highest) + jnp.einsum(
        "ckj,aj->cka", spec_re, sin_inner, precision=highest
    )
    twist_re = inner_re * cos_twid - inner_im * sin_twid
    twist_im = inner_im * cos_twid + inner_re * sin_twid
    result = jnp.einsum("nk,cka->cna", cos_back, twist_re, precision=highest) - jnp.einsum(
        "nk,cka->cna", sin_back, twist_im, precision=highest
    )
    return result / total


def local(tokens, norm_gain, filters, mixing):
    tok_rows, width = tokens.shape
    groups = lax.axis_size("seq")
    values = tokens.astype(jnp.float32)
    scale_row = lax.rsqrt(jnp.mean(values * values, axis=1, keepdims=True) + 1e-05)
    normed = (values * scale_row * norm_gain).astype(jnp.bfloat16)
    taps = lax.all_gather(filters, "seq", axis=1, tiled=True)
    num_filters, length = taps.shape
    blocks = 2 * length // radix
    half = blocks // 2
    tables = make_tables(blocks)
    phi_re, phi_im = forward(taps.reshape(num_filters, half, radix), tables)
    grouped = normed.reshape(tok_rows, groups, width // groups)
    piece = lax.all_to_all(grouped, "seq", split_axis=1, concat_axis=0, tiled=True)
    count = piece.shape[2]
    signal = piece[:, 0, :].astype(jnp.float32).T.reshape(count, half, radix)
    sig_re, sig_im = forward(signal, tables)

    def per_filter(spectrum):
        filt_re, filt_im = spectrum
        prod_re = sig_re * filt_re - sig_im * filt_im
        prod_im = sig_re * filt_im + sig_im * filt_re
        return inverse(prod_re, prod_im, tables).reshape(count, length).astype(jnp.bfloat16)

    features = lax.map(per_filter, (phi_re, phi_im))
    back = lax.all_to_all(features, "seq", split_axis=2, concat_axis=1, tiled=True)
    branch = jnp.einsum(
        "kct,kcd->td",
        back,
        lax.all_gather(mixing, "seq", axis=1, tiled=True),
        preferred_element_type=jnp.float32,
    )
    return (values + branch).astype(jnp.bfloat16)


def solution(mesh):
    in_specs = (P(("dp", "seq"), None), P(), P(None, "seq"), P(None, "seq", None))
    out_specs = P(("dp", "seq"), None)
    return jax.shard_map(local, mesh=mesh, in_specs=in_specs, out_specs=out_specs, check_vma=False)
```

profile of v0, /device:TPU:0, one launch (start us, length us, event | category | flops | bytes accessed | tf_op | source)
XLA Modules:
  0.0 222.8 jit_solution(17295574809434882895)
XLA Ops:
  8.5 5.2 %all-to-all-start = ((bf16[128,8,128]{2,0,1:T(8,128)(2,1)}), bf16[128,8,128]{2,0,1:T(8,128)(2,1)S(1)}, u32[]{:S(2)}, u32[]{:S(2)}) async-start(bf16[128,8,128]{2,0,1:T(8,128)(2,1)} %copy_bitcast_fusion.1), calls=%async_computation | async-start | bytes 524288 | tf_op jit(solution)/shard_map/all_to_all | solution.py:87
  13.7 10.3 %all_gather.6 = f32[12,1024]{1,0:T(8,128)S(1)} all-gather(f32[12,128]{1,0:T(8,128)S(1)} %copy-done.1), channel_id=1, replica_groups=mesh['seq'=8,'dp'=4] {'seq'}, dimensions={1}, use_global_device_ids=true | all-gather | bytes 55296 | tf_op jit(solution)/shard_map/all_gather | solution.py:80
  28.4 1.4 fusion.83
  29.9 1.4 fusion.87
  31.3 1.4 convolution_subtract_fusion.2
  32.7 1.4 convolution_add_fusion.1
  34.2 103.7 %while.12 = (s32[]{:T(128)}, bf16[12,128,1024]{2,1,0:T(8,128)(2,1)}, f32[12,16,128]{2,1,0:T(8,128)S(1)}, f32[128,16,128]{2,0,1:T(8,128)S(1)}, f32[12,16,128]{2,1...) while((s32[]{:T(128)}, bf16[12,128,1024]{2,1,0:T(8,128)(2,1)}, ...), condition=%wide.region_2.3_spmd.clone.clone, body=%wide.region_1.2_spmd.clone.clone.sunk | while | flops 1667530240 | bytes 21365328 | solution.py:98
  35.6 1.3 convolution_add_fusion.4
  38.2 1.4 multiply_add_fusion.11
  39.6 1.3 fusion.225
  40.9 1.3 fusion.226
  44.2 1.3 convolution_add_fusion.4
  45.5 1.2 fusion.224
  46.8 1.4 multiply_add_fusion.11
  48.2 1.3 fusion.225
  49.5 1.3 fusion.226
  52.9 1.3 convolution_add_fusion.4
  54.2 1.2 fusion.224
  55.5 1.4 multiply_add_fusion.11
  56.9 1.3 fusion.225
  58.2 1.3 fusion.226
  61.5 1.3 convolution_add_fusion.4
  62.8 1.2 fusion.224
  64.1 1.4 multiply_add_fusion.11
  65.5 1.3 fusion.225
  66.8 1.3 fusion.226
  70.1 1.3 convolution_add_fusion.4
  72.7 1.4 multiply_add_fusion.11
  74.1 1.3 fusion.225
  75.4 1.3 fusion.226
  78.7 1.3 convolution_add_fusion.4
  81.3 1.4 multiply_add_fusion.11
  82.7 1.3 fusion.225
  84.0 1.3 fusion.226
  87.4 1.3 convolution_add_fusion.4
  90.0 1.4 multiply_add_fusion.11
  91.3 1.3 fusion.225
  92.6 1.3 fusion.226
  96.0 1.3 convolution_add_fusion.4
  97.3 1.2 fusion.224
  98.6 1.4 multiply_add_fusion.11
  100.0 1.3 fusion.225
  101.3 1.3 fusion.226
  104.6 1.3 convolution_add_fusion.4
  107.2 1.4 multiply_add_fusion.11
  108.6 1.3 fusion.225
  109.9 1.3 fusion.226
  113.2 1.3 convolution_add_fusion.4
  115.8 1.4 multiply_add_fusion.11
  117.2 1.3 fusion.225
  118.5 1.3 fusion.226
  121.8 1.3 convolution_add_fusion.4
  124.4 1.4 multiply_add_fusion.11
  125.8 1.3 fusion.225
  127.1 1.3 fusion.226
  130.5 1.3 convolution_add_fusion.4
  133.1 1.4 multiply_add_fusion.11
  134.4 1.3 fusion.225
  135.7 1.3 fusion.226
  137.8 6.8 %copy.21 = bf16[12,128,1024]{1,0,2:T(8,128)(2,1)} copy(bf16[12,128,1024]{2,1,0:T(8,128)(2,1)} %get-tuple-element.79) | data formatting | bytes 6291456 | tf_op jit(solution)/shard_map/while | solution.py:98
  144.6 52.7 %all_to_all.33 = bf16[12,128,1024]{1,0,2:T(8,128)(2,1)S(1)} all-to-all(bf16[12,128,1024]{1,0,2:T(8,128)(2,1)} %copy.21), channel_id=1, replica_groups=mesh['seq'=8,'dp'=4] {'seq'}, dimensions={2} | all-to-all | bytes 6291456 | tf_op jit(solution)/shard_map/all_to_all | solution.py:99
  197.3 3.7 %copy.40 = bf16[12,128,8,128]{1,2,3,0:T(8,128)(2,1)} copy(bf16[12,128,8,128]{1,0,3,2:T(8,128)(2,1)S(1)} %bitcast.118) | data formatting | bytes 6291456 | tf_op jit(solution)/shard_map/all_to_all | solution.py:99
  201.1 4.1 %all_to_all.30 = bf16[12,1024,128]{1,2,0:T(8,128)(2,1)S(1)} reshape(bf16[12,8,128,128]{2,1,3,0:T(8,128)(2,1)} %bitcast.119) | data formatting | bytes 6291456 | tf_op jit(solution)/shard_map/all_to_all | solution.py:99
  205.2 10.7 %fusion.82 = bf16[128,1024]{1,0:T(8,128)(2,1)} fusion(bf16[12,1024,128]{1,2,0:T(8,128)(2,1)S(1)} %all_to_all.30, bf16[12,1024,1024]{2,1,0:T(8,128)(2,1)} %all-gather.2.cloned.1.call-done, bf16[128,1024]{1,0:T(8,128)(2,1)S(1)} %copy-done), kind=kOutput, calls=%fused_computation.95 | convolution fusion | flops 3221618688 | bytes 28835840 | tf_op jit(solution)/shard_map/kct,kcd->td/dot_general | solution.py:100
  (94 shorter events, 42.0 us)
Async XLA Ops:
  6.5 0.9 copy-start
  6.5 1.1 copy-start.2
  6.5 7.1 %copy-start.1 = (f32[12,128]{1,0:T(8,128)S(1)}, f32[12,128]{1,0:T(8,128)}, u32[]{:S(2)}) copy-start(f32[12,128]{1,0:T(8,128)} %param.8) | copy-start | bytes 18436
  6.5 198.7 %all-gather.2.cloned.1.call-start = ((), (), s32[]{:S(2)}) async-start(), calls=%async_computation.2 | async-start | bytes 28311552 | tf_op jit(solution)/shard_map/all_gather | solution.py:103
  8.5 18.2 %all-to-all-start = ((bf16[128,8,128]{2,0,1:T(8,128)(2,1)}), bf16[128,8,128]{2,0,1:T(8,128)(2,1)S(1)}, u32[]{:S(2)}, u32[]{:S(2)}) async-start(bf16[128,8,128]{2,0,1:T(8,128)(2,1)} %copy_bitcast_fusion.1), calls=%async_computation | async-start | bytes 524288 | tf_op jit(solution)/shard_map/all_to_all | solution.py:87
Sparse Core Ops, SparseCore 0:
  9.3 128.0 all-gather.1
where the time goes:
time: 223 us
  matrix products  112 us (50%)
  blocking collectives  62.9 us (28%)
  local copies, waits for them, and re-layouts  25.2 us (11%)
  between operations  13.5 us (6%)
  starting transfers between devices  5.17 us (2%)
    all_to_all x1, blocking collectives, local(): lax.all_to_all(features, 'seq', split_axis=2, concat_axis=1, tiled=True)  52.7 us
    dot_general x12, matrix products, inverse(): jnp.einsum('ckj,aj->cka', spec_im, sin_inner, precision=highest)  16.7 us
    dot_general x12, matrix products, inverse(): jnp.einsum('nk,cka->cna', cos_back, twist_re, precision=highest)  15.3 us
    dot_general x12, matrix products, inverse(): jnp.einsum('ckj,aj->cka', spec_re, sin_inner, precision=highest)  15.2 us
    dot_general x12, matrix products, inverse(): jnp.einsum('nk,cka->cna', sin_back, twist_im, precision=highest)  15.1 us
    dot_general x12, matrix products, inverse(): jnp.einsum('ckj,aj->cka', spec_re, cos_inner, precision=highest)  15 us
    dot_general x12, matrix products, inverse(): jnp.einsum('ckj,aj->cka', spec_im, cos_inner, precision=highest)  14.8 us
    dot_general x1, matrix products, local(): jnp.einsum('kct,kcd->td', back, lax.all_gather(mixing, 'seq', axis=1, til...  10.7 us
  transfers between devices with their start and end apart: 2, of which 0 were waited for; matrix products, arithmetic and copies ran while one was open for 56% of the time, Pallas kernels for 0%

commit v1 on v0

v1 whole, which is shorter than its diff:
```python
import functools

import jax
import jax.numpy as jnp
from jax import lax
from jax.experimental import pallas as pl
from jax.experimental.pallas import tpu as pltpu
from jax.sharding import PartitionSpec as P

MIB = 1024 * 1024
EXTRA = 16
VMEM = pl.BlockSpec(memory_space=pltpu.VMEM)
SMEM = pl.BlockSpec(memory_space=pltpu.SMEM)
HBM = pl.BlockSpec(memory_space=pltpu.HBM)


def swap(value, bits, size):
    return lax.ppermute(value, "seq", [(i, i ^ bits) for i in range(size)])


def kernel_call(kernel, name, out_shape, specs, limit, scratch=()):
    return pl.pallas_call(
        kernel,
        out_shape=out_shape,
        in_specs=specs,
        out_specs=jax.tree.map(lambda _: VMEM, out_shape),
        scratch_shapes=scratch,
        compiler_params=pltpu.CompilerParams(vmem_limit_bytes=limit),
        name=name,
    )


def in_hbm(value):
    return pltpu.with_memory_space_constraint(value, pltpu.HBM)


def norm_kernel(tokens_hbm, gain_hbm, filters_hbm, *refs):
    *out_refs, tokens_ref, gain_ref, filters_ref, sems = refs
    pairs = ((filters_hbm, filters_ref), (gain_hbm, gain_ref), (tokens_hbm, tokens_ref))
    copies = [pltpu.make_async_copy(a, b, sems.at[i]) for i, (a, b) in enumerate(pairs)]
    for copy in copies:
        copy.start()
    chip = lax.axis_index("seq") // 2
    rows, width = tokens_ref.shape
    chips = len(out_refs)
    count = width // chips
    num, span = filters_ref.shape
    packed = out_refs[0].shape[0] > rows
    copies[0].wait()
    if packed:
        flip = (
            lax.broadcasted_iota(jnp.int32, (span, span), 0)
            + lax.broadcasted_iota(jnp.int32, (span, span), 1)
            == span - 1
        ).astype(jnp.bfloat16)
        taps = jnp.dot(
            filters_ref[...].astype(jnp.bfloat16), flip, preferred_element_type=jnp.float32
        )
        taps = jnp.concatenate([taps, jnp.zeros((EXTRA - num, span), jnp.float32)], axis=0)
        taps = jnp.concatenate([taps, jnp.zeros((EXTRA, count - span), jnp.float32)], axis=1)
        taps = taps.astype(jnp.bfloat16)
    copies[1].wait()
    copies[2].wait()
    values = tokens_ref[...].astype(jnp.float32)
    scale = lax.rsqrt(jnp.mean(values * values, axis=1, keepdims=True) + 1e-05)
    normed = (values * scale * gain_ref[...]).astype(jnp.bfloat16)
    for part in range(chips):
        for shift, out_ref in enumerate(out_refs):

            @pl.when(chip == part ^ shift)
            def _(part=part, out_ref=out_ref):
                out_ref[0:rows, :] = normed[:, part * count : (part + 1) * count]

    if packed:
        for out_ref in out_refs:
            out_ref[rows:, :] = taps


def strip_kernel(chips, rows, num, packed, *refs):
    own = refs[:chips]
    pair = refs[chips : 2 * chips]
    refs = refs[2 * chips :]
    mix_hbm, *refs = refs
    if not packed:
        taps_ref, *refs = refs
    signal, strip, mix_ref, base, sem = refs
    copy = pltpu.make_async_copy(mix_hbm, mix_ref, sem)
    copy.start()
    index = lax.axis_index("seq")
    chip = index // 2
    core = index % 2
    devices = 2 * chips
    length = devices * rows
    half = signal.shape[1] // 2
    wide = length + 2 * rows
    base[:, length:] = jnp.zeros((base.shape[0], 2 * rows), jnp.float32)
    for shift in range(chips):
        for which, block in enumerate((own[shift], pair[shift])):
            place = 2 * (chip ^ shift) + (core if which == 0 else 1 - core)
            value = block[0:rows, :]
            turned = jnp.concatenate([value[:, half:], value[:, :half]], axis=1)
            value = jnp.where(core == 0, value, turned)
            signal[pl.ds(pl.multiple_of(place * rows, rows), rows), :] = value
            if packed:
                at = pl.multiple_of((devices - 1 - place) * rows, rows)
                base[:, pl.ds(at, rows)] = block[rows:, 0:rows].astype(jnp.float32)
    if not packed:
        base[:, 0:length] = taps_ref[...]

    def one_filter(k, carry):
        line = jnp.broadcast_to(base[pl.ds(k, 1), :], (8, wide))
        line = pltpu.roll(line, wide - rows + 1, 1, stride=1, stride_axis=0)
        for step in range(rows // 16):
            pieces = [pltpu.roll(line, 16 * step + 8 * h, 1)[:, : length + rows] for h in (0, 1)]
            at = pl.multiple_of(k * rows + 16 * step, 16)
            strip[pl.ds(at, 16), :] = jnp.concatenate(pieces, axis=0).astype(jnp.bfloat16)
        return carry

    lax.fori_loop(0, num, one_filter, 0, unroll=3 if packed else 1)
    copy.wait()


def branch_kernel(chips, rows, shift, *refs):
    if shift is None:
        shift_ref, *refs = refs
        shift = shift_ref[0]
    signal, strip, mix_ref, pair_mix_ref, out_ref, feats = refs
    index = lax.axis_index("seq")
    core = index % 2
    other = (index // 2) ^ shift
    devices = 2 * chips
    num, half, width = mix_ref.shape
    count = 2 * half
    offset = (devices - 1 - (2 * other + core)) * rows
    if chips <= 4:

        def convolve(steps):
            depth = 2 * rows * steps
            left = strip[:, pl.ds(pl.multiple_of(offset, rows), depth)]
            total = jnp.dot(left, signal[0:depth, :], preferred_element_type=jnp.float32)
            for k in range(num):
                for which in range(2):
                    at = (which * num + k) * half
                    feats[:, at : at + half] = total[
                        k * rows : (k + 1) * rows, which * half : (which + 1) * half
                    ].astype(jnp.bfloat16)

        for steps in range(1, chips + 1):
            pl.when(other == steps - 1)(functools.partial(convolve, steps))
        both = num * half
        total = jnp.dot(
            feats[:, :both],
            mix_ref[...].reshape(both, width),
            preferred_element_type=jnp.float32,
        ) + jnp.dot(
            feats[:, both:],
            pair_mix_ref[...].reshape(both, width),
            preferred_element_type=jnp.float32,
        )
    else:
        feats[...] = jnp.zeros(feats.shape, jnp.float32)

        def add_tokens(step, carry):
            at = pl.multiple_of(2 * rows * step, 2 * rows)
            left = strip[:, pl.ds(pl.multiple_of(offset + at, rows), 2 * rows)]
            feats[...] += jnp.dot(
                left, signal[pl.ds(at, 2 * rows), :], preferred_element_type=jnp.float32
            )
            return carry

        lax.fori_loop(0, other + 1, add_tokens, 0)
        total = jnp.zeros((rows, width), jnp.float32)
        for k in range(num):
            found = feats[k * rows : (k + 1) * rows, :].astype(jnp.bfloat16)
            weight = jnp.concatenate([mix_ref[k], pair_mix_ref[k]], axis=0)
            total += jnp.dot(found, weight, preferred_element_type=jnp.float32)
    out_ref[...] = total.astype(out_ref.dtype)


def local(tokens, norm_gain, filters, mixing):
    rows, width = tokens.shape
    devices = lax.axis_size("seq")
    chips = devices // 2
    num, span = filters.shape
    length = devices * rows
    count = width // chips
    packed = count >= span
    few = chips <= 4
    pair_mixing = swap(mixing, 1, devices)
    tall = rows + (EXTRA if packed else 0)
    blocks = kernel_call(
        norm_kernel,
        "norm",
        [jax.ShapeDtypeStruct((tall, count), jnp.bfloat16)] * chips,
        [HBM] * 3,
        8 * MIB,
        [
            pltpu.VMEM((rows, width), tokens.dtype),
            pltpu.VMEM((1, width), norm_gain.dtype),
            pltpu.VMEM((num, span), filters.dtype),
            pltpu.SemaphoreType.DMA((3,)),
        ],
    )(in_hbm(tokens), in_hbm(norm_gain.reshape(1, width)), in_hbm(filters))
    far = [swap(blocks[s], 2 * s, devices) for s in reversed(range(1, chips))]
    own = [blocks[0], *reversed(far)]
    pair = [swap(block, 1, devices) for block in own]
    operands = [*own, *pair, in_hbm(mixing)]
    specs = [VMEM] * (2 * chips) + [HBM]
    if not packed:
        taps = lax.all_gather(filters, "seq", axis=1, tiled=True)[:, ::-1]
        operands.append(jnp.pad(taps, ((0, EXTRA - num), (0, 0))))
        specs.append(VMEM)
    signal, strip, near_mixing = kernel_call(
        functools.partial(strip_kernel, chips, rows, num, packed),
        "strip",
        [
            jax.ShapeDtypeStruct((length, count), jnp.bfloat16),
            jax.ShapeDtypeStruct((num * rows, length + rows), jnp.bfloat16),
            jax.ShapeDtypeStruct(mixing.shape, mixing.dtype),
        ],
        specs,
        16 * MIB if few else 48 * MIB,
        [pltpu.VMEM((EXTRA, length + 2 * rows), jnp.float32), pltpu.SemaphoreType.DMA(())],
    )(*operands)
    fixed = [signal, strip, near_mixing, pair_mixing]
    if few:

        def branch(shift, dtype):
            return kernel_call(
                functools.partial(branch_kernel, chips, rows, shift),
                "branch",
                jax.ShapeDtypeStruct((rows, width), dtype),
                [VMEM] * 4,
                24 * MIB,
                [pltpu.VMEM((rows, num * count), jnp.bfloat16)],
            )(*fixed)

        parts = {s: branch(s, jnp.bfloat16) for s in reversed(range(1, chips))}
        total = branch(0, jnp.float32)
    else:

        def branch(shift):
            return kernel_call(
                functools.partial(branch_kernel, chips, rows, None),
                "branch",
                jax.ShapeDtypeStruct((rows, width), jnp.bfloat16),
                [SMEM] + [VMEM] * 4,
                48 * MIB,
                [pltpu.VMEM((num * rows, count), jnp.float32)],
            )(shift.reshape(1), *fixed)

        parts = lax.map(branch, jnp.arange(chips, dtype=jnp.int32))
        total = parts[0].astype(jnp.float32)
        parts = {s: parts[s] for s in range(1, chips)}
    sent = [swap(value, 2 * s, devices) for s, value in parts.items()]
    total = tokens.astype(jnp.float32) + total
    for value in sent:
        total = total + value.astype(jnp.float32)
    return total.astype(jnp.bfloat16)


def solution(mesh):
    in_specs = (P(("dp", "seq"), None), P(), P(None, "seq"), P(None, "seq", None))
    out_specs = P(("dp", "seq"), None)
    return jax.shard_map(local, mesh=mesh, in_specs=in_specs, out_specs=out_specs, check_vma=False)
```

time: 223 us -> 32.6 us (0.15)
  matrix products: 112 us -> 0 us
  blocking collectives: 62.9 us -> 0 us
  local copies, waits for them, and re-layouts: 25.2 us -> 0.01 us
  between operations: 13.5 us -> 0.09 us
  waiting for transfers between devices: 0.73 us -> 13.2 us
  Pallas kernels: 0 us -> 10.4 us
  starting transfers between devices: 5.17 us -> 7.8 us
    dot_general x85 -> x0, matrix products: 112 us -> none  [the longest x12 16.7 us: inverse(): jnp.einsum('ckj,aj->cka', spec_im, sin_inner, precision=highest)]
    all_to_all x1 -> x0, blocking collectives: 52.7 us -> none  [local(): lax.all_to_all(features, 'seq', split_axis=2, concat_axis=1, tiled=True)]
    ppermute x0 -> x11, waiting for transfers between devices: none -> 13.2 us  [swap(): return lax.ppermute(value, 'seq', [(i, i ^ bits) for i in range(size)])]
    pallas_call x0 -> x6, Pallas kernels: none -> 10.4 us  [the longest x4 6.91 us: branch(): kernel_call(functools.partial(branch_kernel, chips, rows, shift), 'branch...]
    all_gather x1 -> x0, blocking collectives: 10.3 us -> none  [local(): taps = lax.all_gather(filters, 'seq', axis=1, tiled=True)]
    dynamic_update_slice x12 -> x0, local copies, waits for them, and re-layouts: 8.73 us -> none  [local(): features = lax.map(per_filter, (phi_re, phi_im))]
    all_to_all x2 -> x0, local copies, waits for them, and re-layouts: 7.87 us -> none  [local(): lax.all_to_all(features, 'seq', split_axis=2, concat_axis=1, tiled=True)]
    ppermute x0 -> x11, starting transfers between devices: none -> 7.8 us  [swap(): return lax.ppermute(value, 'seq', [(i, i ^ bits) for i in range(size)])]
  transfers between devices with their start and end apart: 2 -> 11, of which waited for: 0 -> 6; matrix products, arithmetic and copies ran while one was open for 56% -> 0% of each run, Pallas kernels for 0% -> 26%
where the time goes in v1:
time: 32.6 us; the launch traced here: 32.4 us
  waiting for transfers between devices  13.2 us (40%)
  Pallas kernels  10.4 us (32%)
  starting transfers between devices  7.8 us (24%)
  other arithmetic  0.9 us (3%)
    ppermute x11, waiting for transfers between devices, swap(): return lax.ppermute(value, 'seq', [(i, i ^ bits) for i in range(size)])  13.2 us
    ppermute x11, starting transfers between devices, swap(): return lax.ppermute(value, 'seq', [(i, i ^ bits) for i in range(size)])  7.8 us
    pallas_call x4, Pallas kernels, branch(): kernel_call(functools.partial(branch_kernel, chips, rows, shift), 'branch...  6.91 us
    pallas_call x1, Pallas kernels, local(): kernel_call(functools.partial(strip_kernel, chips, rows, num, packed), 's...  2.23 us
    pallas_call x1, Pallas kernels, local(): kernel_call(norm_kernel, 'norm', [jax.ShapeDtypeStruct((tall, count), jnp...  1.23 us
    convert_element_type x1, other arithmetic, local(): return total.astype(jnp.bfloat16)  0.9 us
  transfers between devices with their start and end apart: 11, of which 6 were waited for; matrix products, arithmetic and copies ran while one was open for 0% of the time, Pallas kernels for 26%

profile of v1, /device:TPU:0, one launch (start us, length us, event | category | flops | bytes accessed | tf_op | source)
XLA Modules:
  0.0 32.4 jit_solution(12022926680306770595)
XLA Ops:
  0.0 0.5 %collective-permute-start.7 = (bf16[12,128,1024]{2,1,0:T(8,128)(2,1)}, bf16[12,128,1024]{2,1,0:T(8,128)(2,1)S(1)}, u32[]{:S(2)}, u32[]{:S(2)}) collective-permute-start(bf16[12,128,1024]{2,1,0:T(8,128)(2,1)} %refs_8_.1), channel_id=1, source_target_pairs={{0,4},{4,0},{8,12},{12,8},{16,20},{20,16},{24,28},{28,24},{1,5},{5... | collective-permute-start | bytes 9437192 | tf_op jit(solution)/shard_map/ppermute | solution.py:18
  0.5 1.2 %norm.1 = (bf16[144,256]{1,0:T(8,128)(2,1)S(1)}, bf16[144,256]{1,0:T(8,128)(2,1)S(1)}, bf16[144,256]{1,0:T(8,128)(2,1)S(1)}, bf16[144,256]{1,0:T(8,128)(2,1)S(1)}) custom-call(bf16[128,1024]{1,0:T(8,128)(2,1)} %tokens_hbm.1, f32[1,1024]{1,0:T(1,128)} %bitcast.1, f32[12,128]{1,0:T(8,128)} %filters_hbm.1), custom_call_target="tpu_custom_call" | custom-call | tf_op jit(solution)/shard_map/norm/pallas_call | solution.py:191
  1.7 2.6 %collective-permute-start = (bf16[144,256]{1,0:T(8,128)(2,1)S(1)}, bf16[144,256]{1,0:T(8,128)(2,1)S(1)}, u32[]{:S(2)}, u32[]{:S(2)}) collective-permute-start(bf16[144,256]{1,0:T(8,128)(2,1)S(1)} %get-tuple-element.13), channel_id=1, source_target_pairs={{0,8},{4,12},{8,0},{12,4},{16,24},{20,28},{24,16},{28,20},{1,9},{5... | collective-permute-start | bytes 221192 | tf_op jit(solution)/shard_map/ppermute | solution.py:18
  4.2 1.5 %collective-permute-start.1 = (bf16[144,256]{1,0:T(8,128)(2,1)S(1)}, bf16[144,256]{1,0:T(8,128)(2,1)S(1)}, u32[]{:S(2)}, u32[]{:S(2)}) collective-permute-start(bf16[144,256]{1,0:T(8,128)(2,1)S(1)} %get-tuple-element.14), channel_id=1, source_target_pairs={{0,16},{4,20},{8,24},{12,28},{16,0},{20,4},{24,8},{28,12},{1,17},{... | collective-permute-start | bytes 221192 | tf_op jit(solution)/shard_map/ppermute | solution.py:18
  5.8 0.0 collective-permute-start.2
  5.8 0.0 collective-permute-start.3
  5.8 1.4 %collective-permute-done.refs_1_ = bf16[144,256]{1,0:T(8,128)(2,1)S(1)} collective-permute-done((bf16[144,256]{1,0:T(8,128)(2,1)S(1)}, bf16[144,256]{1,0:T(8,128)(2,1)S(1)}, u32[]{:S(2)}, u32[]{:S(2)}) %collective-permute-start) | collective-permute-done | bytes 73760 | tf_op jit(solution)/shard_map/ppermute | solution.py:18
  7.2 0.0 collective-permute-start.4
  7.2 1.7 %collective-permute-done.1.refs_2_ = bf16[144,256]{1,0:T(8,128)(2,1)S(1)} collective-permute-done((bf16[144,256]{1,0:T(8,128)(2,1)S(1)}, bf16[144,256]{1,0:T(8,128)(2,1)S(1)}, u32[]{:S(2)}, u32[]{:S(2)}) %collective-permute-start.1) | collective-permute-done | bytes 73760 | tf_op jit(solution)/shard_map/ppermute | solution.py:18
  8.9 0.0 collective-permute-start.5
  8.9 2.1 %collective-permute-done.2.refs_3_ = bf16[144,256]{1,0:T(8,128)(2,1)S(1)} collective-permute-done((bf16[144,256]{1,0:T(8,128)(2,1)S(1)}, bf16[144,256]{1,0:T(8,128)(2,1)S(1)}, u32[]{:S(2)}, u32[]{:S(2)}) %collective-permute-start.2) | collective-permute-done | bytes 73760 | tf_op jit(solution)/shard_map/ppermute | solution.py:18
  11.0 0.0 collective-permute-start.6
  11.0 0.0 collective-permute-done.3.refs_4_
  11.0 0.0 collective-permute-done.4.refs_5_
  11.0 0.0 collective-permute-done.5.refs_6_
  11.0 1.2 %collective-permute-done.6.refs_7_ = bf16[144,256]{1,0:T(8,128)(2,1)S(1)} collective-permute-done((bf16[144,256]{1,0:T(8,128)(2,1)S(1)}, bf16[144,256]{1,0:T(8,128)(2,1)S(1)}, u32[]{:S(2)}, u32[]{:S(2)}) %collective-permute-start.6) | collective-permute-done | bytes 73760 | tf_op jit(solution)/shard_map/ppermute | solution.py:18
  12.3 2.2 %strip.1 = (bf16[1024,256]{1,0:T(8,128)(2,1)S(1)}, bf16[1536,1152]{1,0:T(8,128)(2,1)S(1)}, bf16[12,128,1024]{2,1,0:T(8,128)(2,1)S(1)}) custom-call(bf16[144,256]{1,0:T(8,128)(2,1)S(1)} %get-tuple-element.12.refs_0_, bf16[144,256]{1,0:T(8,128)(2,1)S(1)} %collective-permute-done.refs_1_, bf16[144,256]{1,0:T(8,128)(2,1)S(1)} %collective-permute-done.1.refs_2_, ...), custom_call_target="tpu_custom_call" | custom-call | tf_op jit(solution)/shard_map/strip/pallas_call | solution.py:213
  14.5 0.0 collective-permute-done.7.refs_3_
  14.5 2.0 %branch.5 = bf16[128,1024]{1,0:T(8,128)(2,1)S(1)} custom-call(bf16[1024,256]{1,0:T(8,128)(2,1)S(1)} %get-tuple-element.16.refs_0_, bf16[1536,1152]{1,0:T(8,128)(2,1)S(1)} %get-tuple-element.17.refs_1_, bf16[12,128,1024]{2,1,0:T(8,128)(2,1)S(1)} %get-tuple-element.18.refs_2_, bf16[12,128,1024]{2,1,0:T(8,128)(2,1)S(1)} %collective-permute-done.7.refs_3_), custom_call_target="tpu_custom_call" | custom-call | tf_op jit(solution)/shard_map/branch/pallas_call | solution.py:229
  16.5 0.3 collective-permute-start.8
  16.8 1.8 %branch.6 = bf16[128,1024]{1,0:T(8,128)(2,1)S(1)} custom-call(bf16[1024,256]{1,0:T(8,128)(2,1)S(1)} %get-tuple-element.16.refs_0_, bf16[1536,1152]{1,0:T(8,128)(2,1)S(1)} %get-tuple-element.17.refs_1_, bf16[12,128,1024]{2,1,0:T(8,128)(2,1)S(1)} %get-tuple-element.18.refs_2_, bf16[12,128,1024]{2,1,0:T(8,128)(2,1)S(1)} %collective-permute-done.7.refs_3_), custom_call_target="tpu_custom_call" | custom-call | tf_op jit(solution)/shard_map/branch/pallas_call | solution.py:229
  18.6 1.2 %collective-permute-start.9 = (bf16[128,1024]{1,0:T(8,128)(2,1)S(1)}, bf16[128,1024]{1,0:T(8,128)(2,1)S(1)}, u32[]{:S(2)}, u32[]{:S(2)}) collective-permute-start(bf16[128,1024]{1,0:T(8,128)(2,1)S(1)} %branch.6), channel_id=1, source_target_pairs={{0,16},{4,20},{8,24},{12,28},{16,0},{20,4},{24,8},{28,12},{1,17},{... | collective-permute-start | bytes 786440 | tf_op jit(solution)/shard_map/ppermute | solution.py:18
  19.8 1.6 %branch.7 = bf16[128,1024]{1,0:T(8,128)(2,1)S(1)} custom-call(bf16[1024,256]{1,0:T(8,128)(2,1)S(1)} %get-tuple-element.16.refs_0_, bf16[1536,1152]{1,0:T(8,128)(2,1)S(1)} %get-tuple-element.17.refs_1_, bf16[12,128,1024]{2,1,0:T(8,128)(2,1)S(1)} %get-tuple-element.18.refs_2_, bf16[12,128,1024]{2,1,0:T(8,128)(2,1)S(1)} %collective-permute-done.7.refs_3_), custom_call_target="tpu_custom_call" | custom-call | tf_op jit(solution)/shard_map/branch/pallas_call | solution.py:229
  21.4 0.0 copy-start
  21.4 1.7 %collective-permute-start.10 = (bf16[128,1024]{1,0:T(8,128)(2,1)S(1)}, bf16[128,1024]{1,0:T(8,128)(2,1)S(1)}, u32[]{:S(2)}, u32[]{:S(2)}) collective-permute-start(bf16[128,1024]{1,0:T(8,128)(2,1)S(1)} %branch.7), channel_id=1, source_target_pairs={{0,8},{4,12},{8,0},{12,4},{16,24},{20,28},{24,16},{28,20},{1,9},{5... | collective-permute-start | bytes 786440 | tf_op jit(solution)/shard_map/ppermute | solution.py:18
  23.2 1.5 %branch.4 = f32[128,1024]{1,0:T(8,128)S(1)} custom-call(bf16[1024,256]{1,0:T(8,128)(2,1)S(1)} %get-tuple-element.16.refs_0_, bf16[1536,1152]{1,0:T(8,128)(2,1)S(1)} %get-tuple-element.17.refs_1_, bf16[12,128,1024]{2,1,0:T(8,128)(2,1)S(1)} %get-tuple-element.18.refs_2_, bf16[12,128,1024]{2,1,0:T(8,128)(2,1)S(1)} %collective-permute-done.7.refs_3_), custom_call_target="tpu_custom_call" | custom-call | tf_op jit(solution)/shard_map/branch/pallas_call | solution.py:229
  24.7 2.0 %collective-permute-done.8 = bf16[128,1024]{1,0:T(8,128)(2,1)S(1)} collective-permute-done((bf16[128,1024]{1,0:T(8,128)(2,1)S(1)}, bf16[128,1024]{1,0:T(8,128)(2,1)S(1)}, u32[]{:S(2)}, u32[]{:S(2)}) %collective-permute-start.8) | collective-permute-done | bytes 262176 | tf_op jit(solution)/shard_map/ppermute | solution.py:18
  26.7 4.8 %collective-permute-done.9 = bf16[128,1024]{1,0:T(8,128)(2,1)S(1)} collective-permute-done((bf16[128,1024]{1,0:T(8,128)(2,1)S(1)}, bf16[128,1024]{1,0:T(8,128)(2,1)S(1)}, u32[]{:S(2)}, u32[]{:S(2)}) %collective-permute-start.9) | collective-permute-done | bytes 262176 | tf_op jit(solution)/shard_map/ppermute | solution.py:18
  31.5 0.0 collective-permute-done.10
  31.5 0.0 copy-done
  31.5 0.9 %add_convert_fusion = bf16[128,1024]{1,0:T(8,128)(2,1)} fusion(bf16[128,1024]{1,0:T(8,128)(2,1)S(1)} %collective-permute-done.10, bf16[128,1024]{1,0:T(8,128)(2,1)S(1)} %collective-permute-done.9, bf16[128,1024]{1,0:T(8,128)(2,1)S(1)} %collective-permute-done.8, f32[128,1024]{1,0:T(8,128)S(1)} %branch.4, bf16[128,1024]{1,0:T(8,128)(2,1)S(1)} %copy-done), kind=kLoop, calls=%fused_computation | loop fusion | flops 1179648 | bytes 1835008 | tf_op jit(solution)/shard_map/convert_element_type | solution.py:259
Async XLA Ops:
  0.0 14.5 %collective-permute-start.7 = (bf16[12,128,1024]{2,1,0:T(8,128)(2,1)}, bf16[12,128,1024]{2,1,0:T(8,128)(2,1)S(1)}, u32[]{:S(2)}, u32[]{:S(2)}) collective-permute-start(bf16[12,128,1024]{2,1,0:T(8,128)(2,1)} %refs_8_.1), channel_id=1, source_target_pairs={{0,4},{4,0},{8,12},{12,8},{16,20},{20,16},{24,28},{28,24},{1,5},{5... | collective-permute-start | bytes 9437192 | tf_op jit(solution)/shard_map/ppermute | solution.py:18
  1.7 5.5 %collective-permute-start = (bf16[144,256]{1,0:T(8,128)(2,1)S(1)}, bf16[144,256]{1,0:T(8,128)(2,1)S(1)}, u32[]{:S(2)}, u32[]{:S(2)}) collective-permute-start(bf16[144,256]{1,0:T(8,128)(2,1)S(1)} %get-tuple-element.13), channel_id=1, source_target_pairs={{0,8},{4,12},{8,0},{12,4},{16,24},{20,28},{24,16},{28,20},{1,9},{5... | collective-permute-start | bytes 221192 | tf_op jit(solution)/shard_map/ppermute | solution.py:18
  4.2 4.7 %collective-permute-start.1 = (bf16[144,256]{1,0:T(8,128)(2,1)S(1)}, bf16[144,256]{1,0:T(8,128)(2,1)S(1)}, u32[]{:S(2)}, u32[]{:S(2)}) collective-permute-start(bf16[144,256]{1,0:T(8,128)(2,1)S(1)} %get-tuple-element.14), channel_id=1, source_target_pairs={{0,16},{4,20},{8,24},{12,28},{16,0},{20,4},{24,8},{28,12},{1,17},{... | collective-permute-start | bytes 221192 | tf_op jit(solution)/shard_map/ppermute | solution.py:18
  5.8 5.3 %collective-permute-start.2 = (bf16[144,256]{1,0:T(8,128)(2,1)S(1)}, bf16[144,256]{1,0:T(8,128)(2,1)S(1)}, u32[]{:S(2)}, u32[]{:S(2)}) collective-permute-start(bf16[144,256]{1,0:T(8,128)(2,1)S(1)} %get-tuple-element.15), channel_id=1, source_target_pairs={{0,24},{4,28},{8,16},{12,20},{16,8},{20,12},{24,0},{28,4},{1,25},{... | collective-permute-start | bytes 221192 | tf_op jit(solution)/shard_map/ppermute | solution.py:18
  5.8 5.2 %collective-permute-start.3 = (bf16[144,256]{1,0:T(8,128)(2,1)S(1)}, bf16[144,256]{1,0:T(8,128)(2,1)S(1)}, u32[]{:S(2)}, u32[]{:S(2)}) collective-permute-start(bf16[144,256]{1,0:T(8,128)(2,1)S(1)} %get-tuple-element.12.refs_0_), channel_id=1, source_target_pairs={{0,4},{4,0},{8,12},{12,8},{16,20},{20,16},{24,28},{28,24},{1,5},{5... | collective-permute-start | bytes 221192 | tf_op jit(solution)/shard_map/ppermute | solution.py:18
  7.2 3.8 %collective-permute-start.4 = (bf16[144,256]{1,0:T(8,128)(2,1)S(1)}, bf16[144,256]{1,0:T(8,128)(2,1)S(1)}, u32[]{:S(2)}, u32[]{:S(2)}) collective-permute-start(bf16[144,256]{1,0:T(8,128)(2,1)S(1)} %collective-permute-done.refs_1_), channel_id=1, source_target_pairs={{0,4},{4,0},{8,12},{12,8},{16,20},{20,16},{24,28},{28,24},{1,5},{5... | collective-permute-start | bytes 221192 | tf_op jit(solution)/shard_map/ppermute | solution.py:18
  8.9 2.1 %collective-permute-start.5 = (bf16[144,256]{1,0:T(8,128)(2,1)S(1)}, bf16[144,256]{1,0:T(8,128)(2,1)S(1)}, u32[]{:S(2)}, u32[]{:S(2)}) collective-permute-start(bf16[144,256]{1,0:T(8,128)(2,1)S(1)} %collective-permute-done.1.refs_2_), channel_id=1, source_target_pairs={{0,4},{4,0},{8,12},{12,8},{16,20},{20,16},{24,28},{28,24},{1,5},{5... | collective-permute-start | bytes 221192 | tf_op jit(solution)/shard_map/ppermute | solution.py:18
  11.0 1.3 %collective-permute-start.6 = (bf16[144,256]{1,0:T(8,128)(2,1)S(1)}, bf16[144,256]{1,0:T(8,128)(2,1)S(1)}, u32[]{:S(2)}, u32[]{:S(2)}) collective-permute-start(bf16[144,256]{1,0:T(8,128)(2,1)S(1)} %collective-permute-done.2.refs_3_), channel_id=1, source_target_pairs={{0,4},{4,0},{8,12},{12,8},{16,20},{20,16},{24,28},{28,24},{1,5},{5... | collective-permute-start | bytes 221192 | tf_op jit(solution)/shard_map/ppermute | solution.py:18
  16.5 10.2 %collective-permute-start.8 = (bf16[128,1024]{1,0:T(8,128)(2,1)S(1)}, bf16[128,1024]{1,0:T(8,128)(2,1)S(1)}, u32[]{:S(2)}, u32[]{:S(2)}) collective-permute-start(bf16[128,1024]{1,0:T(8,128)(2,1)S(1)} %branch.5), channel_id=1, source_target_pairs={{0,24},{4,28},{8,16},{12,20},{16,8},{20,12},{24,0},{28,4},{1,25},{... | collective-permute-start | bytes 786440 | tf_op jit(solution)/shard_map/ppermute | solution.py:18
  18.6 12.8 %collective-permute-start.9 = (bf16[128,1024]{1,0:T(8,128)(2,1)S(1)}, bf16[128,1024]{1,0:T(8,128)(2,1)S(1)}, u32[]{:S(2)}, u32[]{:S(2)}) collective-permute-start(bf16[128,1024]{1,0:T(8,128)(2,1)S(1)} %branch.6), channel_id=1, source_target_pairs={{0,16},{4,20},{8,24},{12,28},{16,0},{20,4},{24,8},{28,12},{1,17},{... | collective-permute-start | bytes 786440 | tf_op jit(solution)/shard_map/ppermute | solution.py:18
  21.4 10.1 %copy-start = (bf16[128,1024]{1,0:T(8,128)(2,1)S(1)}, bf16[128,1024]{1,0:T(8,128)(2,1)}, u32[]{:S(2)}) copy-start(bf16[128,1024]{1,0:T(8,128)(2,1)} %tokens_hbm.1) | copy-start | bytes 786436
  21.4 10.1 %collective-permute-start.10 = (bf16[128,1024]{1,0:T(8,128)(2,1)S(1)}, bf16[128,1024]{1,0:T(8,128)(2,1)S(1)}, u32[]{:S(2)}, u32[]{:S(2)}) collective-permute-start(bf16[128,1024]{1,0:T(8,128)(2,1)S(1)} %branch.7), channel_id=1, source_target_pairs={{0,8},{4,12},{8,0},{12,4},{16,24},{20,28},{24,16},{28,20},{1,9},{5... | collective-permute-start | bytes 786440 | tf_op jit(solution)/shard_map/ppermute | solution.py:18

commit v2 on v1

--- a/solution.py
+++ b/solution.py
@@ -76,11 +76,38 @@
             out_ref[rows:, :] = taps
 
 
+def aim(chip, core, kind):
+    if kind == "far":
+        return chip ^ 3, 1 - core
+    if kind == "own":
+        return chip, core
+    return chip ^ (1 + core), core if kind == "same" else 1 - core
+
+
+def write_features(feats, total, k, half, num):
+    for which in range(2):
+        at = (which * num + k) * half
+        feats[:, at : at + half] = total[:, which * half : (which + 1) * half].astype(jnp.bfloat16)
+
+
+def project(feats, mix_ref, pair_mix_ref):
+    num, half, width = mix_ref.shape
+    both = num * half
+    return jnp.dot(
+        feats[:, :both],
+        mix_ref[...].reshape(both, width),
+        preferred_element_type=jnp.float32,
+    ) + jnp.dot(
+        feats[:, both:],
+        pair_mix_ref[...].reshape(both, width),
+        preferred_element_type=jnp.float32,
+    )
+
+
 def strip_kernel(chips, rows, num, packed, *refs):
     own = refs[:chips]
     pair = refs[chips : 2 * chips]
-    refs = refs[2 * chips :]
-    mix_hbm, *refs = refs
+    mix_hbm, *refs = refs[2 * chips :]
     if not packed:
         taps_ref, *refs = refs
     signal, strip, mix_ref, base, sem = refs
@@ -116,64 +143,54 @@
             strip[pl.ds(at, 16), :] = jnp.concatenate(pieces, axis=0).astype(jnp.bfloat16)
         return carry
 
-    lax.fori_loop(0, num, one_filter, 0, unroll=3 if packed else 1)
+    lax.fori_loop(0, num, one_filter, 0, unroll=num if packed else 1)
     copy.wait()
 
 
-def branch_kernel(chips, rows, shift, *refs):
-    if shift is None:
-        shift_ref, *refs = refs
-        shift = shift_ref[0]
+def branch_kernel(chips, rows, kind, *refs):
     signal, strip, mix_ref, pair_mix_ref, out_ref, feats = refs
     index = lax.axis_index("seq")
-    core = index % 2
-    other = (index // 2) ^ shift
+    other, part = aim(index // 2, index % 2, kind)
     devices = 2 * chips
     num, half, width = mix_ref.shape
-    count = 2 * half
-    offset = (devices - 1 - (2 * other + core)) * rows
-    if chips <= 4:
-
-        def convolve(steps):
-            depth = 2 * rows * steps
-            left = strip[:, pl.ds(pl.multiple_of(offset, rows), depth)]
-            total = jnp.dot(left, signal[0:depth, :], preferred_element_type=jnp.float32)
-            for k in range(num):
-                for which in range(2):
-                    at = (which * num + k) * half
-                    feats[:, at : at + half] = total[
-                        k * rows : (k + 1) * rows, which * half : (which + 1) * half
-                    ].astype(jnp.bfloat16)
-
-        for steps in range(1, chips + 1):
-            pl.when(other == steps - 1)(functools.partial(convolve, steps))
-        both = num * half
-        total = jnp.dot(
-            feats[:, :both],
-            mix_ref[...].reshape(both, width),
-            preferred_element_type=jnp.float32,
-        ) + jnp.dot(
-            feats[:, both:],
-            pair_mix_ref[...].reshape(both, width),
-            preferred_element_type=jnp.float32,
+    offset = (devices - 1 - (2 * other + part)) * rows
+
+    def convolve(steps):
+        depth = 2 * rows * steps
+        left = strip[:, pl.ds(pl.multiple_of(offset, rows), depth)]
+        total = jnp.dot(left, signal[0:depth, :], preferred_element_type=jnp.float32)
+        for k in range(num):
+            write_features(feats, total[k * rows : (k + 1) * rows], k, half, num)
+
+    for steps in range(1, chips + 1):
+        pl.when(other == steps - 1)(functools.partial(convolve, steps))
+    total = project(feats, mix_ref, pair_mix_ref)
+    out_ref[...] = total.astype(out_ref.dtype)
+
+
+def shifted_kernel(chips, rows, shift_ref, *refs):
+    signal, strip, mix_ref, pair_mix_ref, out_ref, sums = refs
+    index = lax.axis_index("seq")
+    other = (index // 2) ^ shift_ref[0]
+    devices = 2 * chips
+    num, half, width = mix_ref.shape
+    offset = (devices - 1 - (2 * other + index % 2)) * rows
+    sums[...] = jnp.zeros(sums.shape, jnp.float32)
+
+    def add_tokens(step, carry):
+        at = pl.multiple_of(2 * rows * step, 2 * rows)
+        left = strip[:, pl.ds(pl.multiple_of(offset + at, rows), 2 * rows)]
+        sums[...] += jnp.dot(
+            left, signal[pl.ds(at, 2 * rows), :], preferred_element_type=jnp.float32
         )
-    else:
-        feats[...] = jnp.zeros(feats.shape, jnp.float32)
-
-        def add_tokens(step, carry):
-            at = pl.multiple_of(2 * rows * step, 2 * rows)
-            left = strip[:, pl.ds(pl.multiple_of(offset + at, rows), 2 * rows)]
-            feats[...] += jnp.dot(
-                left, signal[pl.ds(at, 2 * rows), :], preferred_element_type=jnp.float32
-            )
-            return carry
-
-        lax.fori_loop(0, other + 1, add_tokens, 0)
-        total = jnp.zeros((rows, width), jnp.float32)
-        for k in range(num):
-            found = feats[k * rows : (k + 1) * rows, :].astype(jnp.bfloat16)
-            weight = jnp.concatenate([mix_ref[k], pair_mix_ref[k]], axis=0)
-            total += jnp.dot(found, weight, preferred_element_type=jnp.float32)
+        return carry
+
+    lax.fori_loop(0, other + 1, add_tokens, 0)
+    total = jnp.zeros((rows, width), jnp.float32)
+    for k in range(num):
+        found = sums[k * rows : (k + 1) * rows, :].astype(jnp.bfloat16)
+        weight = jnp.concatenate([mix_ref[k], pair_mix_ref[k]], axis=0)
+        total += jnp.dot(found, weight, preferred_element_type=jnp.float32)
     out_ref[...] = total.astype(out_ref.dtype)
 
 
@@ -185,7 +202,7 @@
     length = devices * rows
     count = width // chips
     packed = count >= span
-    few = chips <= 4
+    relay = chips == 4 and packed and count % 256 == 0
     pair_mixing = swap(mixing, 1, devices)
     tall = rows + (EXTRA if packed else 0)
     blocks = kernel_call(
@@ -206,6 +223,16 @@
     pair = [swap(block, 1, devices) for block in own]
     operands = [*own, *pair, in_hbm(mixing)]
     specs = [VMEM] * (2 * chips) + [HBM]
+    feats = pltpu.VMEM((rows, num * count), jnp.bfloat16)
+    shapes = [
+        jax.ShapeDtypeStruct((length, count), jnp.bfloat16),
+        jax.ShapeDtypeStruct((num * rows, length + rows), jnp.bfloat16),
+        jax.ShapeDtypeStruct(mixing.shape, mixing.dtype),
+    ]
+    scratch = [
+        pltpu.VMEM((EXTRA, length + 2 * rows), jnp.float32),
+        pltpu.SemaphoreType.DMA(()),
+    ]
     if not packed:
         taps = lax.all_gather(filters, "seq", axis=1, tiled=True)[:, ::-1]
         operands.append(jnp.pad(taps, ((0, EXTRA - num), (0, 0))))
@@ -213,35 +240,39 @@
     signal, strip, near_mixing = kernel_call(
         functools.partial(strip_kernel, chips, rows, num, packed),
         "strip",
-        [
-            jax.ShapeDtypeStruct((length, count), jnp.bfloat16),
-            jax.ShapeDtypeStruct((num * rows, length + rows), jnp.bfloat16),
-            jax.ShapeDtypeStruct(mixing.shape, mixing.dtype),
-        ],
+        shapes,
         specs,
-        16 * MIB if few else 48 * MIB,
-        [pltpu.VMEM((EXTRA, length + 2 * rows), jnp.float32), pltpu.SemaphoreType.DMA(())],
+        24 * MIB if relay else 48 * MIB,
+        scratch,
     )(*operands)
     fixed = [signal, strip, near_mixing, pair_mixing]
-    if few:
-
-        def branch(shift, dtype):
+    total = tokens.astype(jnp.float32)
+    if relay:
+
+        def branch(kind, dtype):
             return kernel_call(
-                functools.partial(branch_kernel, chips, rows, shift),
+                functools.partial(branch_kernel, chips, rows, kind),
                 "branch",
                 jax.ShapeDtypeStruct((rows, width), dtype),
                 [VMEM] * 4,
                 24 * MIB,
-                [pltpu.VMEM((rows, num * count), jnp.bfloat16)],
+                [feats],
             )(*fixed)
 
-        parts = {s: branch(s, jnp.bfloat16) for s in reversed(range(1, chips))}
-        total = branch(0, jnp.float32)
+        pairs = [(c, q) for c in range(chips) for q in range(2)]
+        across = [(2 * c + q, 2 * (c ^ (1 + q)) + 1 - q) for c, q in pairs]
+        along = [(2 * c + q, 2 * (c ^ (1 + q)) + q) for c, q in pairs]
+        far = lax.ppermute(branch("far", jnp.bfloat16), "seq", across)
+        other = lax.ppermute(branch("other", jnp.bfloat16), "seq", across)
+        same = (branch("same", jnp.float32) + far.astype(jnp.float32)).astype(jnp.bfloat16)
+        same = lax.ppermute(same, "seq", along)
+        total = total + branch("own", jnp.float32)
+        sent = [other, same]
     else:
 
         def branch(shift):
             return kernel_call(
-                functools.partial(branch_kernel, chips, rows, None),
+                functools.partial(shifted_kernel, chips, rows),
                 "branch",
                 jax.ShapeDtypeStruct((rows, width), jnp.bfloat16),
                 [SMEM] + [VMEM] * 4,
@@ -250,10 +281,7 @@
             )(shift.reshape(1), *fixed)
 
         parts = lax.map(branch, jnp.arange(chips, dtype=jnp.int32))
-        total = parts[0].astype(jnp.float32)
-        parts = {s: parts[s] for s in range(1, chips)}
-    sent = [swap(value, 2 * s, devices) for s, value in parts.items()]
-    total = tokens.astype(jnp.float32) + total
+        sent = [parts[0]] + [swap(parts[s], 2 * s, devices) for s in range(1, chips)]
     for value in sent:
         total = total + value.astype(jnp.float32)
     return total.astype(jnp.bfloat16)

time: 32.6 us -> 29.7 us (0.911)
  starting transfers between devices: 7.8 us -> 6.01 us
  waiting for transfers between devices: 13.2 us -> 12.6 us
  Pallas kernels: 10.4 us -> 9.88 us
    ppermute x11 -> x8, waiting for transfers between devices: 13.2 us -> 6.47 us  [swap(): return lax.ppermute(value, 'seq', [(i, i ^ bits) for i in range(size)])]
    ppermute x0 -> x3, waiting for transfers between devices: none -> 6.15 us  [the longest x1 3.7 us: local(): same = lax.ppermute(same, 'seq', along)]
    ppermute x11 -> x8, starting transfers between devices: 7.8 us -> 4.55 us  [swap(): return lax.ppermute(value, 'seq', [(i, i ^ bits) for i in range(size)])]
    ppermute x0 -> x3, starting transfers between devices: none -> 1.46 us  [the longest x1 0.87 us: local(): other = lax.ppermute(branch('other', jnp.bfloat16), 'seq', across)]
  transfers between devices with their start and end apart: 11 -> 11, of which waited for: 6 -> 7; matrix products, arithmetic and copies ran while one was open for 0% -> 0% of each run, Pallas kernels for 26% -> 27%
where the time goes in v2:
time: 29.7 us; the launch traced here: 29.5 us
  waiting for transfers between devices  12.6 us (42%)
  Pallas kernels  9.88 us (33%)
  starting transfers between devices  6.01 us (20%)
  other arithmetic  0.9 us (3%)
    pallas_call x4, Pallas kernels, branch(): kernel_call(functools.partial(branch_kernel, chips, rows, kind), 'branch'...  6.66 us
    ppermute x8, waiting for transfers between devices, swap(): return lax.ppermute(value, 'seq', [(i, i ^ bits) for i in range(size)])  6.47 us
    ppermute x8, starting transfers between devices, swap(): return lax.ppermute(value, 'seq', [(i, i ^ bits) for i in range(size)])  4.55 us
    ppermute x1, waiting for transfers between devices, local(): same = lax.ppermute(same, 'seq', along)  3.7 us
    pallas_call x1, Pallas kernels, local(): kernel_call(functools.partial(strip_kernel, chips, rows, num, packed), 's...  1.99 us
    ppermute x1, waiting for transfers between devices, local(): far = lax.ppermute(branch('far', jnp.bfloat16), 'seq', across)  1.49 us
    pallas_call x1, Pallas kernels, local(): kernel_call(norm_kernel, 'norm', [jax.ShapeDtypeStruct((tall, count), jnp...  1.23 us
    ppermute x1, waiting for transfers between devices, local(): other = lax.ppermute(branch('other', jnp.bfloat16), 'seq', across)  0.96 us
  transfers between devices with their start and end apart: 11, of which 7 were waited for; matrix products, arithmetic and copies ran while one was open for 0% of the time, Pallas kernels for 27%

profile of v2, /device:TPU:0, one launch (start us, length us, event | category | flops | bytes accessed | tf_op | source)
XLA Modules:
  0.0 29.5 jit_solution(17685952869882704360)
XLA Ops:
  0.0 0.5 %collective-permute-start.7 = (bf16[12,128,1024]{2,1,0:T(8,128)(2,1)}, bf16[12,128,1024]{2,1,0:T(8,128)(2,1)S(1)}, u32[]{:S(2)}, u32[]{:S(2)}) collective-permute-start(bf16[12,128,1024]{2,1,0:T(8,128)(2,1)} %refs_8_.1), channel_id=1, source_target_pairs={{0,4},{4,0},{8,12},{12,8},{16,20},{20,16},{24,28},{28,24},{1,5},{5... | collective-permute-start | bytes 9437192 | tf_op jit(solution)/shard_map/ppermute | solution.py:18
  0.5 1.2 %norm.1 = (bf16[144,256]{1,0:T(8,128)(2,1)S(1)}, bf16[144,256]{1,0:T(8,128)(2,1)S(1)}, bf16[144,256]{1,0:T(8,128)(2,1)S(1)}, bf16[144,256]{1,0:T(8,128)(2,1)S(1)}) custom-call(bf16[128,1024]{1,0:T(8,128)(2,1)} %tokens_hbm.1, f32[1,1024]{1,0:T(1,128)} %bitcast.1, f32[12,128]{1,0:T(8,128)} %filters_hbm.1), custom_call_target="tpu_custom_call" | custom-call | tf_op jit(solution)/shard_map/norm/pallas_call | solution.py:208
  1.7 2.6 %collective-permute-start = (bf16[144,256]{1,0:T(8,128)(2,1)S(1)}, bf16[144,256]{1,0:T(8,128)(2,1)S(1)}, u32[]{:S(2)}, u32[]{:S(2)}) collective-permute-start(bf16[144,256]{1,0:T(8,128)(2,1)S(1)} %get-tuple-element.13), channel_id=1, source_target_pairs={{0,8},{4,12},{8,0},{12,4},{16,24},{20,28},{24,16},{28,20},{1,9},{5... | collective-permute-start | bytes 221192 | tf_op jit(solution)/shard_map/ppermute | solution.py:18
  4.2 1.5 %collective-permute-start.1 = (bf16[144,256]{1,0:T(8,128)(2,1)S(1)}, bf16[144,256]{1,0:T(8,128)(2,1)S(1)}, u32[]{:S(2)}, u32[]{:S(2)}) collective-permute-start(bf16[144,256]{1,0:T(8,128)(2,1)S(1)} %get-tuple-element.14), channel_id=1, source_target_pairs={{0,16},{4,20},{8,24},{12,28},{16,0},{20,4},{24,8},{28,12},{1,17},{... | collective-permute-start | bytes 221192 | tf_op jit(solution)/shard_map/ppermute | solution.py:18
  5.8 0.0 collective-permute-start.2
  5.8 0.0 collective-permute-start.3
  5.8 1.4 %collective-permute-done.refs_1_ = bf16[144,256]{1,0:T(8,128)(2,1)S(1)} collective-permute-done((bf16[144,256]{1,0:T(8,128)(2,1)S(1)}, bf16[144,256]{1,0:T(8,128)(2,1)S(1)}, u32[]{:S(2)}, u32[]{:S(2)}) %collective-permute-start) | collective-permute-done | bytes 73760 | tf_op jit(solution)/shard_map/ppermute | solution.py:18
  7.2 0.0 collective-permute-start.4
  7.2 1.7 %collective-permute-done.1.refs_2_ = bf16[144,256]{1,0:T(8,128)(2,1)S(1)} collective-permute-done((bf16[144,256]{1,0:T(8,128)(2,1)S(1)}, bf16[144,256]{1,0:T(8,128)(2,1)S(1)}, u32[]{:S(2)}, u32[]{:S(2)}) %collective-permute-start.1) | collective-permute-done | bytes 73760 | tf_op jit(solution)/shard_map/ppermute | solution.py:18
  8.9 0.0 collective-permute-start.5
  8.9 2.1 %collective-permute-done.2.refs_3_ = bf16[144,256]{1,0:T(8,128)(2,1)S(1)} collective-permute-done((bf16[144,256]{1,0:T(8,128)(2,1)S(1)}, bf16[144,256]{1,0:T(8,128)(2,1)S(1)}, u32[]{:S(2)}, u32[]{:S(2)}) %collective-permute-start.2) | collective-permute-done | bytes 73760 | tf_op jit(solution)/shard_map/ppermute | solution.py:18
  11.0 0.0 collective-permute-start.6
  11.0 0.0 collective-permute-done.3.refs_4_
  11.0 0.0 collective-permute-done.4.refs_5_
  11.0 0.0 collective-permute-done.5.refs_6_
  11.0 1.2 %collective-permute-done.6.refs_7_ = bf16[144,256]{1,0:T(8,128)(2,1)S(1)} collective-permute-done((bf16[144,256]{1,0:T(8,128)(2,1)S(1)}, bf16[144,256]{1,0:T(8,128)(2,1)S(1)}, u32[]{:S(2)}, u32[]{:S(2)}) %collective-permute-start.6) | collective-permute-done | bytes 73760 | tf_op jit(solution)/shard_map/ppermute | solution.py:18
  12.3 2.0 %strip.1 = (bf16[1024,256]{1,0:T(8,128)(2,1)S(1)}, bf16[1536,1152]{1,0:T(8,128)(2,1)S(1)}, bf16[12,128,1024]{2,1,0:T(8,128)(2,1)S(1)}) custom-call(bf16[144,256]{1,0:T(8,128)(2,1)S(1)} %get-tuple-element.12.refs_0_, bf16[144,256]{1,0:T(8,128)(2,1)S(1)} %collective-permute-done.refs_1_, bf16[144,256]{1,0:T(8,128)(2,1)S(1)} %collective-permute-done.1.refs_2_, ...), custom_call_target="tpu_custom_call" | custom-call | tf_op jit(solution)/shard_map/strip/pallas_call | solution.py:240
  14.3 0.0 collective-permute-done.7.refs_3_
  14.3 2.0 %branch.7 = bf16[128,1024]{1,0:T(8,128)(2,1)S(1)} custom-call(bf16[1024,256]{1,0:T(8,128)(2,1)S(1)} %get-tuple-element.16.refs_0_, bf16[1536,1152]{1,0:T(8,128)(2,1)S(1)} %get-tuple-element.17.refs_1_, bf16[12,128,1024]{2,1,0:T(8,128)(2,1)S(1)} %get-tuple-element.18.refs_2_, bf16[12,128,1024]{2,1,0:T(8,128)(2,1)S(1)} %collective-permute-done.7.refs_3_), custom_call_target="tpu_custom_call" | custom-call | tf_op jit(solution)/shard_map/branch/pallas_call | solution.py:253
  16.3 0.2 collective-permute-start.9
  16.5 1.6 %branch.5 = bf16[128,1024]{1,0:T(8,128)(2,1)S(1)} custom-call(bf16[1024,256]{1,0:T(8,128)(2,1)S(1)} %get-tuple-element.16.refs_0_, bf16[1536,1152]{1,0:T(8,128)(2,1)S(1)} %get-tuple-element.17.refs_1_, bf16[12,128,1024]{2,1,0:T(8,128)(2,1)S(1)} %get-tuple-element.18.refs_2_, bf16[12,128,1024]{2,1,0:T(8,128)(2,1)S(1)} %collective-permute-done.7.refs_3_), custom_call_target="tpu_custom_call" | custom-call | tf_op jit(solution)/shard_map/branch/pallas_call | solution.py:253
  18.0 0.9 %collective-permute-start.8 = (bf16[128,1024]{1,0:T(8,128)(2,1)S(1)}, bf16[128,1024]{1,0:T(8,128)(2,1)S(1)}, u32[]{:S(2)}, u32[]{:S(2)}) collective-permute-start(bf16[128,1024]{1,0:T(8,128)(2,1)S(1)} %branch.5), channel_id=1, source_target_pairs={{0,12},{4,16},{8,4},{12,24},{16,28},{20,0},{24,20},{28,8},{1,13},{... | collective-permute-start | bytes 786440 | tf_op jit(solution)/shard_map/ppermute | solution.py:266
  18.9 1.7 %branch.6 = f32[128,1024]{1,0:T(8,128)S(1)} custom-call(bf16[1024,256]{1,0:T(8,128)(2,1)S(1)} %get-tuple-element.16.refs_0_, bf16[1536,1152]{1,0:T(8,128)(2,1)S(1)} %get-tuple-element.17.refs_1_, bf16[12,128,1024]{2,1,0:T(8,128)(2,1)S(1)} %get-tuple-element.18.refs_2_, bf16[12,128,1024]{2,1,0:T(8,128)(2,1)S(1)} %collective-permute-done.7.refs_3_), custom_call_target="tpu_custom_call" | custom-call | tf_op jit(solution)/shard_map/branch/pallas_call | solution.py:253
  20.7 1.5 %collective-permute-done.9 = bf16[128,1024]{1,0:T(8,128)(2,1)S(1)} collective-permute-done((bf16[128,1024]{1,0:T(8,128)(2,1)S(1)}, bf16[128,1024]{1,0:T(8,128)(2,1)S(1)}, u32[]{:S(2)}, u32[]{:S(2)}) %collective-permute-start.9) | collective-permute-done | bytes 262176 | tf_op jit(solution)/shard_map/ppermute | solution.py:265
  22.1 0.1 add_convert_fusion.1
  22.2 0.0 copy-start
  22.2 0.4 %collective-permute-start.10 = (bf16[128,1024]{1,0:T(8,128)(2,1)S(1)}, bf16[128,1024]{1,0:T(8,128)(2,1)S(1)}, u32[]{:S(2)}, u32[]{:S(2)}) collective-permute-start(bf16[128,1024]{1,0:T(8,128)(2,1)S(1)} %add_convert_fusion.1), channel_id=1, source_target_pairs={{0,8},{4,20},{8,0},{12,28},{16,24},{20,4},{24,16},{28,12},{1,9},{5... | collective-permute-start | bytes 786440 | tf_op jit(solution)/shard_map/ppermute | solution.py:268
  22.6 1.4 %branch.4 = f32[128,1024]{1,0:T(8,128)S(1)} custom-call(bf16[1024,256]{1,0:T(8,128)(2,1)S(1)} %get-tuple-element.16.refs_0_, bf16[1536,1152]{1,0:T(8,128)(2,1)S(1)} %get-tuple-element.17.refs_1_, bf16[12,128,1024]{2,1,0:T(8,128)(2,1)S(1)} %get-tuple-element.18.refs_2_, bf16[12,128,1024]{2,1,0:T(8,128)(2,1)S(1)} %collective-permute-done.7.refs_3_), custom_call_target="tpu_custom_call" | custom-call | tf_op jit(solution)/shard_map/branch/pallas_call | solution.py:253
  24.0 1.0 %collective-permute-done.8 = bf16[128,1024]{1,0:T(8,128)(2,1)S(1)} collective-permute-done((bf16[128,1024]{1,0:T(8,128)(2,1)S(1)}, bf16[128,1024]{1,0:T(8,128)(2,1)S(1)}, u32[]{:S(2)}, u32[]{:S(2)}) %collective-permute-start.8) | collective-permute-done | bytes 262176 | tf_op jit(solution)/shard_map/ppermute | solution.py:266
  25.0 3.7 %collective-permute-done.10 = bf16[128,1024]{1,0:T(8,128)(2,1)S(1)} collective-permute-done((bf16[128,1024]{1,0:T(8,128)(2,1)S(1)}, bf16[128,1024]{1,0:T(8,128)(2,1)S(1)}, u32[]{:S(2)}, u32[]{:S(2)}) %collective-permute-start.10) | collective-permute-done | bytes 262176 | tf_op jit(solution)/shard_map/ppermute | solution.py:268
  28.7 0.0 copy-done
  28.7 0.8 %add_convert_fusion = bf16[128,1024]{1,0:T(8,128)(2,1)} fusion(bf16[128,1024]{1,0:T(8,128)(2,1)S(1)} %collective-permute-done.10, bf16[128,1024]{1,0:T(8,128)(2,1)S(1)} %collective-permute-done.8, f32[128,1024]{1,0:T(8,128)S(1)} %branch.4, bf16[128,1024]{1,0:T(8,128)(2,1)S(1)} %copy-done), kind=kLoop, calls=%fused_computation | loop fusion | flops 917504 | bytes 1572864 | tf_op jit(solution)/shard_map/convert_element_type | solution.py:287
Async XLA Ops:
  0.0 14.3 %collective-permute-start.7 = (bf16[12,128,1024]{2,1,0:T(8,128)(2,1)}, bf16[12,128,1024]{2,1,0:T(8,128)(2,1)S(1)}, u32[]{:S(2)}, u32[]{:S(2)}) collective-permute-start(bf16[12,128,1024]{2,1,0:T(8,128)(2,1)} %refs_8_.1), channel_id=1, source_target_pairs={{0,4},{4,0},{8,12},{12,8},{16,20},{20,16},{24,28},{28,24},{1,5},{5... | collective-permute-start | bytes 9437192 | tf_op jit(solution)/shard_map/ppermute | solution.py:18
  1.7 5.5 %collective-permute-start = (bf16[144,256]{1,0:T(8,128)(2,1)S(1)}, bf16[144,256]{1,0:T(8,128)(2,1)S(1)}, u32[]{:S(2)}, u32[]{:S(2)}) collective-permute-start(bf16[144,256]{1,0:T(8,128)(2,1)S(1)} %get-tuple-element.13), channel_id=1, source_target_pairs={{0,8},{4,12},{8,0},{12,4},{16,24},{20,28},{24,16},{28,20},{1,9},{5... | collective-permute-start | bytes 221192 | tf_op jit(solution)/shard_map/ppermute | solution.py:18
  4.2 4.7 %collective-permute-start.1 = (bf16[144,256]{1,0:T(8,128)(2,1)S(1)}, bf16[144,256]{1,0:T(8,128)(2,1)S(1)}, u32[]{:S(2)}, u32[]{:S(2)}) collective-permute-start(bf16[144,256]{1,0:T(8,128)(2,1)S(1)} %get-tuple-element.14), channel_id=1, source_target_pairs={{0,16},{4,20},{8,24},{12,28},{16,0},{20,4},{24,8},{28,12},{1,17},{... | collective-permute-start | bytes 221192 | tf_op jit(solution)/shard_map/ppermute | solution.py:18
  5.8 5.3 %collective-permute-start.2 = (bf16[144,256]{1,0:T(8,128)(2,1)S(1)}, bf16[144,256]{1,0:T(8,128)(2,1)S(1)}, u32[]{:S(2)}, u32[]{:S(2)}) collective-permute-start(bf16[144,256]{1,0:T(8,128)(2,1)S(1)} %get-tuple-element.15), channel_id=1, source_target_pairs={{0,24},{4,28},{8,16},{12,20},{16,8},{20,12},{24,0},{28,4},{1,25},{... | collective-permute-start | bytes 221192 | tf_op jit(solution)/shard_map/ppermute | solution.py:18
  5.8 5.2 %collective-permute-start.3 = (bf16[144,256]{1,0:T(8,128)(2,1)S(1)}, bf16[144,256]{1,0:T(8,128)(2,1)S(1)}, u32[]{:S(2)}, u32[]{:S(2)}) collective-permute-start(bf16[144,256]{1,0:T(8,128)(2,1)S(1)} %get-tuple-element.12.refs_0_), channel_id=1, source_target_pairs={{0,4},{4,0},{8,12},{12,8},{16,20},{20,16},{24,28},{28,24},{1,5},{5... | collective-permute-start | bytes 221192 | tf_op jit(solution)/shard_map/ppermute | solution.py:18
  7.2 3.8 %collective-permute-start.4 = (bf16[144,256]{1,0:T(8,128)(2,1)S(1)}, bf16[144,256]{1,0:T(8,128)(2,1)S(1)}, u32[]{:S(2)}, u32[]{:S(2)}) collective-permute-start(bf16[144,256]{1,0:T(8,128)(2,1)S(1)} %collective-permute-done.refs_1_), channel_id=1, source_target_pairs={{0,4},{4,0},{8,12},{12,8},{16,20},{20,16},{24,28},{28,24},{1,5},{5... | collective-permute-start | bytes 221192 | tf_op jit(solution)/shard_map/ppermute | solution.py:18
  8.9 2.1 %collective-permute-start.5 = (bf16[144,256]{1,0:T(8,128)(2,1)S(1)}, bf16[144,256]{1,0:T(8,128)(2,1)S(1)}, u32[]{:S(2)}, u32[]{:S(2)}) collective-permute-start(bf16[144,256]{1,0:T(8,128)(2,1)S(1)} %collective-permute-done.1.refs_2_), channel_id=1, source_target_pairs={{0,4},{4,0},{8,12},{12,8},{16,20},{20,16},{24,28},{28,24},{1,5},{5... | collective-permute-start | bytes 221192 | tf_op jit(solution)/shard_map/ppermute | solution.py:18
  11.0 1.3 %collective-permute-start.6 = (bf16[144,256]{1,0:T(8,128)(2,1)S(1)}, bf16[144,256]{1,0:T(8,128)(2,1)S(1)}, u32[]{:S(2)}, u32[]{:S(2)}) collective-permute-start(bf16[144,256]{1,0:T(8,128)(2,1)S(1)} %collective-permute-done.2.refs_3_), channel_id=1, source_target_pairs={{0,4},{4,0},{8,12},{12,8},{16,20},{20,16},{24,28},{28,24},{1,5},{5... | collective-permute-start | bytes 221192 | tf_op jit(solution)/shard_map/ppermute | solution.py:18
  16.3 5.8 %collective-permute-start.9 = (bf16[128,1024]{1,0:T(8,128)(2,1)S(1)}, bf16[128,1024]{1,0:T(8,128)(2,1)S(1)}, u32[]{:S(2)}, u32[]{:S(2)}) collective-permute-start(bf16[128,1024]{1,0:T(8,128)(2,1)S(1)} %branch.7), channel_id=1, source_target_pairs={{0,12},{4,16},{8,4},{12,24},{16,28},{20,0},{24,20},{28,8},{1,13},{... | collective-permute-start | bytes 786440 | tf_op jit(solution)/shard_map/ppermute | solution.py:265
  18.0 6.9 %collective-permute-start.8 = (bf16[128,1024]{1,0:T(8,128)(2,1)S(1)}, bf16[128,1024]{1,0:T(8,128)(2,1)S(1)}, u32[]{:S(2)}, u32[]{:S(2)}) collective-permute-start(bf16[128,1024]{1,0:T(8,128)(2,1)S(1)} %branch.5), channel_id=1, source_target_pairs={{0,12},{4,16},{8,4},{12,24},{16,28},{20,0},{24,20},{28,8},{1,13},{... | collective-permute-start | bytes 786440 | tf_op jit(solution)/shard_map/ppermute | solution.py:266
  22.2 6.5 %copy-start = (bf16[128,1024]{1,0:T(8,128)(2,1)S(1)}, bf16[128,1024]{1,0:T(8,128)(2,1)}, u32[]{:S(2)}) copy-start(bf16[128,1024]{1,0:T(8,128)(2,1)} %tokens_hbm.1) | copy-start | bytes 786436
  22.2 6.4 %collective-permute-start.10 = (bf16[128,1024]{1,0:T(8,128)(2,1)S(1)}, bf16[128,1024]{1,0:T(8,128)(2,1)S(1)}, u32[]{:S(2)}, u32[]{:S(2)}) collective-permute-start(bf16[128,1024]{1,0:T(8,128)(2,1)S(1)} %add_convert_fusion.1), channel_id=1, source_target_pairs={{0,8},{4,20},{8,0},{12,28},{16,24},{20,4},{24,16},{28,12},{1,9},{5... | collective-permute-start | bytes 786440 | tf_op jit(solution)/shard_map/ppermute | solution.py:268

commit v3 on v2

--- a/solution.py
+++ b/solution.py
@@ -76,18 +76,19 @@
             out_ref[rows:, :] = taps
 
 
+def stage_kernel(mix_hbm, block_ref, mix_ref, out_ref, sem):
+    copy = pltpu.make_async_copy(mix_hbm, mix_ref, sem)
+    copy.start()
+    out_ref[...] = block_ref[...]
+    copy.wait()
+
+
 def aim(chip, core, kind):
     if kind == "far":
         return chip ^ 3, 1 - core
     if kind == "own":
         return chip, core
     return chip ^ (1 + core), core if kind == "same" else 1 - core
-
-
-def write_features(feats, total, k, half, num):
-    for which in range(2):
-        at = (which * num + k) * half
-        feats[:, at : at + half] = total[:, which * half : (which + 1) * half].astype(jnp.bfloat16)
 
 
 def project(feats, mix_ref, pair_mix_ref):
@@ -104,22 +105,25 @@
     )
 
 
-def strip_kernel(chips, rows, num, packed, *refs):
+def strip_kernel(chips, rows, num, fine, packed, *refs):
     own = refs[:chips]
     pair = refs[chips : 2 * chips]
-    mix_hbm, *refs = refs[2 * chips :]
+    refs = refs[2 * chips :]
     if not packed:
         taps_ref, *refs = refs
-    signal, strip, mix_ref, base, sem = refs
-    copy = pltpu.make_async_copy(mix_hbm, mix_ref, sem)
-    copy.start()
+    signal, strip, base = refs
     index = lax.axis_index("seq")
     chip = index // 2
     core = index % 2
     devices = 2 * chips
     length = devices * rows
-    half = signal.shape[1] // 2
+    groups = rows // fine
+    count = signal.shape[1] // groups
+    half = count // 2
     wide = length + 2 * rows
+    late = [rows - fine * (g + 1) for g in range(groups)]
+    for g in range(groups - 1):
+        signal[0 : late[g], g * count : (g + 1) * count] = jnp.zeros((late[g], count), signal.dtype)
     base[:, length:] = jnp.zeros((base.shape[0], 2 * rows), jnp.float32)
     for shift in range(chips):
         for which, block in enumerate((own[shift], pair[shift])):
@@ -127,7 +131,9 @@
             value = block[0:rows, :]
             turned = jnp.concatenate([value[:, half:], value[:, :half]], axis=1)
             value = jnp.where(core == 0, value, turned)
-            signal[pl.ds(pl.multiple_of(place * rows, rows), rows), :] = value
+            for g in range(groups):
+                at = pl.multiple_of(place * rows + late[g], fine)
+                signal[pl.ds(at, rows), g * count : (g + 1) * count] = value
             if packed:
                 at = pl.multiple_of((devices - 1 - place) * rows, rows)
                 base[:, pl.ds(at, rows)] = block[rows:, 0:rows].astype(jnp.float32)
@@ -136,18 +142,17 @@
 
     def one_filter(k, carry):
         line = jnp.broadcast_to(base[pl.ds(k, 1), :], (8, wide))
-        line = pltpu.roll(line, wide - rows + 1, 1, stride=1, stride_axis=0)
-        for step in range(rows // 16):
+        line = pltpu.roll(line, wide - fine + 1, 1, stride=1, stride_axis=0)
+        for step in range(fine // 16):
             pieces = [pltpu.roll(line, 16 * step + 8 * h, 1)[:, : length + rows] for h in (0, 1)]
-            at = pl.multiple_of(k * rows + 16 * step, 16)
+            at = pl.multiple_of(k * fine + 16 * step, 16)
             strip[pl.ds(at, 16), :] = jnp.concatenate(pieces, axis=0).astype(jnp.bfloat16)
         return carry
 
     lax.fori_loop(0, num, one_filter, 0, unroll=num if packed else 1)
-    copy.wait()
-
-
-def branch_kernel(chips, rows, kind, *refs):
+
+
+def branch_kernel(chips, rows, fine, kind, *refs):
     signal, strip, mix_ref, pair_mix_ref, out_ref, feats = refs
     index = lax.axis_index("seq")
     other, part = aim(index // 2, index % 2, kind)
@@ -160,7 +165,13 @@
         left = strip[:, pl.ds(pl.multiple_of(offset, rows), depth)]
         total = jnp.dot(left, signal[0:depth, :], preferred_element_type=jnp.float32)
         for k in range(num):
-            write_features(feats, total[k * rows : (k + 1) * rows], k, half, num)
+            for which in range(2):
+                for g in range(rows // fine):
+                    to = (which * num + k) * half
+                    at = (2 * g + which) * half
+                    feats[g * fine : (g + 1) * fine, to : to + half] = total[
+                        k * fine : (k + 1) * fine, at : at + half
+                    ].astype(jnp.bfloat16)
 
     for steps in range(1, chips + 1):
         pl.when(other == steps - 1)(functools.partial(convolve, steps))
@@ -204,6 +215,7 @@
     packed = count >= span
     relay = chips == 4 and packed and count % 256 == 0
     pair_mixing = swap(mixing, 1, devices)
+    fine = 32 if relay else rows
     tall = rows + (EXTRA if packed else 0)
     blocks = kernel_call(
         norm_kernel,
@@ -220,25 +232,32 @@
     )(in_hbm(tokens), in_hbm(norm_gain.reshape(1, width)), in_hbm(filters))
     far = [swap(blocks[s], 2 * s, devices) for s in reversed(range(1, chips))]
     own = [blocks[0], *reversed(far)]
-    pair = [swap(block, 1, devices) for block in own]
-    operands = [*own, *pair, in_hbm(mixing)]
-    specs = [VMEM] * (2 * chips) + [HBM]
+    near_mixing, first = kernel_call(
+        stage_kernel,
+        "stage",
+        [
+            jax.ShapeDtypeStruct(mixing.shape, mixing.dtype),
+            jax.ShapeDtypeStruct(blocks[0].shape, blocks[0].dtype),
+        ],
+        [HBM, VMEM],
+        8 * MIB,
+        [pltpu.SemaphoreType.DMA(())],
+    )(in_hbm(mixing), blocks[0])
+    pair = [swap(block, 1, devices) for block in (first, *own[1:])]
+    operands = [*own, *pair]
+    specs = [VMEM] * (2 * chips)
     feats = pltpu.VMEM((rows, num * count), jnp.bfloat16)
     shapes = [
-        jax.ShapeDtypeStruct((length, count), jnp.bfloat16),
-        jax.ShapeDtypeStruct((num * rows, length + rows), jnp.bfloat16),
-        jax.ShapeDtypeStruct(mixing.shape, mixing.dtype),
+        jax.ShapeDtypeStruct((length + rows, rows // fine * count), jnp.bfloat16),
+        jax.ShapeDtypeStruct((num * fine, length + rows), jnp.bfloat16),
     ]
-    scratch = [
-        pltpu.VMEM((EXTRA, length + 2 * rows), jnp.float32),
-        pltpu.SemaphoreType.DMA(()),
-    ]
+    scratch = [pltpu.VMEM((EXTRA, length + 2 * rows), jnp.float32)]
     if not packed:
         taps = lax.all_gather(filters, "seq", axis=1, tiled=True)[:, ::-1]
         operands.append(jnp.pad(taps, ((0, EXTRA - num), (0, 0))))
         specs.append(VMEM)
-    signal, strip, near_mixing = kernel_call(
-        functools.partial(strip_kernel, chips, rows, num, packed),
+    signal, strip = kernel_call(
+        functools.partial(strip_kernel, chips, rows, num, fine, packed),
         "strip",
         shapes,
         specs,
@@ -251,7 +270,7 @@
 
         def branch(kind, dtype):
             return kernel_call(
-                functools.partial(branch_kernel, chips, rows, kind),
+                functools.partial(branch_kernel, chips, rows, fine, kind),
                 "branch",
                 jax.ShapeDtypeStruct((rows, width), dtype),
                 [VMEM] * 4,

time: 29.7 us -> 28.8 us (0.970)
  waiting for transfers between devices: 12.6 us -> 10.3 us
  Pallas kernels: 9.88 us -> 10.7 us
  starting transfers between devices: 6.01 us -> 6.56 us
    ppermute x8, waiting for transfers between devices: 6.47 us -> 4 us  [swap(): return lax.ppermute(value, 'seq', [(i, i ^ bits) for i in range(size)])]
    pallas_call x5 -> x6, Pallas kernels: 8.65 us -> 9.5 us  [the longest x4 6.5 us: branch(): kernel_call(functools.partial(branch_kernel, chips, rows, fine, kind), 'b...]
    ppermute x8, starting transfers between devices: 4.55 us -> 5.11 us  [swap(): return lax.ppermute(value, 'seq', [(i, i ^ bits) for i in range(size)])]
  transfers between devices with their start and end apart: 11 -> 11, of which waited for: 7 -> 6; matrix products, arithmetic and copies ran while one was open for 0% -> 0% of each run, Pallas kernels for 27% -> 31%
where the time goes in v3:
time: 28.8 us; the launch traced here: 28.6 us
  Pallas kernels  10.7 us (37%)
  waiting for transfers between devices  10.3 us (36%)
  starting transfers between devices  6.56 us (23%)
  other arithmetic  0.9 us (3%)
    pallas_call x4, Pallas kernels, branch(): kernel_call(functools.partial(branch_kernel, chips, rows, fine, kind), 'b...  6.5 us
    ppermute x8, starting transfers between devices, swap(): return lax.ppermute(value, 'seq', [(i, i ^ bits) for i in range(size)])  5.11 us
    ppermute x8, waiting for transfers between devices, swap(): return lax.ppermute(value, 'seq', [(i, i ^ bits) for i in range(size)])  4 us
    ppermute x1, waiting for transfers between devices, local(): same = lax.ppermute(same, 'seq', along)  3.7 us
    pallas_call x1, Pallas kernels, local(): kernel_call(stage_kernel, 'stage', [jax.ShapeDtypeStruct(mixing.shape, mi...  1.9 us
    ppermute x1, waiting for transfers between devices, local(): far = lax.ppermute(branch('far', jnp.bfloat16), 'seq', across)  1.65 us
    pallas_call x1, Pallas kernels, local(): kernel_call(norm_kernel, 'norm', [jax.ShapeDtypeStruct((tall, count), jnp...  1.23 us
    pallas_call x1, Pallas kernels, local(): kernel_call(functools.partial(strip_kernel, chips, rows, num, fine, packe...  1.1 us
  transfers between devices with their start and end apart: 11, of which 6 were waited for; matrix products, arithmetic and copies ran while one was open for 0% of the time, Pallas kernels for 31%

profile of v3, /device:TPU:0, one launch (start us, length us, event | category | flops | bytes accessed | tf_op | source)
XLA Modules:
  0.0 28.6 jit_solution(1085488979084756515)
XLA Ops:
  0.0 0.5 %collective-permute-start.7 = (bf16[12,128,1024]{2,1,0:T(8,128)(2,1)}, bf16[12,128,1024]{2,1,0:T(8,128)(2,1)S(1)}, u32[]{:S(2)}, u32[]{:S(2)}) collective-permute-start(bf16[12,128,1024]{2,1,0:T(8,128)(2,1)} %mix_hbm.1), channel_id=1, source_target_pairs={{0,4},{4,0},{8,12},{12,8},{16,20},{20,16},{24,28},{28,24},{1,5},{5... | collective-permute-start | bytes 9437192 | tf_op jit(solution)/shard_map/ppermute | solution.py:18
  0.5 1.2 %norm.1 = (bf16[144,256]{1,0:T(8,128)(2,1)S(1)}, bf16[144,256]{1,0:T(8,128)(2,1)S(1)}, bf16[144,256]{1,0:T(8,128)(2,1)S(1)}, bf16[144,256]{1,0:T(8,128)(2,1)S(1)}) custom-call(bf16[128,1024]{1,0:T(8,128)(2,1)} %tokens_hbm.1, f32[1,1024]{1,0:T(1,128)} %bitcast.1, f32[12,128]{1,0:T(8,128)} %filters_hbm.1), custom_call_target="tpu_custom_call" | custom-call | tf_op jit(solution)/shard_map/norm/pallas_call | solution.py:220
  1.7 2.6 %collective-permute-start = (bf16[144,256]{1,0:T(8,128)(2,1)S(1)}, bf16[144,256]{1,0:T(8,128)(2,1)S(1)}, u32[]{:S(2)}, u32[]{:S(2)}) collective-permute-start(bf16[144,256]{1,0:T(8,128)(2,1)S(1)} %get-tuple-element.14), channel_id=1, source_target_pairs={{0,8},{4,12},{8,0},{12,4},{16,24},{20,28},{24,16},{28,20},{1,9},{5... | collective-permute-start | bytes 221192 | tf_op jit(solution)/shard_map/ppermute | solution.py:18
  4.2 1.5 %collective-permute-start.1 = (bf16[144,256]{1,0:T(8,128)(2,1)S(1)}, bf16[144,256]{1,0:T(8,128)(2,1)S(1)}, u32[]{:S(2)}, u32[]{:S(2)}) collective-permute-start(bf16[144,256]{1,0:T(8,128)(2,1)S(1)} %get-tuple-element.15), channel_id=1, source_target_pairs={{0,16},{4,20},{8,24},{12,28},{16,0},{20,4},{24,8},{28,12},{1,17},{... | collective-permute-start | bytes 221192 | tf_op jit(solution)/shard_map/ppermute | solution.py:18
  5.8 0.0 collective-permute-start.2
  5.8 1.9 %stage.1 = (bf16[12,128,1024]{2,1,0:T(8,128)(2,1)S(1)}, bf16[144,256]{1,0:T(8,128)(2,1)S(1)}) custom-call(bf16[12,128,1024]{2,1,0:T(8,128)(2,1)} %mix_hbm.1, bf16[144,256]{1,0:T(8,128)(2,1)S(1)} %get-tuple-element.13.block_ref.refs_0_), custom_call_target="tpu_custom_call" | custom-call | tf_op jit(solution)/shard_map/stage/pallas_call | solution.py:235
  7.7 0.1 collective-permute-start.3
  7.8 0.0 collective-permute-done.refs_1_
  7.8 0.5 %collective-permute-start.4 = (bf16[144,256]{1,0:T(8,128)(2,1)S(1)}, bf16[144,256]{1,0:T(8,128)(2,1)S(1)}, u32[]{:S(2)}, u32[]{:S(2)}) collective-permute-start(bf16[144,256]{1,0:T(8,128)(2,1)S(1)} %collective-permute-done.refs_1_), channel_id=1, source_target_pairs={{0,4},{4,0},{8,12},{12,8},{16,20},{20,16},{24,28},{28,24},{1,5},{5... | collective-permute-start | bytes 221192 | tf_op jit(solution)/shard_map/ppermute | solution.py:18
  8.3 0.6 %collective-permute-done.1.refs_2_ = bf16[144,256]{1,0:T(8,128)(2,1)S(1)} collective-permute-done((bf16[144,256]{1,0:T(8,128)(2,1)S(1)}, bf16[144,256]{1,0:T(8,128)(2,1)S(1)}, u32[]{:S(2)}, u32[]{:S(2)}) %collective-permute-start.1) | collective-permute-done | bytes 73760 | tf_op jit(solution)/shard_map/ppermute | solution.py:18
  8.9 0.0 collective-permute-start.5
  8.9 2.1 %collective-permute-done.2.refs_3_ = bf16[144,256]{1,0:T(8,128)(2,1)S(1)} collective-permute-done((bf16[144,256]{1,0:T(8,128)(2,1)S(1)}, bf16[144,256]{1,0:T(8,128)(2,1)S(1)}, u32[]{:S(2)}, u32[]{:S(2)}) %collective-permute-start.2) | collective-permute-done | bytes 73760 | tf_op jit(solution)/shard_map/ppermute | solution.py:18
  11.0 0.0 collective-permute-start.6
  11.0 0.0 collective-permute-done.3.refs_4_
  11.0 0.0 collective-permute-done.4.refs_5_
  11.0 0.0 collective-permute-done.5.refs_6_
  11.0 1.2 %collective-permute-done.6.refs_7_ = bf16[144,256]{1,0:T(8,128)(2,1)S(1)} collective-permute-done((bf16[144,256]{1,0:T(8,128)(2,1)S(1)}, bf16[144,256]{1,0:T(8,128)(2,1)S(1)}, u32[]{:S(2)}, u32[]{:S(2)}) %collective-permute-start.6) | collective-permute-done | bytes 73760 | tf_op jit(solution)/shard_map/ppermute | solution.py:18
  12.3 1.1 %strip.1 = (bf16[1152,1024]{1,0:T(8,128)(2,1)S(1)}, bf16[384,1152]{1,0:T(8,128)(2,1)S(1)}) custom-call(bf16[144,256]{1,0:T(8,128)(2,1)S(1)} %get-tuple-element.13.block_ref.refs_0_, bf16[144,256]{1,0:T(8,128)(2,1)S(1)} %collective-permute-done.refs_1_, bf16[144,256]{1,0:T(8,128)(2,1)S(1)} %collective-permute-done.1.refs_2_, ...), custom_call_target="tpu_custom_call" | custom-call | tf_op jit(solution)/shard_map/strip/pallas_call | solution.py:259
  13.4 0.0 collective-permute-done.7.refs_3_
  13.4 2.0 %branch.7 = bf16[128,1024]{1,0:T(8,128)(2,1)S(1)} custom-call(bf16[1152,1024]{1,0:T(8,128)(2,1)S(1)} %get-tuple-element.18.refs_0_, bf16[384,1152]{1,0:T(8,128)(2,1)S(1)} %get-tuple-element.19.refs_1_, bf16[12,128,1024]{2,1,0:T(8,128)(2,1)S(1)} %get-tuple-element.20.refs_2_, bf16[12,128,1024]{2,1,0:T(8,128)(2,1)S(1)} %collective-permute-done.7.refs_3_), custom_call_target="tpu_custom_call" | custom-call | tf_op jit(solution)/shard_map/branch/pallas_call | solution.py:272
  15.4 0.2 collective-permute-start.9
  15.6 1.6 %branch.5 = bf16[128,1024]{1,0:T(8,128)(2,1)S(1)} custom-call(bf16[1152,1024]{1,0:T(8,128)(2,1)S(1)} %get-tuple-element.18.refs_0_, bf16[384,1152]{1,0:T(8,128)(2,1)S(1)} %get-tuple-element.19.refs_1_, bf16[12,128,1024]{2,1,0:T(8,128)(2,1)S(1)} %get-tuple-element.20.refs_2_, bf16[12,128,1024]{2,1,0:T(8,128)(2,1)S(1)} %collective-permute-done.7.refs_3_), custom_call_target="tpu_custom_call" | custom-call | tf_op jit(solution)/shard_map/branch/pallas_call | solution.py:272
  17.1 0.9 %collective-permute-start.8 = (bf16[128,1024]{1,0:T(8,128)(2,1)S(1)}, bf16[128,1024]{1,0:T(8,128)(2,1)S(1)}, u32[]{:S(2)}, u32[]{:S(2)}) collective-permute-start(bf16[128,1024]{1,0:T(8,128)(2,1)S(1)} %branch.5), channel_id=1, source_target_pairs={{0,12},{4,16},{8,4},{12,24},{16,28},{20,0},{24,20},{28,8},{1,13},{... | collective-permute-start | bytes 786440 | tf_op jit(solution)/shard_map/ppermute | solution.py:285
  18.0 1.6 %branch.6 = f32[128,1024]{1,0:T(8,128)S(1)} custom-call(bf16[1152,1024]{1,0:T(8,128)(2,1)S(1)} %get-tuple-element.18.refs_0_, bf16[384,1152]{1,0:T(8,128)(2,1)S(1)} %get-tuple-element.19.refs_1_, bf16[12,128,1024]{2,1,0:T(8,128)(2,1)S(1)} %get-tuple-element.20.refs_2_, bf16[12,128,1024]{2,1,0:T(8,128)(2,1)S(1)} %collective-permute-done.7.refs_3_), custom_call_target="tpu_custom_call" | custom-call | tf_op jit(solution)/shard_map/branch/pallas_call | solution.py:272
  19.6 1.7 %collective-permute-done.9 = bf16[128,1024]{1,0:T(8,128)(2,1)S(1)} collective-permute-done((bf16[128,1024]{1,0:T(8,128)(2,1)S(1)}, bf16[128,1024]{1,0:T(8,128)(2,1)S(1)}, u32[]{:S(2)}, u32[]{:S(2)}) %collective-permute-start.9) | collective-permute-done | bytes 262176 | tf_op jit(solution)/shard_map/ppermute | solution.py:284
  21.3 0.1 add_convert_fusion.1
  21.3 0.0 copy-start
  21.3 0.4 %collective-permute-start.10 = (bf16[128,1024]{1,0:T(8,128)(2,1)S(1)}, bf16[128,1024]{1,0:T(8,128)(2,1)S(1)}, u32[]{:S(2)}, u32[]{:S(2)}) collective-permute-start(bf16[128,1024]{1,0:T(8,128)(2,1)S(1)} %add_convert_fusion.1), channel_id=1, source_target_pairs={{0,8},{4,20},{8,0},{12,28},{16,24},{20,4},{24,16},{28,12},{1,9},{5... | collective-permute-start | bytes 786440 | tf_op jit(solution)/shard_map/ppermute | solution.py:287
  21.7 1.4 %branch.4 = f32[128,1024]{1,0:T(8,128)S(1)} custom-call(bf16[1152,1024]{1,0:T(8,128)(2,1)S(1)} %get-tuple-element.18.refs_0_, bf16[384,1152]{1,0:T(8,128)(2,1)S(1)} %get-tuple-element.19.refs_1_, bf16[12,128,1024]{2,1,0:T(8,128)(2,1)S(1)} %get-tuple-element.20.refs_2_, bf16[12,128,1024]{2,1,0:T(8,128)(2,1)S(1)} %collective-permute-done.7.refs_3_), custom_call_target="tpu_custom_call" | custom-call | tf_op jit(solution)/shard_map/branch/pallas_call | solution.py:272
  23.1 0.9 %collective-permute-done.8 = bf16[128,1024]{1,0:T(8,128)(2,1)S(1)} collective-permute-done((bf16[128,1024]{1,0:T(8,128)(2,1)S(1)}, bf16[128,1024]{1,0:T(8,128)(2,1)S(1)}, u32[]{:S(2)}, u32[]{:S(2)}) %collective-permute-start.8) | collective-permute-done | bytes 262176 | tf_op jit(solution)/shard_map/ppermute | solution.py:285
  24.1 3.7 %collective-permute-done.10 = bf16[128,1024]{1,0:T(8,128)(2,1)S(1)} collective-permute-done((bf16[128,1024]{1,0:T(8,128)(2,1)S(1)}, bf16[128,1024]{1,0:T(8,128)(2,1)S(1)}, u32[]{:S(2)}, u32[]{:S(2)}) %collective-permute-start.10) | collective-permute-done | bytes 262176 | tf_op jit(solution)/shard_map/ppermute | solution.py:287
  27.8 0.0 copy-done
  27.8 0.8 %add_convert_fusion = bf16[128,1024]{1,0:T(8,128)(2,1)} fusion(bf16[128,1024]{1,0:T(8,128)(2,1)S(1)} %collective-permute-done.10, bf16[128,1024]{1,0:T(8,128)(2,1)S(1)} %collective-permute-done.8, f32[128,1024]{1,0:T(8,128)S(1)} %branch.4, bf16[128,1024]{1,0:T(8,128)(2,1)S(1)} %copy-done), kind=kLoop, calls=%fused_computation | loop fusion | flops 917504 | bytes 1572864 | tf_op jit(solution)/shard_map/convert_element_type | solution.py:306
Async XLA Ops:
  0.0 13.4 %collective-permute-start.7 = (bf16[12,128,1024]{2,1,0:T(8,128)(2,1)}, bf16[12,128,1024]{2,1,0:T(8,128)(2,1)S(1)}, u32[]{:S(2)}, u32[]{:S(2)}) collective-permute-start(bf16[12,128,1024]{2,1,0:T(8,128)(2,1)} %mix_hbm.1), channel_id=1, source_target_pairs={{0,4},{4,0},{8,12},{12,8},{16,20},{20,16},{24,28},{28,24},{1,5},{5... | collective-permute-start | bytes 9437192 | tf_op jit(solution)/shard_map/ppermute | solution.py:18
  1.7 6.1 %collective-permute-start = (bf16[144,256]{1,0:T(8,128)(2,1)S(1)}, bf16[144,256]{1,0:T(8,128)(2,1)S(1)}, u32[]{:S(2)}, u32[]{:S(2)}) collective-permute-start(bf16[144,256]{1,0:T(8,128)(2,1)S(1)} %get-tuple-element.14), channel_id=1, source_target_pairs={{0,8},{4,12},{8,0},{12,4},{16,24},{20,28},{24,16},{28,20},{1,9},{5... | collective-permute-start | bytes 221192 | tf_op jit(solution)/shard_map/ppermute | solution.py:18
  4.2 4.7 %collective-permute-start.1 = (bf16[144,256]{1,0:T(8,128)(2,1)S(1)}, bf16[144,256]{1,0:T(8,128)(2,1)S(1)}, u32[]{:S(2)}, u32[]{:S(2)}) collective-permute-start(bf16[144,256]{1,0:T(8,128)(2,1)S(1)} %get-tuple-element.15), channel_id=1, source_target_pairs={{0,16},{4,20},{8,24},{12,28},{16,0},{20,4},{24,8},{28,12},{1,17},{... | collective-permute-start | bytes 221192 | tf_op jit(solution)/shard_map/ppermute | solution.py:18
  5.8 5.3 %collective-permute-start.2 = (bf16[144,256]{1,0:T(8,128)(2,1)S(1)}, bf16[144,256]{1,0:T(8,128)(2,1)S(1)}, u32[]{:S(2)}, u32[]{:S(2)}) collective-permute-start(bf16[144,256]{1,0:T(8,128)(2,1)S(1)} %get-tuple-element.16), channel_id=1, source_target_pairs={{0,24},{4,28},{8,16},{12,20},{16,8},{20,12},{24,0},{28,4},{1,25},{... | collective-permute-start | bytes 221192 | tf_op jit(solution)/shard_map/ppermute | solution.py:18
  7.7 3.3 %collective-permute-start.3 = (bf16[144,256]{1,0:T(8,128)(2,1)S(1)}, bf16[144,256]{1,0:T(8,128)(2,1)S(1)}, u32[]{:S(2)}, u32[]{:S(2)}) collective-permute-start(bf16[144,256]{1,0:T(8,128)(2,1)S(1)} %get-tuple-element.17), channel_id=1, source_target_pairs={{0,4},{4,0},{8,12},{12,8},{16,20},{20,16},{24,28},{28,24},{1,5},{5... | collective-permute-start | bytes 221192 | tf_op jit(solution)/shard_map/ppermute | solution.py:18
  7.8 3.2 %collective-permute-start.4 = (bf16[144,256]{1,0:T(8,128)(2,1)S(1)}, bf16[144,256]{1,0:T(8,128)(2,1)S(1)}, u32[]{:S(2)}, u32[]{:S(2)}) collective-permute-start(bf16[144,256]{1,0:T(8,128)(2,1)S(1)} %collective-permute-done.refs_1_), channel_id=1, source_target_pairs={{0,4},{4,0},{8,12},{12,8},{16,20},{20,16},{24,28},{28,24},{1,5},{5... | collective-permute-start | bytes 221192 | tf_op jit(solution)/shard_map/ppermute | solution.py:18
  8.9 2.1 %collective-permute-start.5 = (bf16[144,256]{1,0:T(8,128)(2,1)S(1)}, bf16[144,256]{1,0:T(8,128)(2,1)S(1)}, u32[]{:S(2)}, u32[]{:S(2)}) collective-permute-start(bf16[144,256]{1,0:T(8,128)(2,1)S(1)} %collective-permute-done.1.refs_2_), channel_id=1, source_target_pairs={{0,4},{4,0},{8,12},{12,8},{16,20},{20,16},{24,28},{28,24},{1,5},{5... | collective-permute-start | bytes 221192 | tf_op jit(solution)/shard_map/ppermute | solution.py:18
  11.0 1.3 %collective-permute-start.6 = (bf16[144,256]{1,0:T(8,128)(2,1)S(1)}, bf16[144,256]{1,0:T(8,128)(2,1)S(1)}, u32[]{:S(2)}, u32[]{:S(2)}) collective-permute-start(bf16[144,256]{1,0:T(8,128)(2,1)S(1)} %collective-permute-done.2.refs_3_), channel_id=1, source_target_pairs={{0,4},{4,0},{8,12},{12,8},{16,20},{20,16},{24,28},{28,24},{1,5},{5... | collective-permute-start | bytes 221192 | tf_op jit(solution)/shard_map/ppermute | solution.py:18
  15.4 5.8 %collective-permute-start.9 = (bf16[128,1024]{1,0:T(8,128)(2,1)S(1)}, bf16[128,1024]{1,0:T(8,128)(2,1)S(1)}, u32[]{:S(2)}, u32[]{:S(2)}) collective-permute-start(bf16[128,1024]{1,0:T(8,128)(2,1)S(1)} %branch.7), channel_id=1, source_target_pairs={{0,12},{4,16},{8,4},{12,24},{16,28},{20,0},{24,20},{28,8},{1,13},{... | collective-permute-start | bytes 786440 | tf_op jit(solution)/shard_map/ppermute | solution.py:284
  17.1 6.9 %collective-permute-start.8 = (bf16[128,1024]{1,0:T(8,128)(2,1)S(1)}, bf16[128,1024]{1,0:T(8,128)(2,1)S(1)}, u32[]{:S(2)}, u32[]{:S(2)}) collective-permute-start(bf16[128,1024]{1,0:T(8,128)(2,1)S(1)} %branch.5), channel_id=1, source_target_pairs={{0,12},{4,16},{8,4},{12,24},{16,28},{20,0},{24,20},{28,8},{1,13},{... | collective-permute-start | bytes 786440 | tf_op jit(solution)/shard_map/ppermute | solution.py:285
  21.3 6.5 %copy-start = (bf16[128,1024]{1,0:T(8,128)(2,1)S(1)}, bf16[128,1024]{1,0:T(8,128)(2,1)}, u32[]{:S(2)}) copy-start(bf16[128,1024]{1,0:T(8,128)(2,1)} %tokens_hbm.1) | copy-start | bytes 786436
  21.3 6.4 %collective-permute-start.10 = (bf16[128,1024]{1,0:T(8,128)(2,1)S(1)}, bf16[128,1024]{1,0:T(8,128)(2,1)S(1)}, u32[]{:S(2)}, u32[]{:S(2)}) collective-permute-start(bf16[128,1024]{1,0:T(8,128)(2,1)S(1)} %add_convert_fusion.1), channel_id=1, source_target_pairs={{0,8},{4,20},{8,0},{12,28},{16,24},{20,4},{24,16},{28,12},{1,9},{5... | collective-permute-start | bytes 786440 | tf_op jit(solution)/shard_map/ppermute | solution.py:287

commit v4 on v3

--- a/solution.py
+++ b/solution.py
@@ -85,10 +85,10 @@
 
 def aim(chip, core, kind):
     if kind == "far":
-        return chip ^ 3, 1 - core
+        return chip ^ 3, core
     if kind == "own":
         return chip, core
-    return chip ^ (1 + core), core if kind == "same" else 1 - core
+    return chip ^ (1 + core), core if kind == "early" else 1 - core
 
 
 def project(feats, mix_ref, pair_mix_ref):
@@ -105,51 +105,96 @@
     )
 
 
-def strip_kernel(chips, rows, num, fine, packed, *refs):
-    own = refs[:chips]
-    pair = refs[chips : 2 * chips]
-    refs = refs[2 * chips :]
-    if not packed:
-        taps_ref, *refs = refs
-    signal, strip, base = refs
+def block_places(chips, shifts):
     index = lax.axis_index("seq")
     chip = index // 2
     core = index % 2
+    first = [core if s == 0 else 1 - core for s in shifts]
+    return [(2 * (chip ^ s) + q, 2 * (chip ^ s) + 1 - q) for s, q in zip(shifts, first, strict=True)]
+
+
+def rotate_taps(block_refs, places, rows, num, fine, out_ref, devices):
+    for block, place in zip(block_refs, places, strict=True):
+        taps = block[rows:, 0:rows].astype(jnp.float32)
+        at = pl.multiple_of((devices - 1 - place) * rows, rows)
+        for k in range(num):
+            line = jnp.broadcast_to(taps[k : k + 1, :], (8, rows))
+            line = pltpu.roll(line, rows - fine + 1, 1, stride=1, stride_axis=0)
+            lines = [line] + [pltpu.roll(line, step, 1) for step in range(8, fine, 8)]
+            out_ref[k * fine : (k + 1) * fine, pl.ds(at, rows)] = jnp.concatenate(
+                lines, axis=0
+            ).astype(jnp.bfloat16)
+
+
+def rotate_kernel(chips, shifts, rows, num, fine, *refs):
+    *blocks, out_ref = refs
+    places = [place for pair in zip(*block_places(chips, shifts), strict=True) for place in pair]
+    rotate_taps(blocks, places, rows, num, fine, out_ref, 2 * chips)
+
+
+def merge_kernel(chips, shifts, done, rows, num, fine, *refs):
+    own = refs[:chips]
+    pair = refs[chips : 2 * chips]
+    turned_ref, signal, strip, lines = refs[2 * chips :]
     devices = 2 * chips
     length = devices * rows
     groups = rows // fine
     count = signal.shape[1] // groups
     half = count // 2
-    wide = length + 2 * rows
+    core = lax.axis_index("seq") % 2
     late = [rows - fine * (g + 1) for g in range(groups)]
     for g in range(groups - 1):
         signal[0 : late[g], g * count : (g + 1) * count] = jnp.zeros((late[g], count), signal.dtype)
-    base[:, length:] = jnp.zeros((base.shape[0], 2 * rows), jnp.float32)
-    for shift in range(chips):
-        for which, block in enumerate((own[shift], pair[shift])):
-            place = 2 * (chip ^ shift) + (core if which == 0 else 1 - core)
+    places = block_places(chips, shifts)
+    for own_block, pair_block, both in zip(own, pair, places, strict=True):
+        for block, place in zip((own_block, pair_block), both, strict=True):
             value = block[0:rows, :]
             turned = jnp.concatenate([value[:, half:], value[:, :half]], axis=1)
             value = jnp.where(core == 0, value, turned)
             for g in range(groups):
                 at = pl.multiple_of(place * rows + late[g], fine)
                 signal[pl.ds(at, rows), g * count : (g + 1) * count] = value
-            if packed:
-                at = pl.multiple_of((devices - 1 - place) * rows, rows)
-                base[:, pl.ds(at, rows)] = block[rows:, 0:rows].astype(jnp.float32)
-    if not packed:
-        base[:, 0:length] = taps_ref[...]
+    lines[...] = turned_ref[...]
+    for shift in range(done, chips):
+        rotate_taps((own[shift], pair[shift]), places[shift], rows, num, fine, lines, devices)
+    row = lax.broadcasted_iota(jnp.int32, (fine, rows), 0)
+    lane = lax.broadcasted_iota(jnp.int32, (fine, rows), 1)
+    here = lane - row < rows - fine + 1
+    nothing = jnp.zeros((fine, rows), jnp.bfloat16)
+    for k in range(num):
+        cut = slice(k * fine, (k + 1) * fine)
+        parts = [lines[cut, b * rows : (b + 1) * rows] for b in range(devices)] + [nothing]
+        for b in range(devices):
+            strip[cut, b * rows : (b + 1) * rows] = jnp.where(here, parts[b], parts[b + 1])
+        strip[cut, length:] = nothing
+
+
+def strip_kernel(chips, rows, num, *refs):
+    own = refs[:chips]
+    pair = refs[chips : 2 * chips]
+    taps_ref, signal, strip = refs[2 * chips :]
+    length = 2 * chips * rows
+    half = signal.shape[1] // 2
+    wide = length + 2 * rows
+    core = lax.axis_index("seq") % 2
+    places = block_places(chips, range(chips))
+    for own_block, pair_block, both in zip(own, pair, places, strict=True):
+        for block, place in zip((own_block, pair_block), both, strict=True):
+            value = block[...]
+            turned = jnp.concatenate([value[:, half:], value[:, :half]], axis=1)
+            value = jnp.where(core == 0, value, turned)
+            signal[pl.ds(pl.multiple_of(place * rows, rows), rows), :] = value
 
     def one_filter(k, carry):
-        line = jnp.broadcast_to(base[pl.ds(k, 1), :], (8, wide))
-        line = pltpu.roll(line, wide - fine + 1, 1, stride=1, stride_axis=0)
-        for step in range(fine // 16):
+        line = jnp.broadcast_to(taps_ref[pl.ds(k, 1), :], (8, wide))
+        line = pltpu.roll(line, wide - rows + 1, 1, stride=1, stride_axis=0)
+        for step in range(rows // 16):
             pieces = [pltpu.roll(line, 16 * step + 8 * h, 1)[:, : length + rows] for h in (0, 1)]
-            at = pl.multiple_of(k * fine + 16 * step, 16)
+            at = pl.multiple_of(k * rows + 16 * step, 16)
             strip[pl.ds(at, 16), :] = jnp.concatenate(pieces, axis=0).astype(jnp.bfloat16)
         return carry
 
-    lax.fori_loop(0, num, one_filter, 0, unroll=num if packed else 1)
+    lax.fori_loop(0, num, one_filter, 0)
 
 
 def branch_kernel(chips, rows, fine, kind, *refs):
@@ -212,11 +257,10 @@
     num, span = filters.shape
     length = devices * rows
     count = width // chips
-    packed = count >= span
-    relay = chips == 4 and packed and count % 256 == 0
+    relay = chips == 4 and count % 256 == 0 and span == rows and num <= EXTRA
     pair_mixing = swap(mixing, 1, devices)
     fine = 32 if relay else rows
-    tall = rows + (EXTRA if packed else 0)
+    tall = rows + (EXTRA if relay else 0)
     blocks = kernel_call(
         norm_kernel,
         "norm",
@@ -230,8 +274,6 @@
             pltpu.SemaphoreType.DMA((3,)),
         ],
     )(in_hbm(tokens), in_hbm(norm_gain.reshape(1, width)), in_hbm(filters))
-    far = [swap(blocks[s], 2 * s, devices) for s in reversed(range(1, chips))]
-    own = [blocks[0], *reversed(far)]
     near_mixing, first = kernel_call(
         stage_kernel,
         "stage",
@@ -243,27 +285,46 @@
         8 * MIB,
         [pltpu.SemaphoreType.DMA(())],
     )(in_hbm(mixing), blocks[0])
-    pair = [swap(block, 1, devices) for block in (first, *own[1:])]
-    operands = [*own, *pair]
-    specs = [VMEM] * (2 * chips)
-    feats = pltpu.VMEM((rows, num * count), jnp.bfloat16)
+    work = 2 * num * rows * count * (width + length)
+    shifts = [0, 3, 1, 2] if relay else list(range(chips))
+    own = {s: swap(blocks[s], 2 * s + 1, devices) for s in reversed(shifts) if s}
+    own[0] = first
+    pair = {s: swap(own[s], 1, devices) for s in shifts}
+    own[0] = blocks[0]
+    ends = [own[s] for s in shifts] + [pair[s] for s in shifts]
     shapes = [
         jax.ShapeDtypeStruct((length + rows, rows // fine * count), jnp.bfloat16),
         jax.ShapeDtypeStruct((num * fine, length + rows), jnp.bfloat16),
     ]
-    scratch = [pltpu.VMEM((EXTRA, length + 2 * rows), jnp.float32)]
-    if not packed:
+    if relay:
+        done = chips - 1
+        lines = jax.ShapeDtypeStruct((num * fine, length), jnp.bfloat16)
+        ready = ends[:done] + ends[chips : chips + done]
+        turned = kernel_call(
+            functools.partial(rotate_kernel, chips, shifts[:done], rows, num, fine),
+            "rotate",
+            lines,
+            [VMEM] * len(ready),
+            8 * MIB,
+        )(*ready)
+        signal, strip = kernel_call(
+            functools.partial(merge_kernel, chips, shifts, done, rows, num, fine),
+            "merge",
+            shapes,
+            [VMEM] * (2 * chips + 1),
+            16 * MIB,
+            [pltpu.VMEM(lines.shape, lines.dtype)],
+        )(*ends, turned)
+    else:
         taps = lax.all_gather(filters, "seq", axis=1, tiled=True)[:, ::-1]
-        operands.append(jnp.pad(taps, ((0, EXTRA - num), (0, 0))))
-        specs.append(VMEM)
-    signal, strip = kernel_call(
-        functools.partial(strip_kernel, chips, rows, num, fine, packed),
-        "strip",
-        shapes,
-        specs,
-        24 * MIB if relay else 48 * MIB,
-        scratch,
-    )(*operands)
+        taps = jnp.pad(taps, ((0, EXTRA - num), (0, 2 * rows)))
+        signal, strip = kernel_call(
+            functools.partial(strip_kernel, chips, rows, num),
+            "strip",
+            shapes,
+            [VMEM] * (2 * chips + 1),
+            48 * MIB,
+        )(*ends, taps)
     fixed = [signal, strip, near_mixing, pair_mixing]
     total = tokens.astype(jnp.float32)
     if relay:
@@ -275,18 +336,18 @@
                 jax.ShapeDtypeStruct((rows, width), dtype),
                 [VMEM] * 4,
                 24 * MIB,
-                [feats],
+                [pltpu.VMEM((rows, num * count), jnp.bfloat16)],
             )(*fixed)
 
         pairs = [(c, q) for c in range(chips) for q in range(2)]
         across = [(2 * c + q, 2 * (c ^ (1 + q)) + 1 - q) for c, q in pairs]
         along = [(2 * c + q, 2 * (c ^ (1 + q)) + q) for c, q in pairs]
         far = lax.ppermute(branch("far", jnp.bfloat16), "seq", across)
-        other = lax.ppermute(branch("other", jnp.bfloat16), "seq", across)
-        same = (branch("same", jnp.float32) + far.astype(jnp.float32)).astype(jnp.bfloat16)
-        same = lax.ppermute(same, "seq", along)
+        early = lax.ppermute(branch("early", jnp.bfloat16), "seq", along)
+        late = (branch("late", jnp.float32) + far.astype(jnp.float32)).astype(jnp.bfloat16)
+        late = lax.ppermute(late, "seq", across)
         total = total + branch("own", jnp.float32)
-        sent = [other, same]
+        sent = [early, late]
     else:
 
         def branch(shift):

time: 28.8 us -> 27.4 us (0.951)
  waiting for transfers between devices: 10.3 us -> 6.64 us
  starting transfers between devices: 6.56 us -> 8.35 us
  Pallas kernels: 10.7 us -> 11.2 us
    ppermute x8, waiting for transfers between devices: 4 us -> 2.32 us  [swap(): return lax.ppermute(value, 'seq', [(i, i ^ bits) for i in range(size)])]
    ppermute x2, waiting for transfers between devices: 4.65 us -> 3.31 us  [the longest x1 2.59 us: local(): late = lax.ppermute(late, 'seq', across)]
    ppermute x1, starting transfers between devices: 0.17 us -> 1.17 us  [local(): far = lax.ppermute(branch('far', jnp.bfloat16), 'seq', across)]
    ppermute x1, waiting for transfers between devices: 1.65 us -> 1.01 us  [local(): far = lax.ppermute(branch('far', jnp.bfloat16), 'seq', across)]
    pallas_call x1 -> x2, Pallas kernels: 1.1 us -> 1.58 us  [the longest x1 1.04 us: local(): kernel_call(functools.partial(rotate_kernel, chips, shifts[:done], rows,...]
    ppermute x2, starting transfers between devices: 1.29 us -> 1.69 us  [the longest x1 1.17 us: local(): late = lax.ppermute(late, 'seq', across)]
    ppermute x8, starting transfers between devices: 5.11 us -> 5.49 us  [swap(): return lax.ppermute(value, 'seq', [(i, i ^ bits) for i in range(size)])]
  transfers between devices with their start and end apart: 11 -> 11, of which waited for: 6 -> 5; matrix products, arithmetic and copies ran while one was open for 0% -> 0% of each run, Pallas kernels for 31% -> 34%
where the time goes in v4:
time: 27.4 us; the launch traced here: 27.2 us
  Pallas kernels  11.2 us (41%)
  starting transfers between devices  8.35 us (30%)
  waiting for transfers between devices  6.64 us (24%)
  other arithmetic  0.9 us (3%)
    pallas_call x4, Pallas kernels, branch(): kernel_call(functools.partial(branch_kernel, chips, rows, fine, kind), 'b...  6.51 us
    ppermute x8, starting transfers between devices, swap(): return lax.ppermute(value, 'seq', [(i, i ^ bits) for i in range(size)])  5.49 us
    ppermute x1, waiting for transfers between devices, local(): late = lax.ppermute(late, 'seq', across)  2.59 us
    ppermute x8, waiting for transfers between devices, swap(): return lax.ppermute(value, 'seq', [(i, i ^ bits) for i in range(size)])  2.32 us
    pallas_call x1, Pallas kernels, local(): kernel_call(stage_kernel, 'stage', [jax.ShapeDtypeStruct(mixing.shape, mi...  1.9 us
    pallas_call x1, Pallas kernels, local(): kernel_call(norm_kernel, 'norm', [jax.ShapeDtypeStruct((tall, count), jnp...  1.23 us
    ppermute x1, starting transfers between devices, local(): late = lax.ppermute(late, 'seq', across)  1.17 us
    ppermute x1, starting transfers between devices, local(): far = lax.ppermute(branch('far', jnp.bfloat16), 'seq', across)  1.17 us
  transfers between devices with their start and end apart: 11, of which 5 were waited for; matrix products, arithmetic and copies ran while one was open for 0% of the time, Pallas kernels for 34%

profile of v4, /device:TPU:0, one launch (start us, length us, event | category | flops | bytes accessed | tf_op | source)
XLA Modules:
  0.0 27.2 jit_solution(2067709653552237364)
XLA Ops:
  0.0 0.5 %collective-permute-start.7 = (bf16[12,128,1024]{2,1,0:T(8,128)(2,1)}, bf16[12,128,1024]{2,1,0:T(8,128)(2,1)S(1)}, u32[]{:S(2)}, u32[]{:S(2)}) collective-permute-start(bf16[12,128,1024]{2,1,0:T(8,128)(2,1)} %mix_hbm.1), channel_id=1, source_target_pairs={{0,4},{4,0},{8,12},{12,8},{16,20},{20,16},{24,28},{28,24},{1,5},{5... | collective-permute-start | bytes 9437192 | tf_op jit(solution)/shard_map/ppermute | solution.py:18
  0.5 1.2 %norm.1 = (bf16[144,256]{1,0:T(8,128)(2,1)S(1)}, bf16[144,256]{1,0:T(8,128)(2,1)S(1)}, bf16[144,256]{1,0:T(8,128)(2,1)S(1)}, bf16[144,256]{1,0:T(8,128)(2,1)S(1)}) custom-call(bf16[128,1024]{1,0:T(8,128)(2,1)} %tokens_hbm.1, f32[1,1024]{1,0:T(1,128)} %bitcast.1, f32[12,128]{1,0:T(8,128)} %filters_hbm.1), custom_call_target="tpu_custom_call" | custom-call | tf_op jit(solution)/shard_map/norm/pallas_call | solution.py:264
  1.7 3.6 %collective-permute-start = (bf16[144,256]{1,0:T(8,128)(2,1)S(1)}, bf16[144,256]{1,0:T(8,128)(2,1)S(1)}, u32[]{:S(2)}, u32[]{:S(2)}) collective-permute-start(bf16[144,256]{1,0:T(8,128)(2,1)S(1)} %get-tuple-element.14), channel_id=1, source_target_pairs={{0,28},{4,24},{8,20},{12,16},{16,12},{20,8},{24,4},{28,0},{1,29},{... | collective-permute-start | bytes 221192 | tf_op jit(solution)/shard_map/ppermute | solution.py:18
  5.3 0.1 collective-permute-start.1
  5.5 0.1 collective-permute-start.2
  5.6 1.9 %stage.1 = (bf16[12,128,1024]{2,1,0:T(8,128)(2,1)S(1)}, bf16[144,256]{1,0:T(8,128)(2,1)S(1)}) custom-call(bf16[12,128,1024]{2,1,0:T(8,128)(2,1)} %mix_hbm.1, bf16[144,256]{1,0:T(8,128)(2,1)S(1)} %get-tuple-element.13.block_ref.refs_0_), custom_call_target="tpu_custom_call" | custom-call | tf_op jit(solution)/shard_map/stage/pallas_call | solution.py:277
  7.5 0.6 %collective-permute-start.3 = (bf16[144,256]{1,0:T(8,128)(2,1)S(1)}, bf16[144,256]{1,0:T(8,128)(2,1)S(1)}, u32[]{:S(2)}, u32[]{:S(2)}) collective-permute-start(bf16[144,256]{1,0:T(8,128)(2,1)S(1)} %get-tuple-element.17), channel_id=1, source_target_pairs={{0,4},{4,0},{8,12},{12,8},{16,20},{20,16},{24,28},{28,24},{1,5},{5... | collective-permute-start | bytes 221192 | tf_op jit(solution)/shard_map/ppermute | solution.py:18
  8.0 0.0 collective-permute-done.refs_1_
  8.0 0.1 collective-permute-start.4
  8.1 1.6 %collective-permute-done.1.refs_2_ = bf16[144,256]{1,0:T(8,128)(2,1)S(1)} collective-permute-done((bf16[144,256]{1,0:T(8,128)(2,1)S(1)}, bf16[144,256]{1,0:T(8,128)(2,1)S(1)}, u32[]{:S(2)}, u32[]{:S(2)}) %collective-permute-start.1) | collective-permute-done | bytes 73760 | tf_op jit(solution)/shard_map/ppermute | solution.py:18
  9.7 0.1 collective-permute-start.5
  9.8 0.0 collective-permute-done.2.refs_3_
  9.8 0.4 %collective-permute-start.6 = (bf16[144,256]{1,0:T(8,128)(2,1)S(1)}, bf16[144,256]{1,0:T(8,128)(2,1)S(1)}, u32[]{:S(2)}, u32[]{:S(2)}) collective-permute-start(bf16[144,256]{1,0:T(8,128)(2,1)S(1)} %collective-permute-done.2.refs_3_), channel_id=1, source_target_pairs={{0,4},{4,0},{8,12},{12,8},{16,20},{20,16},{24,28},{28,24},{1,5},{5... | collective-permute-start | bytes 221192 | tf_op jit(solution)/shard_map/ppermute | solution.py:18
  10.2 0.0 collective-permute-done.3.refs_3_.refs_4_
  10.2 0.0 collective-permute-done.4.refs_4_.refs_5_
  10.2 0.7 %collective-permute-done.5.refs_5_.refs_6_ = bf16[144,256]{1,0:T(8,128)(2,1)S(1)} collective-permute-done((bf16[144,256]{1,0:T(8,128)(2,1)S(1)}, bf16[144,256]{1,0:T(8,128)(2,1)S(1)}, u32[]{:S(2)}, u32[]{:S(2)}) %collective-permute-start.5) | collective-permute-done | bytes 73760 | tf_op jit(solution)/shard_map/ppermute | solution.py:18
  11.0 1.0 %rotate.1.refs_8_ = bf16[384,1024]{1,0:T(8,128)(2,1)S(1)} custom-call(bf16[144,256]{1,0:T(8,128)(2,1)S(1)} %get-tuple-element.13.block_ref.refs_0_, bf16[144,256]{1,0:T(8,128)(2,1)S(1)} %collective-permute-done.refs_1_, bf16[144,256]{1,0:T(8,128)(2,1)S(1)} %collective-permute-done.1.refs_2_, bf16[144,256]{1,0:T(8,128)(2,1)S(1)} %collective-permute-done.3.refs_3_.refs_4_, ...), custom_call_target="tpu_custom_call" | custom-call | tf_op jit(solution)/shard_map/rotate/pallas_call | solution.py:303
  12.0 0.0 collective-permute-done.6.refs_7_
  12.0 0.5 %merge.1 = (bf16[1152,1024]{1,0:T(8,128)(2,1)S(1)}, bf16[384,1152]{1,0:T(8,128)(2,1)S(1)}) custom-call(bf16[144,256]{1,0:T(8,128)(2,1)S(1)} %get-tuple-element.13.block_ref.refs_0_, bf16[144,256]{1,0:T(8,128)(2,1)S(1)} %collective-permute-done.refs_1_, bf16[144,256]{1,0:T(8,128)(2,1)S(1)} %collective-permute-done.1.refs_2_, ...), custom_call_target="tpu_custom_call" | custom-call | tf_op jit(solution)/shard_map/merge/pallas_call | solution.py:310
  12.6 0.0 collective-permute-done.7.refs_3_
  12.6 2.0 %branch.7 = bf16[128,1024]{1,0:T(8,128)(2,1)S(1)} custom-call(bf16[1152,1024]{1,0:T(8,128)(2,1)S(1)} %get-tuple-element.18.refs_0_, bf16[384,1152]{1,0:T(8,128)(2,1)S(1)} %get-tuple-element.19.refs_1_, bf16[12,128,1024]{2,1,0:T(8,128)(2,1)S(1)} %get-tuple-element.20.refs_2_, bf16[12,128,1024]{2,1,0:T(8,128)(2,1)S(1)} %collective-permute-done.7.refs_3_), custom_call_target="tpu_custom_call" | custom-call | tf_op jit(solution)/shard_map/branch/pallas_call | solution.py:333
  14.6 1.2 %collective-permute-start.9 = (bf16[128,1024]{1,0:T(8,128)(2,1)S(1)}, bf16[128,1024]{1,0:T(8,128)(2,1)S(1)}, u32[]{:S(2)}, u32[]{:S(2)}) collective-permute-start(bf16[128,1024]{1,0:T(8,128)(2,1)S(1)} %branch.7), channel_id=1, source_target_pairs={{0,12},{4,16},{8,4},{12,24},{16,28},{20,0},{24,20},{28,8},{1,13},{... | collective-permute-start | bytes 786440 | tf_op jit(solution)/shard_map/ppermute | solution.py:345
  15.8 1.6 %branch.5 = bf16[128,1024]{1,0:T(8,128)(2,1)S(1)} custom-call(bf16[1152,1024]{1,0:T(8,128)(2,1)S(1)} %get-tuple-element.18.refs_0_, bf16[384,1152]{1,0:T(8,128)(2,1)S(1)} %get-tuple-element.19.refs_1_, bf16[12,128,1024]{2,1,0:T(8,128)(2,1)S(1)} %get-tuple-element.20.refs_2_, bf16[12,128,1024]{2,1,0:T(8,128)(2,1)S(1)} %collective-permute-done.7.refs_3_), custom_call_target="tpu_custom_call" | custom-call | tf_op jit(solution)/shard_map/branch/pallas_call | solution.py:333
  17.3 0.5 %collective-permute-start.8 = (bf16[128,1024]{1,0:T(8,128)(2,1)S(1)}, bf16[128,1024]{1,0:T(8,128)(2,1)S(1)}, u32[]{:S(2)}, u32[]{:S(2)}) collective-permute-start(bf16[128,1024]{1,0:T(8,128)(2,1)S(1)} %branch.5), channel_id=1, source_target_pairs={{0,8},{4,20},{8,0},{12,28},{16,24},{20,4},{24,16},{28,12},{1,9},{5... | collective-permute-start | bytes 786440 | tf_op jit(solution)/shard_map/ppermute | solution.py:346
  17.9 1.6 %branch.6 = f32[128,1024]{1,0:T(8,128)S(1)} custom-call(bf16[1152,1024]{1,0:T(8,128)(2,1)S(1)} %get-tuple-element.18.refs_0_, bf16[384,1152]{1,0:T(8,128)(2,1)S(1)} %get-tuple-element.19.refs_1_, bf16[12,128,1024]{2,1,0:T(8,128)(2,1)S(1)} %get-tuple-element.20.refs_2_, bf16[12,128,1024]{2,1,0:T(8,128)(2,1)S(1)} %collective-permute-done.7.refs_3_), custom_call_target="tpu_custom_call" | custom-call | tf_op jit(solution)/shard_map/branch/pallas_call | solution.py:333
  19.4 1.0 %collective-permute-done.9 = bf16[128,1024]{1,0:T(8,128)(2,1)S(1)} collective-permute-done((bf16[128,1024]{1,0:T(8,128)(2,1)S(1)}, bf16[128,1024]{1,0:T(8,128)(2,1)S(1)}, u32[]{:S(2)}, u32[]{:S(2)}) %collective-permute-start.9) | collective-permute-done | bytes 262176 | tf_op jit(solution)/shard_map/ppermute | solution.py:345
  20.4 0.1 add_convert_fusion.1
  20.5 0.0 copy-start
  20.5 1.2 %collective-permute-start.10 = (bf16[128,1024]{1,0:T(8,128)(2,1)S(1)}, bf16[128,1024]{1,0:T(8,128)(2,1)S(1)}, u32[]{:S(2)}, u32[]{:S(2)}) collective-permute-start(bf16[128,1024]{1,0:T(8,128)(2,1)S(1)} %add_convert_fusion.1), channel_id=1, source_target_pairs={{0,12},{4,16},{8,4},{12,24},{16,28},{20,0},{24,20},{28,8},{1,13},{... | collective-permute-start | bytes 786440 | tf_op jit(solution)/shard_map/ppermute | solution.py:348
  21.7 1.4 %branch.4 = f32[128,1024]{1,0:T(8,128)S(1)} custom-call(bf16[1152,1024]{1,0:T(8,128)(2,1)S(1)} %get-tuple-element.18.refs_0_, bf16[384,1152]{1,0:T(8,128)(2,1)S(1)} %get-tuple-element.19.refs_1_, bf16[12,128,1024]{2,1,0:T(8,128)(2,1)S(1)} %get-tuple-element.20.refs_2_, bf16[12,128,1024]{2,1,0:T(8,128)(2,1)S(1)} %collective-permute-done.7.refs_3_), custom_call_target="tpu_custom_call" | custom-call | tf_op jit(solution)/shard_map/branch/pallas_call | solution.py:333
  23.1 0.7 %collective-permute-done.8 = bf16[128,1024]{1,0:T(8,128)(2,1)S(1)} collective-permute-done((bf16[128,1024]{1,0:T(8,128)(2,1)S(1)}, bf16[128,1024]{1,0:T(8,128)(2,1)S(1)}, u32[]{:S(2)}, u32[]{:S(2)}) %collective-permute-start.8) | collective-permute-done | bytes 262176 | tf_op jit(solution)/shard_map/ppermute | solution.py:346
  23.8 2.6 %collective-permute-done.10 = bf16[128,1024]{1,0:T(8,128)(2,1)S(1)} collective-permute-done((bf16[128,1024]{1,0:T(8,128)(2,1)S(1)}, bf16[128,1024]{1,0:T(8,128)(2,1)S(1)}, u32[]{:S(2)}, u32[]{:S(2)}) %collective-permute-start.10) | collective-permute-done | bytes 262176 | tf_op jit(solution)/shard_map/ppermute | solution.py:348
  26.4 0.0 copy-done
  26.4 0.8 %add_convert_fusion = bf16[128,1024]{1,0:T(8,128)(2,1)} fusion(bf16[128,1024]{1,0:T(8,128)(2,1)S(1)} %collective-permute-done.10, bf16[128,1024]{1,0:T(8,128)(2,1)S(1)} %collective-permute-done.8, f32[128,1024]{1,0:T(8,128)S(1)} %branch.4, bf16[128,1024]{1,0:T(8,128)(2,1)S(1)} %copy-done), kind=kLoop, calls=%fused_computation | loop fusion | flops 917504 | bytes 1572864 | tf_op jit(solution)/shard_map/convert_element_type | solution.py:367
Async XLA Ops:
  0.0 12.6 %collective-permute-start.7 = (bf16[12,128,1024]{2,1,0:T(8,128)(2,1)}, bf16[12,128,1024]{2,1,0:T(8,128)(2,1)S(1)}, u32[]{:S(2)}, u32[]{:S(2)}) collective-permute-start(bf16[12,128,1024]{2,1,0:T(8,128)(2,1)} %mix_hbm.1), channel_id=1, source_target_pairs={{0,4},{4,0},{8,12},{12,8},{16,20},{20,16},{24,28},{28,24},{1,5},{5... | collective-permute-start | bytes 9437192 | tf_op jit(solution)/shard_map/ppermute | solution.py:18
  1.7 6.4 %collective-permute-start = (bf16[144,256]{1,0:T(8,128)(2,1)S(1)}, bf16[144,256]{1,0:T(8,128)(2,1)S(1)}, u32[]{:S(2)}, u32[]{:S(2)}) collective-permute-start(bf16[144,256]{1,0:T(8,128)(2,1)S(1)} %get-tuple-element.14), channel_id=1, source_target_pairs={{0,28},{4,24},{8,20},{12,16},{16,12},{20,8},{24,4},{28,0},{1,29},{... | collective-permute-start | bytes 221192 | tf_op jit(solution)/shard_map/ppermute | solution.py:18
  5.3 4.4 %collective-permute-start.1 = (bf16[144,256]{1,0:T(8,128)(2,1)S(1)}, bf16[144,256]{1,0:T(8,128)(2,1)S(1)}, u32[]{:S(2)}, u32[]{:S(2)}) collective-permute-start(bf16[144,256]{1,0:T(8,128)(2,1)S(1)} %get-tuple-element.15), channel_id=1, source_target_pairs={{0,12},{4,8},{8,4},{12,0},{16,28},{20,24},{24,20},{28,16},{1,13},{... | collective-permute-start | bytes 221192 | tf_op jit(solution)/shard_map/ppermute | solution.py:18
  5.5 4.4 %collective-permute-start.2 = (bf16[144,256]{1,0:T(8,128)(2,1)S(1)}, bf16[144,256]{1,0:T(8,128)(2,1)S(1)}, u32[]{:S(2)}, u32[]{:S(2)}) collective-permute-start(bf16[144,256]{1,0:T(8,128)(2,1)S(1)} %get-tuple-element.16), channel_id=1, source_target_pairs={{0,20},{4,16},{8,28},{12,24},{16,4},{20,0},{24,12},{28,8},{1,21},{... | collective-permute-start | bytes 221192 | tf_op jit(solution)/shard_map/ppermute | solution.py:18
  7.5 2.7 %collective-permute-start.3 = (bf16[144,256]{1,0:T(8,128)(2,1)S(1)}, bf16[144,256]{1,0:T(8,128)(2,1)S(1)}, u32[]{:S(2)}, u32[]{:S(2)}) collective-permute-start(bf16[144,256]{1,0:T(8,128)(2,1)S(1)} %get-tuple-element.17), channel_id=1, source_target_pairs={{0,4},{4,0},{8,12},{12,8},{16,20},{20,16},{24,28},{28,24},{1,5},{5... | collective-permute-start | bytes 221192 | tf_op jit(solution)/shard_map/ppermute | solution.py:18
  8.0 2.2 %collective-permute-start.4 = (bf16[144,256]{1,0:T(8,128)(2,1)S(1)}, bf16[144,256]{1,0:T(8,128)(2,1)S(1)}, u32[]{:S(2)}, u32[]{:S(2)}) collective-permute-start(bf16[144,256]{1,0:T(8,128)(2,1)S(1)} %collective-permute-done.refs_1_), channel_id=1, source_target_pairs={{0,4},{4,0},{8,12},{12,8},{16,20},{20,16},{24,28},{28,24},{1,5},{5... | collective-permute-start | bytes 221192 | tf_op jit(solution)/shard_map/ppermute | solution.py:18
  9.7 1.3 %collective-permute-start.5 = (bf16[144,256]{1,0:T(8,128)(2,1)S(1)}, bf16[144,256]{1,0:T(8,128)(2,1)S(1)}, u32[]{:S(2)}, u32[]{:S(2)}) collective-permute-start(bf16[144,256]{1,0:T(8,128)(2,1)S(1)} %collective-permute-done.1.refs_2_), channel_id=1, source_target_pairs={{0,4},{4,0},{8,12},{12,8},{16,20},{20,16},{24,28},{28,24},{1,5},{5... | collective-permute-start | bytes 221192 | tf_op jit(solution)/shard_map/ppermute | solution.py:18
  9.8 2.2 %collective-permute-start.6 = (bf16[144,256]{1,0:T(8,128)(2,1)S(1)}, bf16[144,256]{1,0:T(8,128)(2,1)S(1)}, u32[]{:S(2)}, u32[]{:S(2)}) collective-permute-start(bf16[144,256]{1,0:T(8,128)(2,1)S(1)} %collective-permute-done.2.refs_3_), channel_id=1, source_target_pairs={{0,4},{4,0},{8,12},{12,8},{16,20},{20,16},{24,28},{28,24},{1,5},{5... | collective-permute-start | bytes 221192 | tf_op jit(solution)/shard_map/ppermute | solution.py:18
  14.6 5.8 %collective-permute-start.9 = (bf16[128,1024]{1,0:T(8,128)(2,1)S(1)}, bf16[128,1024]{1,0:T(8,128)(2,1)S(1)}, u32[]{:S(2)}, u32[]{:S(2)}) collective-permute-start(bf16[128,1024]{1,0:T(8,128)(2,1)S(1)} %branch.7), channel_id=1, source_target_pairs={{0,12},{4,16},{8,4},{12,24},{16,28},{20,0},{24,20},{28,8},{1,13},{... | collective-permute-start | bytes 786440 | tf_op jit(solution)/shard_map/ppermute | solution.py:345
  17.3 6.4 %collective-permute-start.8 = (bf16[128,1024]{1,0:T(8,128)(2,1)S(1)}, bf16[128,1024]{1,0:T(8,128)(2,1)S(1)}, u32[]{:S(2)}, u32[]{:S(2)}) collective-permute-start(bf16[128,1024]{1,0:T(8,128)(2,1)S(1)} %branch.5), channel_id=1, source_target_pairs={{0,8},{4,20},{8,0},{12,28},{16,24},{20,4},{24,16},{28,12},{1,9},{5... | collective-permute-start | bytes 786440 | tf_op jit(solution)/shard_map/ppermute | solution.py:346
  20.5 5.9 %copy-start = (bf16[128,1024]{1,0:T(8,128)(2,1)S(1)}, bf16[128,1024]{1,0:T(8,128)(2,1)}, u32[]{:S(2)}) copy-start(bf16[128,1024]{1,0:T(8,128)(2,1)} %tokens_hbm.1) | copy-start | bytes 786436
  20.5 5.8 %collective-permute-start.10 = (bf16[128,1024]{1,0:T(8,128)(2,1)S(1)}, bf16[128,1024]{1,0:T(8,128)(2,1)S(1)}, u32[]{:S(2)}, u32[]{:S(2)}) collective-permute-start(bf16[128,1024]{1,0:T(8,128)(2,1)S(1)} %add_convert_fusion.1), channel_id=1, source_target_pairs={{0,12},{4,16},{8,4},{12,24},{16,28},{20,0},{24,20},{28,8},{1,13},{... | collective-permute-start | bytes 786440 | tf_op jit(solution)/shard_map/ppermute | solution.py:348

commit v5 on v4

--- a/solution.py
+++ b/solution.py
@@ -113,60 +113,42 @@
     return [(2 * (chip ^ s) + q, 2 * (chip ^ s) + 1 - q) for s, q in zip(shifts, first, strict=True)]
 
 
-def rotate_taps(block_refs, places, rows, num, fine, out_ref, devices):
-    for block, place in zip(block_refs, places, strict=True):
-        taps = block[rows:, 0:rows].astype(jnp.float32)
-        at = pl.multiple_of((devices - 1 - place) * rows, rows)
-        for k in range(num):
-            line = jnp.broadcast_to(taps[k : k + 1, :], (8, rows))
-            line = pltpu.roll(line, rows - fine + 1, 1, stride=1, stride_axis=0)
-            lines = [line] + [pltpu.roll(line, step, 1) for step in range(8, fine, 8)]
-            out_ref[k * fine : (k + 1) * fine, pl.ds(at, rows)] = jnp.concatenate(
-                lines, axis=0
-            ).astype(jnp.bfloat16)
-
-
-def rotate_kernel(chips, shifts, rows, num, fine, *refs):
-    *blocks, out_ref = refs
-    places = [place for pair in zip(*block_places(chips, shifts), strict=True) for place in pair]
-    rotate_taps(blocks, places, rows, num, fine, out_ref, 2 * chips)
-
-
-def merge_kernel(chips, shifts, done, rows, num, fine, *refs):
+def ordered(value, core):
+    half = value.shape[1] // 2
+    turned = jnp.concatenate([value[:, half:], value[:, :half]], axis=1)
+    return jnp.where(core == 0, value, turned)
+
+
+def merge_kernel(chips, shifts, rows, num, fine, *refs):
     own = refs[:chips]
     pair = refs[chips : 2 * chips]
-    turned_ref, signal, strip, lines = refs[2 * chips :]
+    signal, strip, base = refs[2 * chips :]
     devices = 2 * chips
     length = devices * rows
     groups = rows // fine
     count = signal.shape[1] // groups
-    half = count // 2
+    wide = length + 2 * rows
     core = lax.axis_index("seq") % 2
     late = [rows - fine * (g + 1) for g in range(groups)]
     for g in range(groups - 1):
         signal[0 : late[g], g * count : (g + 1) * count] = jnp.zeros((late[g], count), signal.dtype)
+    base[:, length:] = jnp.zeros((EXTRA, 2 * rows), jnp.float32)
     places = block_places(chips, shifts)
     for own_block, pair_block, both in zip(own, pair, places, strict=True):
         for block, place in zip((own_block, pair_block), both, strict=True):
-            value = block[0:rows, :]
-            turned = jnp.concatenate([value[:, half:], value[:, :half]], axis=1)
-            value = jnp.where(core == 0, value, turned)
+            value = ordered(block[0:rows, :], core)
             for g in range(groups):
                 at = pl.multiple_of(place * rows + late[g], fine)
                 signal[pl.ds(at, rows), g * count : (g + 1) * count] = value
-    lines[...] = turned_ref[...]
-    for shift in range(done, chips):
-        rotate_taps((own[shift], pair[shift]), places[shift], rows, num, fine, lines, devices)
-    row = lax.broadcasted_iota(jnp.int32, (fine, rows), 0)
-    lane = lax.broadcasted_iota(jnp.int32, (fine, rows), 1)
-    here = lane - row < rows - fine + 1
-    nothing = jnp.zeros((fine, rows), jnp.bfloat16)
+            at = pl.multiple_of((devices - 1 - place) * rows, rows)
+            base[:, pl.ds(at, rows)] = block[rows:, 0:rows].astype(jnp.float32)
     for k in range(num):
-        cut = slice(k * fine, (k + 1) * fine)
-        parts = [lines[cut, b * rows : (b + 1) * rows] for b in range(devices)] + [nothing]
-        for b in range(devices):
-            strip[cut, b * rows : (b + 1) * rows] = jnp.where(here, parts[b], parts[b + 1])
-        strip[cut, length:] = nothing
+        line = jnp.broadcast_to(base[k : k + 1, :], (8, wide))
+        line = pltpu.roll(line, wide - fine + 1, 1, stride=1, stride_axis=0)
+        for step in range(0, fine, 16):
+            pieces = [pltpu.roll(line, step + h, 1)[:, : length + rows] for h in (0, 8)]
+            at = k * fine + step
+            strip[at : at + 16, :] = jnp.concatenate(pieces, axis=0).astype(jnp.bfloat16)
 
 
 def strip_kernel(chips, rows, num, *refs):
@@ -297,24 +279,14 @@
         jax.ShapeDtypeStruct((num * fine, length + rows), jnp.bfloat16),
     ]
     if relay:
-        done = chips - 1
-        lines = jax.ShapeDtypeStruct((num * fine, length), jnp.bfloat16)
-        ready = ends[:done] + ends[chips : chips + done]
-        turned = kernel_call(
-            functools.partial(rotate_kernel, chips, shifts[:done], rows, num, fine),
-            "rotate",
-            lines,
-            [VMEM] * len(ready),
-            8 * MIB,
-        )(*ready)
         signal, strip = kernel_call(
-            functools.partial(merge_kernel, chips, shifts, done, rows, num, fine),
+            functools.partial(merge_kernel, chips, shifts, rows, num, fine),
             "merge",
             shapes,
-            [VMEM] * (2 * chips + 1),
+            [VMEM] * (2 * chips),
             16 * MIB,
-            [pltpu.VMEM(lines.shape, lines.dtype)],
-        )(*ends, turned)
+            [pltpu.VMEM((EXTRA, length + 2 * rows), jnp.float32)],
+        )(*ends)
     else:
         taps = lax.all_gather(filters, "seq", axis=1, tiled=True)[:, ::-1]
         taps = jnp.pad(taps, ((0, EXTRA - num), (0, 2 * rows)))

time: 27.4 us -> 27.1 us (0.989)
  Pallas kernels: 11.2 us -> 10.7 us
    pallas_call x2 -> x1, Pallas kernels: 1.58 us -> 1.11 us  [local(): kernel_call(functools.partial(merge_kernel, chips, shifts, rows, num, fin...]
  transfers between devices with their start and end apart: 11 -> 11, of which waited for: 5 -> 6; matrix products, arithmetic and copies ran while one was open for 0% -> 0% of each run, Pallas kernels for 34% -> 32%
where the time goes in v5:
time: 27.1 us; the launch traced here: 26.9 us
  Pallas kernels  10.7 us (39%)
  starting transfers between devices  8.55 us (32%)
  waiting for transfers between devices  6.6 us (24%)
  other arithmetic  0.9 us (3%)
    pallas_call x4, Pallas kernels, branch(): kernel_call(functools.partial(branch_kernel, chips, rows, fine, kind), 'b...  6.5 us
    ppermute x8, starting transfers between devices, swap(): return lax.ppermute(value, 'seq', [(i, i ^ bits) for i in range(size)])  5.49 us
    ppermute x1, waiting for transfers between devices, local(): late = lax.ppermute(late, 'seq', across)  2.58 us
    ppermute x8, waiting for transfers between devices, swap(): return lax.ppermute(value, 'seq', [(i, i ^ bits) for i in range(size)])  2.48 us
    pallas_call x1, Pallas kernels, local(): kernel_call(stage_kernel, 'stage', [jax.ShapeDtypeStruct(mixing.shape, mi...  1.9 us
    pallas_call x1, Pallas kernels, local(): kernel_call(norm_kernel, 'norm', [jax.ShapeDtypeStruct((tall, count), jnp...  1.23 us
    ppermute x1, starting transfers between devices, local(): far = lax.ppermute(branch('far', jnp.bfloat16), 'seq', across)  1.17 us
    ppermute x1, starting transfers between devices, local(): late = lax.ppermute(late, 'seq', across)  1.17 us
  transfers between devices with their start and end apart: 11, of which 6 were waited for; matrix products, arithmetic and copies ran while one was open for 0% of the time, Pallas kernels for 32%

profile of v5, /device:TPU:0, one launch (start us, length us, event | category | flops | bytes accessed | tf_op | source)
XLA Modules:
  0.0 26.9 jit_solution(11675962556374943814)
XLA Ops:
  0.0 0.5 %collective-permute-start.7 = (bf16[12,128,1024]{2,1,0:T(8,128)(2,1)}, bf16[12,128,1024]{2,1,0:T(8,128)(2,1)S(1)}, u32[]{:S(2)}, u32[]{:S(2)}) collective-permute-start(bf16[12,128,1024]{2,1,0:T(8,128)(2,1)} %mix_hbm.1), channel_id=1, source_target_pairs={{0,4},{4,0},{8,12},{12,8},{16,20},{20,16},{24,28},{28,24},{1,5},{5... | collective-permute-start | bytes 9437192 | tf_op jit(solution)/shard_map/ppermute | solution.py:18
  0.5 1.2 %norm.1 = (bf16[144,256]{1,0:T(8,128)(2,1)S(1)}, bf16[144,256]{1,0:T(8,128)(2,1)S(1)}, bf16[144,256]{1,0:T(8,128)(2,1)S(1)}, bf16[144,256]{1,0:T(8,128)(2,1)S(1)}) custom-call(bf16[128,1024]{1,0:T(8,128)(2,1)} %tokens_hbm.1, f32[1,1024]{1,0:T(1,128)} %bitcast.1, f32[12,128]{1,0:T(8,128)} %filters_hbm.1), custom_call_target="tpu_custom_call" | custom-call | tf_op jit(solution)/shard_map/norm/pallas_call | solution.py:246
  1.7 3.6 %collective-permute-start = (bf16[144,256]{1,0:T(8,128)(2,1)S(1)}, bf16[144,256]{1,0:T(8,128)(2,1)S(1)}, u32[]{:S(2)}, u32[]{:S(2)}) collective-permute-start(bf16[144,256]{1,0:T(8,128)(2,1)S(1)} %get-tuple-element.14), channel_id=1, source_target_pairs={{0,28},{4,24},{8,20},{12,16},{16,12},{20,8},{24,4},{28,0},{1,29},{... | collective-permute-start | bytes 221192 | tf_op jit(solution)/shard_map/ppermute | solution.py:18
  5.3 0.1 collective-permute-start.1
  5.5 0.1 collective-permute-start.2
  5.6 1.9 %stage.1 = (bf16[12,128,1024]{2,1,0:T(8,128)(2,1)S(1)}, bf16[144,256]{1,0:T(8,128)(2,1)S(1)}) custom-call(bf16[12,128,1024]{2,1,0:T(8,128)(2,1)} %mix_hbm.1, bf16[144,256]{1,0:T(8,128)(2,1)S(1)} %get-tuple-element.13.block_ref.refs_0_), custom_call_target="tpu_custom_call" | custom-call | tf_op jit(solution)/shard_map/stage/pallas_call | solution.py:259
  7.5 0.6 %collective-permute-start.3 = (bf16[144,256]{1,0:T(8,128)(2,1)S(1)}, bf16[144,256]{1,0:T(8,128)(2,1)S(1)}, u32[]{:S(2)}, u32[]{:S(2)}) collective-permute-start(bf16[144,256]{1,0:T(8,128)(2,1)S(1)} %get-tuple-element.17), channel_id=1, source_target_pairs={{0,4},{4,0},{8,12},{12,8},{16,20},{20,16},{24,28},{28,24},{1,5},{5... | collective-permute-start | bytes 221192 | tf_op jit(solution)/shard_map/ppermute | solution.py:18
  8.0 0.0 collective-permute-done.refs_1_
  8.0 0.1 collective-permute-start.4
  8.1 1.6 %collective-permute-done.1.refs_2_ = bf16[144,256]{1,0:T(8,128)(2,1)S(1)} collective-permute-done((bf16[144,256]{1,0:T(8,128)(2,1)S(1)}, bf16[144,256]{1,0:T(8,128)(2,1)S(1)}, u32[]{:S(2)}, u32[]{:S(2)}) %collective-permute-start.1) | collective-permute-done | bytes 73760 | tf_op jit(solution)/shard_map/ppermute | solution.py:18
  9.7 0.1 collective-permute-start.5
  9.8 0.0 collective-permute-done.2.refs_3_
  9.8 0.4 %collective-permute-start.6 = (bf16[144,256]{1,0:T(8,128)(2,1)S(1)}, bf16[144,256]{1,0:T(8,128)(2,1)S(1)}, u32[]{:S(2)}, u32[]{:S(2)}) collective-permute-start(bf16[144,256]{1,0:T(8,128)(2,1)S(1)} %collective-permute-done.2.refs_3_), channel_id=1, source_target_pairs={{0,4},{4,0},{8,12},{12,8},{16,20},{20,16},{24,28},{28,24},{1,5},{5... | collective-permute-start | bytes 221192 | tf_op jit(solution)/shard_map/ppermute | solution.py:18
  10.2 0.0 collective-permute-done.3.refs_4_
  10.2 0.0 collective-permute-done.4.refs_5_
  10.2 0.7 %collective-permute-done.5.refs_6_ = bf16[144,256]{1,0:T(8,128)(2,1)S(1)} collective-permute-done((bf16[144,256]{1,0:T(8,128)(2,1)S(1)}, bf16[144,256]{1,0:T(8,128)(2,1)S(1)}, u32[]{:S(2)}, u32[]{:S(2)}) %collective-permute-start.5) | collective-permute-done | bytes 73760 | tf_op jit(solution)/shard_map/ppermute | solution.py:18
  11.0 0.2 collective-permute-done.6.refs_7_
  11.1 1.1 %merge.1 = (bf16[1152,1024]{1,0:T(8,128)(2,1)S(1)}, bf16[384,1152]{1,0:T(8,128)(2,1)S(1)}) custom-call(bf16[144,256]{1,0:T(8,128)(2,1)S(1)} %get-tuple-element.13.block_ref.refs_0_, bf16[144,256]{1,0:T(8,128)(2,1)S(1)} %collective-permute-done.refs_1_, bf16[144,256]{1,0:T(8,128)(2,1)S(1)} %collective-permute-done.1.refs_2_, ...), custom_call_target="tpu_custom_call" | custom-call | tf_op jit(solution)/shard_map/merge/pallas_call | solution.py:282
  12.2 0.0 collective-permute-done.7.refs_3_
  12.2 2.0 %branch.7 = bf16[128,1024]{1,0:T(8,128)(2,1)S(1)} custom-call(bf16[1152,1024]{1,0:T(8,128)(2,1)S(1)} %get-tuple-element.18.refs_0_, bf16[384,1152]{1,0:T(8,128)(2,1)S(1)} %get-tuple-element.19.refs_1_, bf16[12,128,1024]{2,1,0:T(8,128)(2,1)S(1)} %get-tuple-element.20.refs_2_, bf16[12,128,1024]{2,1,0:T(8,128)(2,1)S(1)} %collective-permute-done.7.refs_3_), custom_call_target="tpu_custom_call" | custom-call | tf_op jit(solution)/shard_map/branch/pallas_call | solution.py:305
  14.3 1.2 %collective-permute-start.9 = (bf16[128,1024]{1,0:T(8,128)(2,1)S(1)}, bf16[128,1024]{1,0:T(8,128)(2,1)S(1)}, u32[]{:S(2)}, u32[]{:S(2)}) collective-permute-start(bf16[128,1024]{1,0:T(8,128)(2,1)S(1)} %branch.7), channel_id=1, source_target_pairs={{0,12},{4,16},{8,4},{12,24},{16,28},{20,0},{24,20},{28,8},{1,13},{... | collective-permute-start | bytes 786440 | tf_op jit(solution)/shard_map/ppermute | solution.py:317
  15.4 1.6 %branch.5 = bf16[128,1024]{1,0:T(8,128)(2,1)S(1)} custom-call(bf16[1152,1024]{1,0:T(8,128)(2,1)S(1)} %get-tuple-element.18.refs_0_, bf16[384,1152]{1,0:T(8,128)(2,1)S(1)} %get-tuple-element.19.refs_1_, bf16[12,128,1024]{2,1,0:T(8,128)(2,1)S(1)} %get-tuple-element.20.refs_2_, bf16[12,128,1024]{2,1,0:T(8,128)(2,1)S(1)} %collective-permute-done.7.refs_3_), custom_call_target="tpu_custom_call" | custom-call | tf_op jit(solution)/shard_map/branch/pallas_call | solution.py:305
  17.0 0.7 %collective-permute-start.8 = (bf16[128,1024]{1,0:T(8,128)(2,1)S(1)}, bf16[128,1024]{1,0:T(8,128)(2,1)S(1)}, u32[]{:S(2)}, u32[]{:S(2)}) collective-permute-start(bf16[128,1024]{1,0:T(8,128)(2,1)S(1)} %branch.5), channel_id=1, source_target_pairs={{0,8},{4,20},{8,0},{12,28},{16,24},{20,4},{24,16},{28,12},{1,9},{5... | collective-permute-start | bytes 786440 | tf_op jit(solution)/shard_map/ppermute | solution.py:318
  17.7 1.6 %branch.6 = f32[128,1024]{1,0:T(8,128)S(1)} custom-call(bf16[1152,1024]{1,0:T(8,128)(2,1)S(1)} %get-tuple-element.18.refs_0_, bf16[384,1152]{1,0:T(8,128)(2,1)S(1)} %get-tuple-element.19.refs_1_, bf16[12,128,1024]{2,1,0:T(8,128)(2,1)S(1)} %get-tuple-element.20.refs_2_, bf16[12,128,1024]{2,1,0:T(8,128)(2,1)S(1)} %collective-permute-done.7.refs_3_), custom_call_target="tpu_custom_call" | custom-call | tf_op jit(solution)/shard_map/branch/pallas_call | solution.py:305
  19.3 0.8 %collective-permute-done.9 = bf16[128,1024]{1,0:T(8,128)(2,1)S(1)} collective-permute-done((bf16[128,1024]{1,0:T(8,128)(2,1)S(1)}, bf16[128,1024]{1,0:T(8,128)(2,1)S(1)}, u32[]{:S(2)}, u32[]{:S(2)}) %collective-permute-start.9) | collective-permute-done | bytes 262176 | tf_op jit(solution)/shard_map/ppermute | solution.py:317
  20.1 0.1 add_convert_fusion.1
  20.2 0.0 copy-start
  20.2 1.2 %collective-permute-start.10 = (bf16[128,1024]{1,0:T(8,128)(2,1)S(1)}, bf16[128,1024]{1,0:T(8,128)(2,1)S(1)}, u32[]{:S(2)}, u32[]{:S(2)}) collective-permute-start(bf16[128,1024]{1,0:T(8,128)(2,1)S(1)} %add_convert_fusion.1), channel_id=1, source_target_pairs={{0,12},{4,16},{8,4},{12,24},{16,28},{20,0},{24,20},{28,8},{1,13},{... | collective-permute-start | bytes 786440 | tf_op jit(solution)/shard_map/ppermute | solution.py:320
  21.3 1.4 %branch.4 = f32[128,1024]{1,0:T(8,128)S(1)} custom-call(bf16[1152,1024]{1,0:T(8,128)(2,1)S(1)} %get-tuple-element.18.refs_0_, bf16[384,1152]{1,0:T(8,128)(2,1)S(1)} %get-tuple-element.19.refs_1_, bf16[12,128,1024]{2,1,0:T(8,128)(2,1)S(1)} %get-tuple-element.20.refs_2_, bf16[12,128,1024]{2,1,0:T(8,128)(2,1)S(1)} %collective-permute-done.7.refs_3_), custom_call_target="tpu_custom_call" | custom-call | tf_op jit(solution)/shard_map/branch/pallas_call | solution.py:305
  22.7 0.7 %collective-permute-done.8 = bf16[128,1024]{1,0:T(8,128)(2,1)S(1)} collective-permute-done((bf16[128,1024]{1,0:T(8,128)(2,1)S(1)}, bf16[128,1024]{1,0:T(8,128)(2,1)S(1)}, u32[]{:S(2)}, u32[]{:S(2)}) %collective-permute-start.8) | collective-permute-done | bytes 262176 | tf_op jit(solution)/shard_map/ppermute | solution.py:318
  23.4 2.6 %collective-permute-done.10 = bf16[128,1024]{1,0:T(8,128)(2,1)S(1)} collective-permute-done((bf16[128,1024]{1,0:T(8,128)(2,1)S(1)}, bf16[128,1024]{1,0:T(8,128)(2,1)S(1)}, u32[]{:S(2)}, u32[]{:S(2)}) %collective-permute-start.10) | collective-permute-done | bytes 262176 | tf_op jit(solution)/shard_map/ppermute | solution.py:320
  26.0 0.0 copy-done
  26.0 0.8 %add_convert_fusion = bf16[128,1024]{1,0:T(8,128)(2,1)} fusion(bf16[128,1024]{1,0:T(8,128)(2,1)S(1)} %collective-permute-done.10, bf16[128,1024]{1,0:T(8,128)(2,1)S(1)} %collective-permute-done.8, f32[128,1024]{1,0:T(8,128)S(1)} %branch.4, bf16[128,1024]{1,0:T(8,128)(2,1)S(1)} %copy-done), kind=kLoop, calls=%fused_computation | loop fusion | flops 917504 | bytes 1572864 | tf_op jit(solution)/shard_map/convert_element_type | solution.py:339
Async XLA Ops:
  0.0 12.2 %collective-permute-start.7 = (bf16[12,128,1024]{2,1,0:T(8,128)(2,1)}, bf16[12,128,1024]{2,1,0:T(8,128)(2,1)S(1)}, u32[]{:S(2)}, u32[]{:S(2)}) collective-permute-start(bf16[12,128,1024]{2,1,0:T(8,128)(2,1)} %mix_hbm.1), channel_id=1, source_target_pairs={{0,4},{4,0},{8,12},{12,8},{16,20},{20,16},{24,28},{28,24},{1,5},{5... | collective-permute-start | bytes 9437192 | tf_op jit(solution)/shard_map/ppermute | solution.py:18
  1.7 6.4 %collective-permute-start = (bf16[144,256]{1,0:T(8,128)(2,1)S(1)}, bf16[144,256]{1,0:T(8,128)(2,1)S(1)}, u32[]{:S(2)}, u32[]{:S(2)}) collective-permute-start(bf16[144,256]{1,0:T(8,128)(2,1)S(1)} %get-tuple-element.14), channel_id=1, source_target_pairs={{0,28},{4,24},{8,20},{12,16},{16,12},{20,8},{24,4},{28,0},{1,29},{... | collective-permute-start | bytes 221192 | tf_op jit(solution)/shard_map/ppermute | solution.py:18
  5.3 4.4 %collective-permute-start.1 = (bf16[144,256]{1,0:T(8,128)(2,1)S(1)}, bf16[144,256]{1,0:T(8,128)(2,1)S(1)}, u32[]{:S(2)}, u32[]{:S(2)}) collective-permute-start(bf16[144,256]{1,0:T(8,128)(2,1)S(1)} %get-tuple-element.15), channel_id=1, source_target_pairs={{0,12},{4,8},{8,4},{12,0},{16,28},{20,24},{24,20},{28,16},{1,13},{... | collective-permute-start | bytes 221192 | tf_op jit(solution)/shard_map/ppermute | solution.py:18
  5.5 4.4 %collective-permute-start.2 = (bf16[144,256]{1,0:T(8,128)(2,1)S(1)}, bf16[144,256]{1,0:T(8,128)(2,1)S(1)}, u32[]{:S(2)}, u32[]{:S(2)}) collective-permute-start(bf16[144,256]{1,0:T(8,128)(2,1)S(1)} %get-tuple-element.16), channel_id=1, source_target_pairs={{0,20},{4,16},{8,28},{12,24},{16,4},{20,0},{24,12},{28,8},{1,21},{... | collective-permute-start | bytes 221192 | tf_op jit(solution)/shard_map/ppermute | solution.py:18
  7.5 2.7 %collective-permute-start.3 = (bf16[144,256]{1,0:T(8,128)(2,1)S(1)}, bf16[144,256]{1,0:T(8,128)(2,1)S(1)}, u32[]{:S(2)}, u32[]{:S(2)}) collective-permute-start(bf16[144,256]{1,0:T(8,128)(2,1)S(1)} %get-tuple-element.17), channel_id=1, source_target_pairs={{0,4},{4,0},{8,12},{12,8},{16,20},{20,16},{24,28},{28,24},{1,5},{5... | collective-permute-start | bytes 221192 | tf_op jit(solution)/shard_map/ppermute | solution.py:18
  8.0 2.2 %collective-permute-start.4 = (bf16[144,256]{1,0:T(8,128)(2,1)S(1)}, bf16[144,256]{1,0:T(8,128)(2,1)S(1)}, u32[]{:S(2)}, u32[]{:S(2)}) collective-permute-start(bf16[144,256]{1,0:T(8,128)(2,1)S(1)} %collective-permute-done.refs_1_), channel_id=1, source_target_pairs={{0,4},{4,0},{8,12},{12,8},{16,20},{20,16},{24,28},{28,24},{1,5},{5... | collective-permute-start | bytes 221192 | tf_op jit(solution)/shard_map/ppermute | solution.py:18
  9.7 1.3 %collective-permute-start.5 = (bf16[144,256]{1,0:T(8,128)(2,1)S(1)}, bf16[144,256]{1,0:T(8,128)(2,1)S(1)}, u32[]{:S(2)}, u32[]{:S(2)}) collective-permute-start(bf16[144,256]{1,0:T(8,128)(2,1)S(1)} %collective-permute-done.1.refs_2_), channel_id=1, source_target_pairs={{0,4},{4,0},{8,12},{12,8},{16,20},{20,16},{24,28},{28,24},{1,5},{5... | collective-permute-start | bytes 221192 | tf_op jit(solution)/shard_map/ppermute | solution.py:18
  9.8 1.3 %collective-permute-start.6 = (bf16[144,256]{1,0:T(8,128)(2,1)S(1)}, bf16[144,256]{1,0:T(8,128)(2,1)S(1)}, u32[]{:S(2)}, u32[]{:S(2)}) collective-permute-start(bf16[144,256]{1,0:T(8,128)(2,1)S(1)} %collective-permute-done.2.refs_3_), channel_id=1, source_target_pairs={{0,4},{4,0},{8,12},{12,8},{16,20},{20,16},{24,28},{28,24},{1,5},{5... | collective-permute-start | bytes 221192 | tf_op jit(solution)/shard_map/ppermute | solution.py:18
  14.3 5.8 %collective-permute-start.9 = (bf16[128,1024]{1,0:T(8,128)(2,1)S(1)}, bf16[128,1024]{1,0:T(8,128)(2,1)S(1)}, u32[]{:S(2)}, u32[]{:S(2)}) collective-permute-start(bf16[128,1024]{1,0:T(8,128)(2,1)S(1)} %branch.7), channel_id=1, source_target_pairs={{0,12},{4,16},{8,4},{12,24},{16,28},{20,0},{24,20},{28,8},{1,13},{... | collective-permute-start | bytes 786440 | tf_op jit(solution)/shard_map/ppermute | solution.py:317
  17.0 6.4 %collective-permute-start.8 = (bf16[128,1024]{1,0:T(8,128)(2,1)S(1)}, bf16[128,1024]{1,0:T(8,128)(2,1)S(1)}, u32[]{:S(2)}, u32[]{:S(2)}) collective-permute-start(bf16[128,1024]{1,0:T(8,128)(2,1)S(1)} %branch.5), channel_id=1, source_target_pairs={{0,8},{4,20},{8,0},{12,28},{16,24},{20,4},{24,16},{28,12},{1,9},{5... | collective-permute-start | bytes 786440 | tf_op jit(solution)/shard_map/ppermute | solution.py:318
  20.2 5.9 %copy-start = (bf16[128,1024]{1,0:T(8,128)(2,1)S(1)}, bf16[128,1024]{1,0:T(8,128)(2,1)}, u32[]{:S(2)}) copy-start(bf16[128,1024]{1,0:T(8,128)(2,1)} %tokens_hbm.1) | copy-start | bytes 786436
  20.2 5.8 %collective-permute-start.10 = (bf16[128,1024]{1,0:T(8,128)(2,1)S(1)}, bf16[128,1024]{1,0:T(8,128)(2,1)S(1)}, u32[]{:S(2)}, u32[]{:S(2)}) collective-permute-start(bf16[128,1024]{1,0:T(8,128)(2,1)S(1)} %add_convert_fusion.1), channel_id=1, source_target_pairs={{0,12},{4,16},{8,4},{12,24},{16,28},{20,0},{24,20},{28,8},{1,13},{... | collective-permute-start | bytes 786440 | tf_op jit(solution)/shard_map/ppermute | solution.py:320

commit v6 on v5

--- a/solution.py
+++ b/solution.py
@@ -45,7 +45,7 @@
     chips = len(out_refs)
     count = width // chips
     num, span = filters_ref.shape
-    packed = out_refs[0].shape[0] > rows
+    packed = out_refs[0].shape[0] < rows
     copies[0].wait()
     if packed:
         flip = (
@@ -57,8 +57,8 @@
             filters_ref[...].astype(jnp.bfloat16), flip, preferred_element_type=jnp.float32
         )
         taps = jnp.concatenate([taps, jnp.zeros((EXTRA - num, span), jnp.float32)], axis=0)
-        taps = jnp.concatenate([taps, jnp.zeros((EXTRA, count - span), jnp.float32)], axis=1)
-        taps = taps.astype(jnp.bfloat16)
+        for out_ref in out_refs:
+            out_ref[:, rows // EXTRA * count :] = taps.astype(jnp.bfloat16)
     copies[1].wait()
     copies[2].wait()
     values = tokens_ref[...].astype(jnp.float32)
@@ -69,11 +69,12 @@
 
             @pl.when(chip == part ^ shift)
             def _(part=part, out_ref=out_ref):
-                out_ref[0:rows, :] = normed[:, part * count : (part + 1) * count]
-
-    if packed:
-        for out_ref in out_refs:
-            out_ref[rows:, :] = taps
+                value = normed[:, part * count : (part + 1) * count]
+                if not packed:
+                    out_ref[...] = value
+                    return
+                for g in range(rows // EXTRA):
+                    out_ref[:, g * count : (g + 1) * count] = value[g * EXTRA : (g + 1) * EXTRA]
 
 
 def stage_kernel(mix_hbm, block_ref, mix_ref, out_ref, sem):
@@ -127,28 +128,34 @@
     length = devices * rows
     groups = rows // fine
     count = signal.shape[1] // groups
-    wide = length + 2 * rows
     core = lax.axis_index("seq") % 2
     late = [rows - fine * (g + 1) for g in range(groups)]
     for g in range(groups - 1):
         signal[0 : late[g], g * count : (g + 1) * count] = jnp.zeros((late[g], count), signal.dtype)
-    base[:, length:] = jnp.zeros((EXTRA, 2 * rows), jnp.float32)
     places = block_places(chips, shifts)
     for own_block, pair_block, both in zip(own, pair, places, strict=True):
         for block, place in zip((own_block, pair_block), both, strict=True):
-            value = ordered(block[0:rows, :], core)
-            for g in range(groups):
-                at = pl.multiple_of(place * rows + late[g], fine)
-                signal[pl.ds(at, rows), g * count : (g + 1) * count] = value
+            for part in range(rows // EXTRA):
+                value = ordered(block[:, part * count : (part + 1) * count], core)
+                for g in range(groups):
+                    at = pl.multiple_of(place * rows + late[g] + part * EXTRA, EXTRA)
+                    signal[pl.ds(at, EXTRA), g * count : (g + 1) * count] = value
             at = pl.multiple_of((devices - 1 - place) * rows, rows)
-            base[:, pl.ds(at, rows)] = block[rows:, 0:rows].astype(jnp.float32)
+            base[:, pl.ds(at, rows)] = block[:, rows // EXTRA * count :].astype(jnp.float32)
+    row = lax.broadcasted_iota(jnp.int32, (fine, rows), 0)
+    lane = lax.broadcasted_iota(jnp.int32, (fine, rows), 1)
+    kept = lane - row <= rows - fine
+    strip[:, length:] = jnp.zeros((num * fine, rows), jnp.bfloat16)
     for k in range(num):
-        line = jnp.broadcast_to(base[k : k + 1, :], (8, wide))
-        line = pltpu.roll(line, wide - fine + 1, 1, stride=1, stride_axis=0)
-        for step in range(0, fine, 16):
-            pieces = [pltpu.roll(line, step + h, 1)[:, : length + rows] for h in (0, 8)]
-            at = k * fine + step
-            strip[at : at + 16, :] = jnp.concatenate(pieces, axis=0).astype(jnp.bfloat16)
+        line = jnp.broadcast_to(base[k : k + 1, :], (8, length))
+        line = pltpu.roll(line, length - fine + 1, 1, stride=1, stride_axis=0)
+        lines = [line] + [pltpu.roll(line, step, 1) for step in range(8, fine, 8)]
+        whole = jnp.concatenate(lines, axis=0)
+        cut = slice(k * fine, (k + 1) * fine)
+        strip[cut, : length - rows] = whole[:, : length - rows].astype(jnp.bfloat16)
+        strip[cut, length - rows : length] = jnp.where(kept, whole[:, length - rows :], 0.0).astype(
+            jnp.bfloat16
+        )
 
 
 def strip_kernel(chips, rows, num, *refs):
@@ -239,14 +246,14 @@
     num, span = filters.shape
     length = devices * rows
     count = width // chips
-    relay = chips == 4 and count % 256 == 0 and span == rows and num <= EXTRA
+    relay = chips == 4 and count % 256 == 0 and span == rows and rows % EXTRA == 0 and num <= EXTRA
     pair_mixing = swap(mixing, 1, devices)
     fine = 32 if relay else rows
-    tall = rows + (EXTRA if relay else 0)
+    flat = (EXTRA, rows // EXTRA * count + span) if relay else (rows, count)
     blocks = kernel_call(
         norm_kernel,
         "norm",
-        [jax.ShapeDtypeStruct((tall, count), jnp.bfloat16)] * chips,
+        [jax.ShapeDtypeStruct(flat, jnp.bfloat16)] * chips,
         [HBM] * 3,
         8 * MIB,
         [
@@ -285,7 +292,7 @@
             shapes,
             [VMEM] * (2 * chips),
             16 * MIB,
-            [pltpu.VMEM((EXTRA, length + 2 * rows), jnp.float32)],
+            [pltpu.VMEM((EXTRA, length), jnp.float32)],
         )(*ends)
     else:
         taps = lax.all_gather(filters, "seq", axis=1, tiled=True)[:, ::-1]

time: 27.1 us -> 26.6 us (0.982)
  Pallas kernels: 10.7 us -> 10.4 us
    pallas_call x1, Pallas kernels: 1.11 us -> 0.76 us  [local(): kernel_call(functools.partial(merge_kernel, chips, shifts, rows, num, fin...]
where the time goes in v6:
time: 26.6 us; the launch traced here: 26.4 us
  Pallas kernels  10.4 us (39%)
  starting transfers between devices  8.5 us (32%)
  waiting for transfers between devices  6.56 us (25%)
  other arithmetic  0.9 us (3%)
    pallas_call x4, Pallas kernels, branch(): kernel_call(functools.partial(branch_kernel, chips, rows, fine, kind), 'b...  6.5 us
    ppermute x8, starting transfers between devices, swap(): return lax.ppermute(value, 'seq', [(i, i ^ bits) for i in range(size)])  5.49 us
    ppermute x1, waiting for transfers between devices, local(): late = lax.ppermute(late, 'seq', across)  2.59 us
    ppermute x8, waiting for transfers between devices, swap(): return lax.ppermute(value, 'seq', [(i, i ^ bits) for i in range(size)])  2.39 us
    pallas_call x1, Pallas kernels, local(): kernel_call(stage_kernel, 'stage', [jax.ShapeDtypeStruct(mixing.shape, mi...  1.9 us
    pallas_call x1, Pallas kernels, local(): kernel_call(norm_kernel, 'norm', [jax.ShapeDtypeStruct(flat, jnp.bfloat16...  1.22 us
    ppermute x1, starting transfers between devices, local(): far = lax.ppermute(branch('far', jnp.bfloat16), 'seq', across)  1.11 us
    ppermute x1, starting transfers between devices, local(): late = lax.ppermute(late, 'seq', across)  1.11 us
  transfers between devices with their start and end apart: 11, of which 6 were waited for; matrix products, arithmetic and copies ran while one was open for 0% of the time, Pallas kernels for 32%

profile of v6, /device:TPU:0, one launch (start us, length us, event | category | flops | bytes accessed | tf_op | source)
XLA Modules:
  0.0 26.4 jit_solution(2627037415504655498)
XLA Ops:
  0.0 0.5 %collective-permute-start.7 = (bf16[12,128,1024]{2,1,0:T(8,128)(2,1)}, bf16[12,128,1024]{2,1,0:T(8,128)(2,1)S(1)}, u32[]{:S(2)}, u32[]{:S(2)}) collective-permute-start(bf16[12,128,1024]{2,1,0:T(8,128)(2,1)} %mix_hbm.1), channel_id=1, source_target_pairs={{0,4},{4,0},{8,12},{12,8},{16,20},{20,16},{24,28},{28,24},{1,5},{5... | collective-permute-start | bytes 9437192 | tf_op jit(solution)/shard_map/ppermute | solution.py:18
  0.5 1.2 %norm.1 = (bf16[16,2176]{1,0:T(8,128)(2,1)S(1)}, bf16[16,2176]{1,0:T(8,128)(2,1)S(1)}, bf16[16,2176]{1,0:T(8,128)(2,1)S(1)}, bf16[16,2176]{1,0:T(8,128)(2,1)S(1)}) custom-call(bf16[128,1024]{1,0:T(8,128)(2,1)} %tokens_hbm.1, f32[1,1024]{1,0:T(1,128)} %bitcast.1, f32[12,128]{1,0:T(8,128)} %filters_hbm.1), custom_call_target="tpu_custom_call" | custom-call | tf_op jit(solution)/shard_map/norm/pallas_call | solution.py:253
  1.7 3.6 %collective-permute-start = (bf16[16,2176]{1,0:T(8,128)(2,1)S(1)}, bf16[16,2176]{1,0:T(8,128)(2,1)S(1)}, u32[]{:S(2)}, u32[]{:S(2)}) collective-permute-start(bf16[16,2176]{1,0:T(8,128)(2,1)S(1)} %get-tuple-element.14), channel_id=1, source_target_pairs={{0,28},{4,24},{8,20},{12,16},{16,12},{20,8},{24,4},{28,0},{1,29},{... | collective-permute-start | bytes 208904 | tf_op jit(solution)/shard_map/ppermute | solution.py:18
  5.3 0.1 collective-permute-start.1
  5.5 0.1 collective-permute-start.2
  5.6 1.9 %stage.1 = (bf16[12,128,1024]{2,1,0:T(8,128)(2,1)S(1)}, bf16[16,2176]{1,0:T(8,128)(2,1)S(1)}) custom-call(bf16[12,128,1024]{2,1,0:T(8,128)(2,1)} %mix_hbm.1, bf16[16,2176]{1,0:T(8,128)(2,1)S(1)} %get-tuple-element.13.block_ref.refs_0_), custom_call_target="tpu_custom_call" | custom-call | tf_op jit(solution)/shard_map/stage/pallas_call | solution.py:266
  7.5 0.6 %collective-permute-start.3 = (bf16[16,2176]{1,0:T(8,128)(2,1)S(1)}, bf16[16,2176]{1,0:T(8,128)(2,1)S(1)}, u32[]{:S(2)}, u32[]{:S(2)}) collective-permute-start(bf16[16,2176]{1,0:T(8,128)(2,1)S(1)} %get-tuple-element.17), channel_id=1, source_target_pairs={{0,4},{4,0},{8,12},{12,8},{16,20},{20,16},{24,28},{28,24},{1,5},{5... | collective-permute-start | bytes 208904 | tf_op jit(solution)/shard_map/ppermute | solution.py:18
  8.0 0.0 collective-permute-done.refs_1_
  8.0 0.1 collective-permute-start.4
  8.1 1.5 %collective-permute-done.1.refs_2_ = bf16[16,2176]{1,0:T(8,128)(2,1)S(1)} collective-permute-done((bf16[16,2176]{1,0:T(8,128)(2,1)S(1)}, bf16[16,2176]{1,0:T(8,128)(2,1)S(1)}, u32[]{:S(2)}, u32[]{:S(2)}) %collective-permute-start.1) | collective-permute-done | bytes 69664 | tf_op jit(solution)/shard_map/ppermute | solution.py:18
  9.6 0.1 collective-permute-start.5
  9.7 0.0 collective-permute-done.2.refs_3_
  9.7 0.4 %collective-permute-start.6 = (bf16[16,2176]{1,0:T(8,128)(2,1)S(1)}, bf16[16,2176]{1,0:T(8,128)(2,1)S(1)}, u32[]{:S(2)}, u32[]{:S(2)}) collective-permute-start(bf16[16,2176]{1,0:T(8,128)(2,1)S(1)} %collective-permute-done.2.refs_3_), channel_id=1, source_target_pairs={{0,4},{4,0},{8,12},{12,8},{16,20},{20,16},{24,28},{28,24},{1,5},{5... | collective-permute-start | bytes 208904 | tf_op jit(solution)/shard_map/ppermute | solution.py:18
  10.1 0.0 collective-permute-done.3.refs_4_
  10.1 0.0 collective-permute-done.4.refs_5_
  10.1 0.7 %collective-permute-done.5.refs_6_ = bf16[16,2176]{1,0:T(8,128)(2,1)S(1)} collective-permute-done((bf16[16,2176]{1,0:T(8,128)(2,1)S(1)}, bf16[16,2176]{1,0:T(8,128)(2,1)S(1)}, u32[]{:S(2)}, u32[]{:S(2)}) %collective-permute-start.5) | collective-permute-done | bytes 69664 | tf_op jit(solution)/shard_map/ppermute | solution.py:18
  10.9 0.2 collective-permute-done.6.refs_7_
  11.0 0.8 %merge.1 = (bf16[1152,1024]{1,0:T(8,128)(2,1)S(1)}, bf16[384,1152]{1,0:T(8,128)(2,1)S(1)}) custom-call(bf16[16,2176]{1,0:T(8,128)(2,1)S(1)} %get-tuple-element.13.block_ref.refs_0_, bf16[16,2176]{1,0:T(8,128)(2,1)S(1)} %collective-permute-done.refs_1_, bf16[16,2176]{1,0:T(8,128)(2,1)S(1)} %collective-permute-done.1.refs_2_, ...), custom_call_target="tpu_custom_call" | custom-call | tf_op jit(solution)/shard_map/merge/pallas_call | solution.py:289
  11.8 0.0 collective-permute-done.7.refs_3_
  11.8 2.0 %branch.7 = bf16[128,1024]{1,0:T(8,128)(2,1)S(1)} custom-call(bf16[1152,1024]{1,0:T(8,128)(2,1)S(1)} %get-tuple-element.18.refs_0_, bf16[384,1152]{1,0:T(8,128)(2,1)S(1)} %get-tuple-element.19.refs_1_, bf16[12,128,1024]{2,1,0:T(8,128)(2,1)S(1)} %get-tuple-element.20.refs_2_, bf16[12,128,1024]{2,1,0:T(8,128)(2,1)S(1)} %collective-permute-done.7.refs_3_), custom_call_target="tpu_custom_call" | custom-call | tf_op jit(solution)/shard_map/branch/pallas_call | solution.py:312
  13.8 1.1 %collective-permute-start.9 = (bf16[128,1024]{1,0:T(8,128)(2,1)S(1)}, bf16[128,1024]{1,0:T(8,128)(2,1)S(1)}, u32[]{:S(2)}, u32[]{:S(2)}) collective-permute-start(bf16[128,1024]{1,0:T(8,128)(2,1)S(1)} %branch.7), channel_id=1, source_target_pairs={{0,12},{4,16},{8,4},{12,24},{16,28},{20,0},{24,20},{28,8},{1,13},{... | collective-permute-start | bytes 786440 | tf_op jit(solution)/shard_map/ppermute | solution.py:324
  14.9 1.6 %branch.5 = bf16[128,1024]{1,0:T(8,128)(2,1)S(1)} custom-call(bf16[1152,1024]{1,0:T(8,128)(2,1)S(1)} %get-tuple-element.18.refs_0_, bf16[384,1152]{1,0:T(8,128)(2,1)S(1)} %get-tuple-element.19.refs_1_, bf16[12,128,1024]{2,1,0:T(8,128)(2,1)S(1)} %get-tuple-element.20.refs_2_, bf16[12,128,1024]{2,1,0:T(8,128)(2,1)S(1)} %collective-permute-done.7.refs_3_), custom_call_target="tpu_custom_call" | custom-call | tf_op jit(solution)/shard_map/branch/pallas_call | solution.py:312
  16.5 0.8 %collective-permute-start.8 = (bf16[128,1024]{1,0:T(8,128)(2,1)S(1)}, bf16[128,1024]{1,0:T(8,128)(2,1)S(1)}, u32[]{:S(2)}, u32[]{:S(2)}) collective-permute-start(bf16[128,1024]{1,0:T(8,128)(2,1)S(1)} %branch.5), channel_id=1, source_target_pairs={{0,8},{4,20},{8,0},{12,28},{16,24},{20,4},{24,16},{28,12},{1,9},{5... | collective-permute-start | bytes 786440 | tf_op jit(solution)/shard_map/ppermute | solution.py:325
  17.3 1.6 %branch.6 = f32[128,1024]{1,0:T(8,128)S(1)} custom-call(bf16[1152,1024]{1,0:T(8,128)(2,1)S(1)} %get-tuple-element.18.refs_0_, bf16[384,1152]{1,0:T(8,128)(2,1)S(1)} %get-tuple-element.19.refs_1_, bf16[12,128,1024]{2,1,0:T(8,128)(2,1)S(1)} %get-tuple-element.20.refs_2_, bf16[12,128,1024]{2,1,0:T(8,128)(2,1)S(1)} %collective-permute-done.7.refs_3_), custom_call_target="tpu_custom_call" | custom-call | tf_op jit(solution)/shard_map/branch/pallas_call | solution.py:312
  18.9 0.8 %collective-permute-done.9 = bf16[128,1024]{1,0:T(8,128)(2,1)S(1)} collective-permute-done((bf16[128,1024]{1,0:T(8,128)(2,1)S(1)}, bf16[128,1024]{1,0:T(8,128)(2,1)S(1)}, u32[]{:S(2)}, u32[]{:S(2)}) %collective-permute-start.9) | collective-permute-done | bytes 262176 | tf_op jit(solution)/shard_map/ppermute | solution.py:324
  19.7 0.1 add_convert_fusion.1
  19.7 0.0 copy-start
  19.7 1.1 %collective-permute-start.10 = (bf16[128,1024]{1,0:T(8,128)(2,1)S(1)}, bf16[128,1024]{1,0:T(8,128)(2,1)S(1)}, u32[]{:S(2)}, u32[]{:S(2)}) collective-permute-start(bf16[128,1024]{1,0:T(8,128)(2,1)S(1)} %add_convert_fusion.1), channel_id=1, source_target_pairs={{0,12},{4,16},{8,4},{12,24},{16,28},{20,0},{24,20},{28,8},{1,13},{... | collective-permute-start | bytes 786440 | tf_op jit(solution)/shard_map/ppermute | solution.py:327
  20.8 1.4 %branch.4 = f32[128,1024]{1,0:T(8,128)S(1)} custom-call(bf16[1152,1024]{1,0:T(8,128)(2,1)S(1)} %get-tuple-element.18.refs_0_, bf16[384,1152]{1,0:T(8,128)(2,1)S(1)} %get-tuple-element.19.refs_1_, bf16[12,128,1024]{2,1,0:T(8,128)(2,1)S(1)} %get-tuple-element.20.refs_2_, bf16[12,128,1024]{2,1,0:T(8,128)(2,1)S(1)} %collective-permute-done.7.refs_3_), custom_call_target="tpu_custom_call" | custom-call | tf_op jit(solution)/shard_map/branch/pallas_call | solution.py:312
  22.2 0.8 %collective-permute-done.8 = bf16[128,1024]{1,0:T(8,128)(2,1)S(1)} collective-permute-done((bf16[128,1024]{1,0:T(8,128)(2,1)S(1)}, bf16[128,1024]{1,0:T(8,128)(2,1)S(1)}, u32[]{:S(2)}, u32[]{:S(2)}) %collective-permute-start.8) | collective-permute-done | bytes 262176 | tf_op jit(solution)/shard_map/ppermute | solution.py:325
  23.0 2.6 %collective-permute-done.10 = bf16[128,1024]{1,0:T(8,128)(2,1)S(1)} collective-permute-done((bf16[128,1024]{1,0:T(8,128)(2,1)S(1)}, bf16[128,1024]{1,0:T(8,128)(2,1)S(1)}, u32[]{:S(2)}, u32[]{:S(2)}) %collective-permute-start.10) | collective-permute-done | bytes 262176 | tf_op jit(solution)/shard_map/ppermute | solution.py:327
  25.6 0.0 copy-done
  25.6 0.8 %add_convert_fusion = bf16[128,1024]{1,0:T(8,128)(2,1)} fusion(bf16[128,1024]{1,0:T(8,128)(2,1)S(1)} %collective-permute-done.10, bf16[128,1024]{1,0:T(8,128)(2,1)S(1)} %collective-permute-done.8, f32[128,1024]{1,0:T(8,128)S(1)} %branch.4, bf16[128,1024]{1,0:T(8,128)(2,1)S(1)} %copy-done), kind=kLoop, calls=%fused_computation | loop fusion | flops 917504 | bytes 1572864 | tf_op jit(solution)/shard_map/convert_element_type | solution.py:346
Async XLA Ops:
  0.0 11.8 %collective-permute-start.7 = (bf16[12,128,1024]{2,1,0:T(8,128)(2,1)}, bf16[12,128,1024]{2,1,0:T(8,128)(2,1)S(1)}, u32[]{:S(2)}, u32[]{:S(2)}) collective-permute-start(bf16[12,128,1024]{2,1,0:T(8,128)(2,1)} %mix_hbm.1), channel_id=1, source_target_pairs={{0,4},{4,0},{8,12},{12,8},{16,20},{20,16},{24,28},{28,24},{1,5},{5... | collective-permute-start | bytes 9437192 | tf_op jit(solution)/shard_map/ppermute | solution.py:18
  1.7 6.4 %collective-permute-start = (bf16[16,2176]{1,0:T(8,128)(2,1)S(1)}, bf16[16,2176]{1,0:T(8,128)(2,1)S(1)}, u32[]{:S(2)}, u32[]{:S(2)}) collective-permute-start(bf16[16,2176]{1,0:T(8,128)(2,1)S(1)} %get-tuple-element.14), channel_id=1, source_target_pairs={{0,28},{4,24},{8,20},{12,16},{16,12},{20,8},{24,4},{28,0},{1,29},{... | collective-permute-start | bytes 208904 | tf_op jit(solution)/shard_map/ppermute | solution.py:18
  5.3 4.3 %collective-permute-start.1 = (bf16[16,2176]{1,0:T(8,128)(2,1)S(1)}, bf16[16,2176]{1,0:T(8,128)(2,1)S(1)}, u32[]{:S(2)}, u32[]{:S(2)}) collective-permute-start(bf16[16,2176]{1,0:T(8,128)(2,1)S(1)} %get-tuple-element.15), channel_id=1, source_target_pairs={{0,12},{4,8},{8,4},{12,0},{16,28},{20,24},{24,20},{28,16},{1,13},{... | collective-permute-start | bytes 208904 | tf_op jit(solution)/shard_map/ppermute | solution.py:18
  5.5 4.3 %collective-permute-start.2 = (bf16[16,2176]{1,0:T(8,128)(2,1)S(1)}, bf16[16,2176]{1,0:T(8,128)(2,1)S(1)}, u32[]{:S(2)}, u32[]{:S(2)}) collective-permute-start(bf16[16,2176]{1,0:T(8,128)(2,1)S(1)} %get-tuple-element.16), channel_id=1, source_target_pairs={{0,20},{4,16},{8,28},{12,24},{16,4},{20,0},{24,12},{28,8},{1,21},{... | collective-permute-start | bytes 208904 | tf_op jit(solution)/shard_map/ppermute | solution.py:18
  7.5 2.7 %collective-permute-start.3 = (bf16[16,2176]{1,0:T(8,128)(2,1)S(1)}, bf16[16,2176]{1,0:T(8,128)(2,1)S(1)}, u32[]{:S(2)}, u32[]{:S(2)}) collective-permute-start(bf16[16,2176]{1,0:T(8,128)(2,1)S(1)} %get-tuple-element.17), channel_id=1, source_target_pairs={{0,4},{4,0},{8,12},{12,8},{16,20},{20,16},{24,28},{28,24},{1,5},{5... | collective-permute-start | bytes 208904 | tf_op jit(solution)/shard_map/ppermute | solution.py:18
  8.0 2.1 %collective-permute-start.4 = (bf16[16,2176]{1,0:T(8,128)(2,1)S(1)}, bf16[16,2176]{1,0:T(8,128)(2,1)S(1)}, u32[]{:S(2)}, u32[]{:S(2)}) collective-permute-start(bf16[16,2176]{1,0:T(8,128)(2,1)S(1)} %collective-permute-done.refs_1_), channel_id=1, source_target_pairs={{0,4},{4,0},{8,12},{12,8},{16,20},{20,16},{24,28},{28,24},{1,5},{5... | collective-permute-start | bytes 208904 | tf_op jit(solution)/shard_map/ppermute | solution.py:18
  9.6 1.3 %collective-permute-start.5 = (bf16[16,2176]{1,0:T(8,128)(2,1)S(1)}, bf16[16,2176]{1,0:T(8,128)(2,1)S(1)}, u32[]{:S(2)}, u32[]{:S(2)}) collective-permute-start(bf16[16,2176]{1,0:T(8,128)(2,1)S(1)} %collective-permute-done.1.refs_2_), channel_id=1, source_target_pairs={{0,4},{4,0},{8,12},{12,8},{16,20},{20,16},{24,28},{28,24},{1,5},{5... | collective-permute-start | bytes 208904 | tf_op jit(solution)/shard_map/ppermute | solution.py:18
  9.7 1.3 %collective-permute-start.6 = (bf16[16,2176]{1,0:T(8,128)(2,1)S(1)}, bf16[16,2176]{1,0:T(8,128)(2,1)S(1)}, u32[]{:S(2)}, u32[]{:S(2)}) collective-permute-start(bf16[16,2176]{1,0:T(8,128)(2,1)S(1)} %collective-permute-done.2.refs_3_), channel_id=1, source_target_pairs={{0,4},{4,0},{8,12},{12,8},{16,20},{20,16},{24,28},{28,24},{1,5},{5... | collective-permute-start | bytes 208904 | tf_op jit(solution)/shard_map/ppermute | solution.py:18
  13.8 5.8 %collective-permute-start.9 = (bf16[128,1024]{1,0:T(8,128)(2,1)S(1)}, bf16[128,1024]{1,0:T(8,128)(2,1)S(1)}, u32[]{:S(2)}, u32[]{:S(2)}) collective-permute-start(bf16[128,1024]{1,0:T(8,128)(2,1)S(1)} %branch.7), channel_id=1, source_target_pairs={{0,12},{4,16},{8,4},{12,24},{16,28},{20,0},{24,20},{28,8},{1,13},{... | collective-permute-start | bytes 786440 | tf_op jit(solution)/shard_map/ppermute | solution.py:324
  16.5 6.5 %collective-permute-start.8 = (bf16[128,1024]{1,0:T(8,128)(2,1)S(1)}, bf16[128,1024]{1,0:T(8,128)(2,1)S(1)}, u32[]{:S(2)}, u32[]{:S(2)}) collective-permute-start(bf16[128,1024]{1,0:T(8,128)(2,1)S(1)} %branch.5), channel_id=1, source_target_pairs={{0,8},{4,20},{8,0},{12,28},{16,24},{20,4},{24,16},{28,12},{1,9},{5... | collective-permute-start | bytes 786440 | tf_op jit(solution)/shard_map/ppermute | solution.py:325
  19.7 5.9 %copy-start = (bf16[128,1024]{1,0:T(8,128)(2,1)S(1)}, bf16[128,1024]{1,0:T(8,128)(2,1)}, u32[]{:S(2)}) copy-start(bf16[128,1024]{1,0:T(8,128)(2,1)} %tokens_hbm.1) | copy-start | bytes 786436
  19.7 5.8 %collective-permute-start.10 = (bf16[128,1024]{1,0:T(8,128)(2,1)S(1)}, bf16[128,1024]{1,0:T(8,128)(2,1)S(1)}, u32[]{:S(2)}, u32[]{:S(2)}) collective-permute-start(bf16[128,1024]{1,0:T(8,128)(2,1)S(1)} %add_convert_fusion.1), channel_id=1, source_target_pairs={{0,12},{4,16},{8,4},{12,24},{16,28},{20,0},{24,20},{28,8},{1,13},{... | collective-permute-start | bytes 786440 | tf_op jit(solution)/shard_map/ppermute | solution.py:327

commit v7 on v6

--- a/solution.py
+++ b/solution.py
@@ -9,6 +9,7 @@
 
 MIB = 1024 * 1024
 EXTRA = 16
+GROUP = 6
 VMEM = pl.BlockSpec(memory_space=pltpu.VMEM)
 SMEM = pl.BlockSpec(memory_space=pltpu.SMEM)
 HBM = pl.BlockSpec(memory_space=pltpu.HBM)
@@ -120,10 +121,38 @@
     return jnp.where(core == 0, value, turned)
 
 
+def turn_taps(base, strip, k, fine, rows):
+    length = base.shape[1]
+    row = lax.broadcasted_iota(jnp.int32, (fine, rows), 0)
+    lane = lax.broadcasted_iota(jnp.int32, (fine, rows), 1)
+    kept = lane - row <= rows - fine
+    line = jnp.broadcast_to(base[k : k + 1, :], (8, length))
+    line = pltpu.roll(line, length - fine + 1, 1, stride=1, stride_axis=0)
+    lines = [line] + [pltpu.roll(line, step, 1) for step in range(8, fine, 8)]
+    whole = jnp.concatenate(lines, axis=0)
+    cut = slice(k * fine, (k + 1) * fine)
+    strip[cut, : length - rows] = whole[:, : length - rows].astype(jnp.bfloat16)
+    strip[cut, length - rows : length] = jnp.where(kept, whole[:, length - rows :], 0.0).astype(
+        jnp.bfloat16
+    )
+
+
+def write_features(feats, total, k, num, groups):
+    fine = total.shape[0]
+    half = total.shape[1] // groups // 2
+    for which in range(2):
+        for g in range(groups):
+            to = (which * num + k) * half
+            at = (2 * g + which) * half
+            feats[g * fine : (g + 1) * fine, to : to + half] = total[:, at : at + half].astype(
+                jnp.bfloat16
+            )
+
+
 def merge_kernel(chips, shifts, rows, num, fine, *refs):
     own = refs[:chips]
     pair = refs[chips : 2 * chips]
-    signal, strip, base = refs[2 * chips :]
+    mix_ref, pair_mix_ref, signal, strip, out_ref, base, feats = refs[2 * chips :]
     devices = 2 * chips
     length = devices * rows
     groups = rows // fine
@@ -142,20 +171,26 @@
                     signal[pl.ds(at, EXTRA), g * count : (g + 1) * count] = value
             at = pl.multiple_of((devices - 1 - place) * rows, rows)
             base[:, pl.ds(at, rows)] = block[:, rows // EXTRA * count :].astype(jnp.float32)
-    row = lax.broadcasted_iota(jnp.int32, (fine, rows), 0)
-    lane = lax.broadcasted_iota(jnp.int32, (fine, rows), 1)
-    kept = lane - row <= rows - fine
     strip[:, length:] = jnp.zeros((num * fine, rows), jnp.bfloat16)
-    for k in range(num):
-        line = jnp.broadcast_to(base[k : k + 1, :], (8, length))
-        line = pltpu.roll(line, length - fine + 1, 1, stride=1, stride_axis=0)
-        lines = [line] + [pltpu.roll(line, step, 1) for step in range(8, fine, 8)]
-        whole = jnp.concatenate(lines, axis=0)
-        cut = slice(k * fine, (k + 1) * fine)
-        strip[cut, : length - rows] = whole[:, : length - rows].astype(jnp.bfloat16)
-        strip[cut, length - rows : length] = jnp.where(kept, whole[:, length - rows :], 0.0).astype(
-            jnp.bfloat16
-        )
+    other, part = aim(lax.axis_index("seq") // 2, core, "far")
+    offset = (devices - 1 - (2 * other + part)) * rows
+
+    def convolve(steps):
+        depth = 2 * rows * steps
+        for first in range(0, num, GROUP):
+            for k in range(first, first + GROUP):
+                turn_taps(base, strip, k, fine, rows)
+            left = strip[
+                first * fine : (first + GROUP) * fine, pl.ds(pl.multiple_of(offset, rows), depth)
+            ]
+            total = jnp.dot(left, signal[0:depth, :], preferred_element_type=jnp.float32)
+            for k in range(first, first + GROUP):
+                write_features(feats, total[(k - first) * fine : (k - first + 1) * fine], k, num, groups)
+
+    for steps in range(1, chips + 1):
+        pl.when(other == steps - 1)(functools.partial(convolve, steps))
+    total = project(feats, mix_ref, pair_mix_ref)
+    out_ref[...] = total.astype(out_ref.dtype)
 
 
 def strip_kernel(chips, rows, num, *refs):
@@ -199,13 +234,7 @@
         left = strip[:, pl.ds(pl.multiple_of(offset, rows), depth)]
         total = jnp.dot(left, signal[0:depth, :], preferred_element_type=jnp.float32)
         for k in range(num):
-            for which in range(2):
-                for g in range(rows // fine):
-                    to = (which * num + k) * half
-                    at = (2 * g + which) * half
-                    feats[g * fine : (g + 1) * fine, to : to + half] = total[
-                        k * fine : (k + 1) * fine, at : at + half
-                    ].astype(jnp.bfloat16)
+            write_features(feats, total[k * fine : (k + 1) * fine], k, num, rows // fine)
 
     for steps in range(1, chips + 1):
         pl.when(other == steps - 1)(functools.partial(convolve, steps))
@@ -246,7 +275,7 @@
     num, span = filters.shape
     length = devices * rows
     count = width // chips
-    relay = chips == 4 and count % 256 == 0 and span == rows and rows % EXTRA == 0 and num <= EXTRA
+    relay = chips == 4 and count % 256 == 0 and span == rows and rows % EXTRA == 0 and num <= EXTRA and num % GROUP == 0
     pair_mixing = swap(mixing, 1, devices)
     fine = 32 if relay else rows
     flat = (EXTRA, rows // EXTRA * count + span) if relay else (rows, count)
@@ -286,14 +315,18 @@
         jax.ShapeDtypeStruct((num * fine, length + rows), jnp.bfloat16),
     ]
     if relay:
-        signal, strip = kernel_call(
+        block = jax.ShapeDtypeStruct((rows, width), jnp.bfloat16)
+        signal, strip, far = kernel_call(
             functools.partial(merge_kernel, chips, shifts, rows, num, fine),
             "merge",
-            shapes,
-            [VMEM] * (2 * chips),
-            16 * MIB,
-            [pltpu.VMEM((EXTRA, length), jnp.float32)],
-        )(*ends)
+            [*shapes, block],
+            [VMEM] * (2 * chips + 2),
+            24 * MIB,
+            [
+                pltpu.VMEM((EXTRA, length), jnp.float32),
+                pltpu.VMEM((rows, num * count), jnp.bfloat16),
+            ],
+        )(*ends, near_mixing, pair_mixing)
     else:
         taps = lax.all_gather(filters, "seq", axis=1, tiled=True)[:, ::-1]
         taps = jnp.pad(taps, ((0, EXTRA - num), (0, 2 * rows)))
@@ -321,7 +354,7 @@
         pairs = [(c, q) for c in range(chips) for q in range(2)]
         across = [(2 * c + q, 2 * (c ^ (1 + q)) + 1 - q) for c, q in pairs]
         along = [(2 * c + q, 2 * (c ^ (1 + q)) + q) for c, q in pairs]
-        far = lax.ppermute(branch("far", jnp.bfloat16), "seq", across)
+        far = lax.ppermute(far, "seq", across)
         early = lax.ppermute(branch("early", jnp.bfloat16), "seq", along)
         late = (branch("late", jnp.float32) + far.astype(jnp.float32)).astype(jnp.bfloat16)
         late = lax.ppermute(late, "seq", across)

time: 26.6 us -> 26.3 us (0.989)
  Pallas kernels: 10.4 us -> 10.1 us
    pallas_call x4 -> x3, Pallas kernels: 6.5 us -> 4.5 us  [branch(): kernel_call(functools.partial(branch_kernel, chips, rows, fine, kind), 'b...]
    pallas_call x1, Pallas kernels: 0.76 us -> 2.44 us  [local(): kernel_call(functools.partial(merge_kernel, chips, shifts, rows, num, fin...]
  transfers between devices with their start and end apart: 11 -> 11, of which waited for: 6 -> 6; matrix products, arithmetic and copies ran while one was open for 0% -> 0% of each run, Pallas kernels for 32% -> 29%
where the time goes in v7:
time: 26.3 us; the launch traced here: 26.1 us
  Pallas kernels  10.1 us (38%)
  starting transfers between devices  8.5 us (32%)
  waiting for transfers between devices  6.55 us (25%)
  other arithmetic  0.9 us (3%)
    ppermute x8, starting transfers between devices, swap(): return lax.ppermute(value, 'seq', [(i, i ^ bits) for i in range(size)])  5.49 us
    pallas_call x3, Pallas kernels, branch(): kernel_call(functools.partial(branch_kernel, chips, rows, fine, kind), 'b...  4.5 us
    ppermute x1, waiting for transfers between devices, local(): late = lax.ppermute(late, 'seq', across)  2.58 us
    pallas_call x1, Pallas kernels, local(): kernel_call(functools.partial(merge_kernel, chips, shifts, rows, num, fin...  2.44 us
    ppermute x8, waiting for transfers between devices, swap(): return lax.ppermute(value, 'seq', [(i, i ^ bits) for i in range(size)])  2.39 us
    pallas_call x1, Pallas kernels, local(): kernel_call(stage_kernel, 'stage', [jax.ShapeDtypeStruct(mixing.shape, mi...  1.9 us
    pallas_call x1, Pallas kernels, local(): kernel_call(norm_kernel, 'norm', [jax.ShapeDtypeStruct(flat, jnp.bfloat16...  1.22 us
    ppermute x1, starting transfers between devices, local(): far = lax.ppermute(far, 'seq', across)  1.11 us
  transfers between devices with their start and end apart: 11, of which 6 were waited for; matrix products, arithmetic and copies ran while one was open for 0% of the time, Pallas kernels for 29%

profile of v7, /device:TPU:0, one launch (start us, length us, event | category | flops | bytes accessed | tf_op | source)
XLA Modules:
  0.0 26.1 jit_solution(8011941017392420515)
XLA Ops:
  0.0 0.5 %collective-permute-start.7 = (bf16[12,128,1024]{2,1,0:T(8,128)(2,1)}, bf16[12,128,1024]{2,1,0:T(8,128)(2,1)S(1)}, u32[]{:S(2)}, u32[]{:S(2)}) collective-permute-start(bf16[12,128,1024]{2,1,0:T(8,128)(2,1)} %mix_hbm.1), channel_id=1, source_target_pairs={{0,4},{4,0},{8,12},{12,8},{16,20},{20,16},{24,28},{28,24},{1,5},{5... | collective-permute-start | bytes 9437192 | tf_op jit(solution)/shard_map/ppermute | solution.py:19
  0.5 1.2 %norm.1 = (bf16[16,2176]{1,0:T(8,128)(2,1)S(1)}, bf16[16,2176]{1,0:T(8,128)(2,1)S(1)}, bf16[16,2176]{1,0:T(8,128)(2,1)S(1)}, bf16[16,2176]{1,0:T(8,128)(2,1)S(1)}) custom-call(bf16[128,1024]{1,0:T(8,128)(2,1)} %tokens_hbm.1, f32[1,1024]{1,0:T(1,128)} %bitcast.1, f32[12,128]{1,0:T(8,128)} %filters_hbm.1), custom_call_target="tpu_custom_call" | custom-call | tf_op jit(solution)/shard_map/norm/pallas_call | solution.py:282
  1.7 3.6 %collective-permute-start = (bf16[16,2176]{1,0:T(8,128)(2,1)S(1)}, bf16[16,2176]{1,0:T(8,128)(2,1)S(1)}, u32[]{:S(2)}, u32[]{:S(2)}) collective-permute-start(bf16[16,2176]{1,0:T(8,128)(2,1)S(1)} %get-tuple-element.15), channel_id=1, source_target_pairs={{0,28},{4,24},{8,20},{12,16},{16,12},{20,8},{24,4},{28,0},{1,29},{... | collective-permute-start | bytes 208904 | tf_op jit(solution)/shard_map/ppermute | solution.py:19
  5.3 0.1 collective-permute-start.1
  5.5 0.1 collective-permute-start.2
  5.6 1.9 %stage.1 = (bf16[12,128,1024]{2,1,0:T(8,128)(2,1)S(1)}, bf16[16,2176]{1,0:T(8,128)(2,1)S(1)}) custom-call(bf16[12,128,1024]{2,1,0:T(8,128)(2,1)} %mix_hbm.1, bf16[16,2176]{1,0:T(8,128)(2,1)S(1)} %get-tuple-element.14.block_ref.refs_0_), custom_call_target="tpu_custom_call" | custom-call | tf_op jit(solution)/shard_map/stage/pallas_call | solution.py:295
  7.5 0.6 %collective-permute-start.3 = (bf16[16,2176]{1,0:T(8,128)(2,1)S(1)}, bf16[16,2176]{1,0:T(8,128)(2,1)S(1)}, u32[]{:S(2)}, u32[]{:S(2)}) collective-permute-start(bf16[16,2176]{1,0:T(8,128)(2,1)S(1)} %get-tuple-element.18), channel_id=1, source_target_pairs={{0,4},{4,0},{8,12},{12,8},{16,20},{20,16},{24,28},{28,24},{1,5},{5... | collective-permute-start | bytes 208904 | tf_op jit(solution)/shard_map/ppermute | solution.py:19
  8.0 0.0 collective-permute-done.refs_1_
  8.0 0.1 collective-permute-start.4
  8.1 1.5 %collective-permute-done.1.refs_2_ = bf16[16,2176]{1,0:T(8,128)(2,1)S(1)} collective-permute-done((bf16[16,2176]{1,0:T(8,128)(2,1)S(1)}, bf16[16,2176]{1,0:T(8,128)(2,1)S(1)}, u32[]{:S(2)}, u32[]{:S(2)}) %collective-permute-start.1) | collective-permute-done | bytes 69664 | tf_op jit(solution)/shard_map/ppermute | solution.py:19
  9.6 0.1 collective-permute-start.5
  9.7 0.0 collective-permute-done.2.refs_3_
  9.7 0.4 %collective-permute-start.6 = (bf16[16,2176]{1,0:T(8,128)(2,1)S(1)}, bf16[16,2176]{1,0:T(8,128)(2,1)S(1)}, u32[]{:S(2)}, u32[]{:S(2)}) collective-permute-start(bf16[16,2176]{1,0:T(8,128)(2,1)S(1)} %collective-permute-done.2.refs_3_), channel_id=1, source_target_pairs={{0,4},{4,0},{8,12},{12,8},{16,20},{20,16},{24,28},{28,24},{1,5},{5... | collective-permute-start | bytes 208904 | tf_op jit(solution)/shard_map/ppermute | solution.py:19
  10.1 0.0 collective-permute-done.3.refs_4_
  10.1 0.0 collective-permute-done.4.refs_5_
  10.1 0.7 %collective-permute-done.5.refs_6_ = bf16[16,2176]{1,0:T(8,128)(2,1)S(1)} collective-permute-done((bf16[16,2176]{1,0:T(8,128)(2,1)S(1)}, bf16[16,2176]{1,0:T(8,128)(2,1)S(1)}, u32[]{:S(2)}, u32[]{:S(2)}) %collective-permute-start.5) | collective-permute-done | bytes 69664 | tf_op jit(solution)/shard_map/ppermute | solution.py:19
  10.9 0.2 collective-permute-done.6.refs_7_
  11.0 0.0 collective-permute-done.7.refs_9_.refs_3_
  11.0 2.4 %merge.1 = (bf16[1152,1024]{1,0:T(8,128)(2,1)S(1)}, bf16[384,1152]{1,0:T(8,128)(2,1)S(1)}, bf16[128,1024]{1,0:T(8,128)(2,1)S(1)}) custom-call(bf16[16,2176]{1,0:T(8,128)(2,1)S(1)} %get-tuple-element.14.block_ref.refs_0_, bf16[16,2176]{1,0:T(8,128)(2,1)S(1)} %collective-permute-done.refs_1_, bf16[16,2176]{1,0:T(8,128)(2,1)S(1)} %collective-permute-done.1.refs_2_, ...), custom_call_target="tpu_custom_call" | custom-call | tf_op jit(solution)/shard_map/merge/pallas_call | solution.py:319
  13.5 1.1 %collective-permute-start.9 = (bf16[128,1024]{1,0:T(8,128)(2,1)S(1)}, bf16[128,1024]{1,0:T(8,128)(2,1)S(1)}, u32[]{:S(2)}, u32[]{:S(2)}) collective-permute-start(bf16[128,1024]{1,0:T(8,128)(2,1)S(1)} %get-tuple-element.22), channel_id=1, source_target_pairs={{0,12},{4,16},{8,4},{12,24},{16,28},{20,0},{24,20},{28,8},{1,13},{... | collective-permute-start | bytes 786440 | tf_op jit(solution)/shard_map/ppermute | solution.py:357
  14.6 1.6 %branch.4 = bf16[128,1024]{1,0:T(8,128)(2,1)S(1)} custom-call(bf16[1152,1024]{1,0:T(8,128)(2,1)S(1)} %get-tuple-element.20.refs_0_, bf16[384,1152]{1,0:T(8,128)(2,1)S(1)} %get-tuple-element.21.refs_1_, bf16[12,128,1024]{2,1,0:T(8,128)(2,1)S(1)} %get-tuple-element.19.refs_8_.refs_2_, bf16[12,128,1024]{2,1,0:T(8,128)(2,1)S(1)} %collective-permute-done.7.refs_9_.refs_3_), custom_call_target="tpu_custom_call" | custom-call | tf_op jit(solution)/shard_map/branch/pallas_call | solution.py:345
  16.2 0.8 %collective-permute-start.8 = (bf16[128,1024]{1,0:T(8,128)(2,1)S(1)}, bf16[128,1024]{1,0:T(8,128)(2,1)S(1)}, u32[]{:S(2)}, u32[]{:S(2)}) collective-permute-start(bf16[128,1024]{1,0:T(8,128)(2,1)S(1)} %branch.4), channel_id=1, source_target_pairs={{0,8},{4,20},{8,0},{12,28},{16,24},{20,4},{24,16},{28,12},{1,9},{5... | collective-permute-start | bytes 786440 | tf_op jit(solution)/shard_map/ppermute | solution.py:358
  16.9 1.6 %branch.5 = f32[128,1024]{1,0:T(8,128)S(1)} custom-call(bf16[1152,1024]{1,0:T(8,128)(2,1)S(1)} %get-tuple-element.20.refs_0_, bf16[384,1152]{1,0:T(8,128)(2,1)S(1)} %get-tuple-element.21.refs_1_, bf16[12,128,1024]{2,1,0:T(8,128)(2,1)S(1)} %get-tuple-element.19.refs_8_.refs_2_, bf16[12,128,1024]{2,1,0:T(8,128)(2,1)S(1)} %collective-permute-done.7.refs_9_.refs_3_), custom_call_target="tpu_custom_call" | custom-call | tf_op jit(solution)/shard_map/branch/pallas_call | solution.py:345
  18.5 0.8 %collective-permute-done.9 = bf16[128,1024]{1,0:T(8,128)(2,1)S(1)} collective-permute-done((bf16[128,1024]{1,0:T(8,128)(2,1)S(1)}, bf16[128,1024]{1,0:T(8,128)(2,1)S(1)}, u32[]{:S(2)}, u32[]{:S(2)}) %collective-permute-start.9) | collective-permute-done | bytes 262176 | tf_op jit(solution)/shard_map/ppermute | solution.py:357
  19.3 0.1 add_convert_fusion.1
  19.4 0.0 copy-start
  19.4 1.1 %collective-permute-start.10 = (bf16[128,1024]{1,0:T(8,128)(2,1)S(1)}, bf16[128,1024]{1,0:T(8,128)(2,1)S(1)}, u32[]{:S(2)}, u32[]{:S(2)}) collective-permute-start(bf16[128,1024]{1,0:T(8,128)(2,1)S(1)} %add_convert_fusion.1), channel_id=1, source_target_pairs={{0,12},{4,16},{8,4},{12,24},{16,28},{20,0},{24,20},{28,8},{1,13},{... | collective-permute-start | bytes 786440 | tf_op jit(solution)/shard_map/ppermute | solution.py:360
  20.5 1.4 %branch.3 = f32[128,1024]{1,0:T(8,128)S(1)} custom-call(bf16[1152,1024]{1,0:T(8,128)(2,1)S(1)} %get-tuple-element.20.refs_0_, bf16[384,1152]{1,0:T(8,128)(2,1)S(1)} %get-tuple-element.21.refs_1_, bf16[12,128,1024]{2,1,0:T(8,128)(2,1)S(1)} %get-tuple-element.19.refs_8_.refs_2_, bf16[12,128,1024]{2,1,0:T(8,128)(2,1)S(1)} %collective-permute-done.7.refs_9_.refs_3_), custom_call_target="tpu_custom_call" | custom-call | tf_op jit(solution)/shard_map/branch/pallas_call | solution.py:345
  21.9 0.8 %collective-permute-done.8 = bf16[128,1024]{1,0:T(8,128)(2,1)S(1)} collective-permute-done((bf16[128,1024]{1,0:T(8,128)(2,1)S(1)}, bf16[128,1024]{1,0:T(8,128)(2,1)S(1)}, u32[]{:S(2)}, u32[]{:S(2)}) %collective-permute-start.8) | collective-permute-done | bytes 262176 | tf_op jit(solution)/shard_map/ppermute | solution.py:358
  22.7 2.6 %collective-permute-done.10 = bf16[128,1024]{1,0:T(8,128)(2,1)S(1)} collective-permute-done((bf16[128,1024]{1,0:T(8,128)(2,1)S(1)}, bf16[128,1024]{1,0:T(8,128)(2,1)S(1)}, u32[]{:S(2)}, u32[]{:S(2)}) %collective-permute-start.10) | collective-permute-done | bytes 262176 | tf_op jit(solution)/shard_map/ppermute | solution.py:360
  25.2 0.0 copy-done
  25.2 0.8 %add_convert_fusion = bf16[128,1024]{1,0:T(8,128)(2,1)} fusion(bf16[128,1024]{1,0:T(8,128)(2,1)S(1)} %collective-permute-done.10, bf16[128,1024]{1,0:T(8,128)(2,1)S(1)} %collective-permute-done.8, f32[128,1024]{1,0:T(8,128)S(1)} %branch.3, bf16[128,1024]{1,0:T(8,128)(2,1)S(1)} %copy-done), kind=kLoop, calls=%fused_computation | loop fusion | flops 917504 | bytes 1572864 | tf_op jit(solution)/shard_map/convert_element_type | solution.py:379
Async XLA Ops:
  0.0 11.0 %collective-permute-start.7 = (bf16[12,128,1024]{2,1,0:T(8,128)(2,1)}, bf16[12,128,1024]{2,1,0:T(8,128)(2,1)S(1)}, u32[]{:S(2)}, u32[]{:S(2)}) collective-permute-start(bf16[12,128,1024]{2,1,0:T(8,128)(2,1)} %mix_hbm.1), channel_id=1, source_target_pairs={{0,4},{4,0},{8,12},{12,8},{16,20},{20,16},{24,28},{28,24},{1,5},{5... | collective-permute-start | bytes 9437192 | tf_op jit(solution)/shard_map/ppermute | solution.py:19
  1.7 6.4 %collective-permute-start = (bf16[16,2176]{1,0:T(8,128)(2,1)S(1)}, bf16[16,2176]{1,0:T(8,128)(2,1)S(1)}, u32[]{:S(2)}, u32[]{:S(2)}) collective-permute-start(bf16[16,2176]{1,0:T(8,128)(2,1)S(1)} %get-tuple-element.15), channel_id=1, source_target_pairs={{0,28},{4,24},{8,20},{12,16},{16,12},{20,8},{24,4},{28,0},{1,29},{... | collective-permute-start | bytes 208904 | tf_op jit(solution)/shard_map/ppermute | solution.py:19
  5.3 4.3 %collective-permute-start.1 = (bf16[16,2176]{1,0:T(8,128)(2,1)S(1)}, bf16[16,2176]{1,0:T(8,128)(2,1)S(1)}, u32[]{:S(2)}, u32[]{:S(2)}) collective-permute-start(bf16[16,2176]{1,0:T(8,128)(2,1)S(1)} %get-tuple-element.16), channel_id=1, source_target_pairs={{0,12},{4,8},{8,4},{12,0},{16,28},{20,24},{24,20},{28,16},{1,13},{... | collective-permute-start | bytes 208904 | tf_op jit(solution)/shard_map/ppermute | solution.py:19
  5.5 4.3 %collective-permute-start.2 = (bf16[16,2176]{1,0:T(8,128)(2,1)S(1)}, bf16[16,2176]{1,0:T(8,128)(2,1)S(1)}, u32[]{:S(2)}, u32[]{:S(2)}) collective-permute-start(bf16[16,2176]{1,0:T(8,128)(2,1)S(1)} %get-tuple-element.17), channel_id=1, source_target_pairs={{0,20},{4,16},{8,28},{12,24},{16,4},{20,0},{24,12},{28,8},{1,21},{... | collective-permute-start | bytes 208904 | tf_op jit(solution)/shard_map/ppermute | solution.py:19
  7.5 2.7 %collective-permute-start.3 = (bf16[16,2176]{1,0:T(8,128)(2,1)S(1)}, bf16[16,2176]{1,0:T(8,128)(2,1)S(1)}, u32[]{:S(2)}, u32[]{:S(2)}) collective-permute-start(bf16[16,2176]{1,0:T(8,128)(2,1)S(1)} %get-tuple-element.18), channel_id=1, source_target_pairs={{0,4},{4,0},{8,12},{12,8},{16,20},{20,16},{24,28},{28,24},{1,5},{5... | collective-permute-start | bytes 208904 | tf_op jit(solution)/shard_map/ppermute | solution.py:19
  8.0 2.1 %collective-permute-start.4 = (bf16[16,2176]{1,0:T(8,128)(2,1)S(1)}, bf16[16,2176]{1,0:T(8,128)(2,1)S(1)}, u32[]{:S(2)}, u32[]{:S(2)}) collective-permute-start(bf16[16,2176]{1,0:T(8,128)(2,1)S(1)} %collective-permute-done.refs_1_), channel_id=1, source_target_pairs={{0,4},{4,0},{8,12},{12,8},{16,20},{20,16},{24,28},{28,24},{1,5},{5... | collective-permute-start | bytes 208904 | tf_op jit(solution)/shard_map/ppermute | solution.py:19
  9.6 1.3 %collective-permute-start.5 = (bf16[16,2176]{1,0:T(8,128)(2,1)S(1)}, bf16[16,2176]{1,0:T(8,128)(2,1)S(1)}, u32[]{:S(2)}, u32[]{:S(2)}) collective-permute-start(bf16[16,2176]{1,0:T(8,128)(2,1)S(1)} %collective-permute-done.1.refs_2_), channel_id=1, source_target_pairs={{0,4},{4,0},{8,12},{12,8},{16,20},{20,16},{24,28},{28,24},{1,5},{5... | collective-permute-start | bytes 208904 | tf_op jit(solution)/shard_map/ppermute | solution.py:19
  9.7 1.3 %collective-permute-start.6 = (bf16[16,2176]{1,0:T(8,128)(2,1)S(1)}, bf16[16,2176]{1,0:T(8,128)(2,1)S(1)}, u32[]{:S(2)}, u32[]{:S(2)}) collective-permute-start(bf16[16,2176]{1,0:T(8,128)(2,1)S(1)} %collective-permute-done.2.refs_3_), channel_id=1, source_target_pairs={{0,4},{4,0},{8,12},{12,8},{16,20},{20,16},{24,28},{28,24},{1,5},{5... | collective-permute-start | bytes 208904 | tf_op jit(solution)/shard_map/ppermute | solution.py:19
  13.5 5.8 %collective-permute-start.9 = (bf16[128,1024]{1,0:T(8,128)(2,1)S(1)}, bf16[128,1024]{1,0:T(8,128)(2,1)S(1)}, u32[]{:S(2)}, u32[]{:S(2)}) collective-permute-start(bf16[128,1024]{1,0:T(8,128)(2,1)S(1)} %get-tuple-element.22), channel_id=1, source_target_pairs={{0,12},{4,16},{8,4},{12,24},{16,28},{20,0},{24,20},{28,8},{1,13},{... | collective-permute-start | bytes 786440 | tf_op jit(solution)/shard_map/ppermute | solution.py:357
  16.2 6.5 %collective-permute-start.8 = (bf16[128,1024]{1,0:T(8,128)(2,1)S(1)}, bf16[128,1024]{1,0:T(8,128)(2,1)S(1)}, u32[]{:S(2)}, u32[]{:S(2)}) collective-permute-start(bf16[128,1024]{1,0:T(8,128)(2,1)S(1)} %branch.4), channel_id=1, source_target_pairs={{0,8},{4,20},{8,0},{12,28},{16,24},{20,4},{24,16},{28,12},{1,9},{5... | collective-permute-start | bytes 786440 | tf_op jit(solution)/shard_map/ppermute | solution.py:358
  19.4 5.9 %copy-start = (bf16[128,1024]{1,0:T(8,128)(2,1)S(1)}, bf16[128,1024]{1,0:T(8,128)(2,1)}, u32[]{:S(2)}) copy-start(bf16[128,1024]{1,0:T(8,128)(2,1)} %tokens_hbm.1) | copy-start | bytes 786436
  19.4 5.8 %collective-permute-start.10 = (bf16[128,1024]{1,0:T(8,128)(2,1)S(1)}, bf16[128,1024]{1,0:T(8,128)(2,1)S(1)}, u32[]{:S(2)}, u32[]{:S(2)}) collective-permute-start(bf16[128,1024]{1,0:T(8,128)(2,1)S(1)} %add_convert_fusion.1), channel_id=1, source_target_pairs={{0,12},{4,16},{8,4},{12,24},{16,28},{20,0},{24,20},{28,8},{1,13},{... | collective-permute-start | bytes 786440 | tf_op jit(solution)/shard_map/ppermute | solution.py:360

commit v8 on v7

--- a/solution.py
+++ b/solution.py
@@ -9,6 +9,7 @@
 
 MIB = 1024 * 1024
 EXTRA = 16
+PARTS = 2
 GROUP = 6
 VMEM = pl.BlockSpec(memory_space=pltpu.VMEM)
 SMEM = pl.BlockSpec(memory_space=pltpu.SMEM)
@@ -85,12 +86,26 @@
     copy.wait()
 
 
+def finish_kernel(tokens_ref, own_ref, early_ref, late_ref, out_hbm, held, sems):
+    chunk = held.shape[0] // PARTS
+    copies = []
+    for i in range(PARTS):
+        cut = pl.ds(i * chunk, chunk)
+        total = tokens_ref[cut, :].astype(jnp.float32) + own_ref[cut, :]
+        total = total + early_ref[cut, :].astype(jnp.float32)
+        held[cut, :] = (total + late_ref[cut, :].astype(jnp.float32)).astype(held.dtype)
+        copies.append(pltpu.make_async_copy(held.at[cut], out_hbm.at[cut], sems.at[i]))
+        copies[-1].start()
+    for copy in copies:
+        copy.wait()
+
+
 def aim(chip, core, kind):
     if kind == "far":
         return chip ^ 3, core
     if kind == "own":
         return chip, core
-    return chip ^ (1 + core), core if kind == "early" else 1 - core
+    return chip ^ (2 - core), core if kind == "early" else 1 - core
 
 
 def project(feats, mix_ref, pair_mix_ref):
@@ -304,7 +319,7 @@
         [pltpu.SemaphoreType.DMA(())],
     )(in_hbm(mixing), blocks[0])
     work = 2 * num * rows * count * (width + length)
-    shifts = [0, 3, 1, 2] if relay else list(range(chips))
+    shifts = [0, 3, 2, 1] if relay else list(range(chips))
     own = {s: swap(blocks[s], 2 * s + 1, devices) for s in reversed(shifts) if s}
     own[0] = first
     pair = {s: swap(own[s], 1, devices) for s in shifts}
@@ -338,7 +353,6 @@
             48 * MIB,
         )(*ends, taps)
     fixed = [signal, strip, near_mixing, pair_mixing]
-    total = tokens.astype(jnp.float32)
     if relay:
 
         def branch(kind, dtype):
@@ -352,14 +366,24 @@
             )(*fixed)
 
         pairs = [(c, q) for c in range(chips) for q in range(2)]
-        across = [(2 * c + q, 2 * (c ^ (1 + q)) + 1 - q) for c, q in pairs]
-        along = [(2 * c + q, 2 * (c ^ (1 + q)) + q) for c, q in pairs]
+        across = [(2 * c + q, 2 * (c ^ (2 - q)) + 1 - q) for c, q in pairs]
+        along = [(2 * c + q, 2 * (c ^ (2 - q)) + q) for c, q in pairs]
         far = lax.ppermute(far, "seq", across)
         early = lax.ppermute(branch("early", jnp.bfloat16), "seq", along)
         late = (branch("late", jnp.float32) + far.astype(jnp.float32)).astype(jnp.bfloat16)
         late = lax.ppermute(late, "seq", across)
-        total = total + branch("own", jnp.float32)
-        sent = [early, late]
+        return pl.pallas_call(
+            finish_kernel,
+            out_shape=jax.ShapeDtypeStruct((rows, width), tokens.dtype),
+            in_specs=[VMEM] * 4,
+            out_specs=HBM,
+            scratch_shapes=[
+                pltpu.VMEM((rows, width), tokens.dtype),
+                pltpu.SemaphoreType.DMA((PARTS,)),
+            ],
+            compiler_params=pltpu.CompilerParams(vmem_limit_bytes=8 * MIB),
+            name="finish",
+        )(tokens, branch("own", jnp.float32), early, late)
     else:
 
         def branch(shift):
@@ -374,6 +398,7 @@
 
         parts = lax.map(branch, jnp.arange(chips, dtype=jnp.int32))
         sent = [parts[0]] + [swap(parts[s], 2 * s, devices) for s in range(1, chips)]
+    total = tokens.astype(jnp.float32)
     for value in sent:
         total = total + value.astype(jnp.float32)
     return total.astype(jnp.bfloat16)

time: 26.3 us -> 26.2 us (level)
  Pallas kernels: 10.1 us -> 11.3 us
  other arithmetic: 0.9 us -> 0.05 us
    convert_element_type x1 -> x0, other arithmetic: 0.85 us -> none  [local(): return total.astype(jnp.bfloat16)]
    pallas_call x0 -> x1, Pallas kernels: none -> 0.79 us  [local(): pl.pallas_call(finish_kernel, out_shape=jax.ShapeDtypeStruct((rows, width...]
    pallas_call x3, Pallas kernels: 4.5 us -> 4.92 us  [branch(): kernel_call(functools.partial(branch_kernel, chips, rows, fine, kind), 'b...]
  transfers between devices with their start and end apart: 11 -> 11, of which waited for: 6 -> 6; matrix products, arithmetic and copies ran while one was open for 0% -> 0% of each run, Pallas kernels for 29% -> 31%
where the time goes in v8:
time: 26.2 us; the launch traced here: 26 us
  Pallas kernels  11.3 us (43%)
  starting transfers between devices  8.28 us (32%)
  waiting for transfers between devices  6.35 us (24%)
    ppermute x8, starting transfers between devices, swap(): return lax.ppermute(value, 'seq', [(i, i ^ bits) for i in range(size)])  5.49 us
    pallas_call x3, Pallas kernels, branch(): kernel_call(functools.partial(branch_kernel, chips, rows, fine, kind), 'b...  4.92 us
    ppermute x1, waiting for transfers between devices, local(): late = lax.ppermute(late, 'seq', across)  2.45 us
    pallas_call x1, Pallas kernels, local(): kernel_call(functools.partial(merge_kernel, chips, shifts, rows, num, fin...  2.44 us
    ppermute x8, waiting for transfers between devices, swap(): return lax.ppermute(value, 'seq', [(i, i ^ bits) for i in range(size)])  2.39 us
    pallas_call x1, Pallas kernels, local(): kernel_call(stage_kernel, 'stage', [jax.ShapeDtypeStruct(mixing.shape, mi...  1.9 us
    pallas_call x1, Pallas kernels, local(): kernel_call(norm_kernel, 'norm', [jax.ShapeDtypeStruct(flat, jnp.bfloat16...  1.22 us
    ppermute x1, starting transfers between devices, local(): late = lax.ppermute(late, 'seq', across)  1.1 us
  transfers between devices with their start and end apart: 11, of which 6 were waited for; matrix products, arithmetic and copies ran while one was open for 0% of the time, Pallas kernels for 31%

profile of v8, /device:TPU:0, one launch (start us, length us, event | category | flops | bytes accessed | tf_op | source)
XLA Modules:
  0.0 26.0 jit_solution(3022365698939227596)
XLA Ops:
  0.0 0.5 %collective-permute-start.7 = (bf16[12,128,1024]{2,1,0:T(8,128)(2,1)}, bf16[12,128,1024]{2,1,0:T(8,128)(2,1)S(1)}, u32[]{:S(2)}, u32[]{:S(2)}) collective-permute-start(bf16[12,128,1024]{2,1,0:T(8,128)(2,1)} %mix_hbm.1), channel_id=1, source_target_pairs={{0,4},{4,0},{8,12},{12,8},{16,20},{20,16},{24,28},{28,24},{1,5},{5... | collective-permute-start | bytes 9437192 | tf_op jit(solution)/shard_map/ppermute | solution.py:20
  0.5 1.2 %norm.1 = (bf16[16,2176]{1,0:T(8,128)(2,1)S(1)}, bf16[16,2176]{1,0:T(8,128)(2,1)S(1)}, bf16[16,2176]{1,0:T(8,128)(2,1)S(1)}, bf16[16,2176]{1,0:T(8,128)(2,1)S(1)}) custom-call(bf16[128,1024]{1,0:T(8,128)(2,1)} %tokens_ref.1, f32[1,1024]{1,0:T(1,128)} %bitcast.1, f32[12,128]{1,0:T(8,128)} %filters_hbm.1), custom_call_target="tpu_custom_call" | custom-call | tf_op jit(solution)/shard_map/norm/pallas_call | solution.py:297
  1.7 3.6 %collective-permute-start = (bf16[16,2176]{1,0:T(8,128)(2,1)S(1)}, bf16[16,2176]{1,0:T(8,128)(2,1)S(1)}, u32[]{:S(2)}, u32[]{:S(2)}) collective-permute-start(bf16[16,2176]{1,0:T(8,128)(2,1)S(1)} %get-tuple-element.15), channel_id=1, source_target_pairs={{0,28},{4,24},{8,20},{12,16},{16,12},{20,8},{24,4},{28,0},{1,29},{... | collective-permute-start | bytes 208904 | tf_op jit(solution)/shard_map/ppermute | solution.py:20
  5.3 0.1 collective-permute-start.1
  5.4 0.1 collective-permute-start.2
  5.6 1.9 %stage.1 = (bf16[12,128,1024]{2,1,0:T(8,128)(2,1)S(1)}, bf16[16,2176]{1,0:T(8,128)(2,1)S(1)}) custom-call(bf16[12,128,1024]{2,1,0:T(8,128)(2,1)} %mix_hbm.1, bf16[16,2176]{1,0:T(8,128)(2,1)S(1)} %get-tuple-element.14.block_ref.refs_0_), custom_call_target="tpu_custom_call" | custom-call | tf_op jit(solution)/shard_map/stage/pallas_call | solution.py:310
  7.5 0.6 %collective-permute-start.3 = (bf16[16,2176]{1,0:T(8,128)(2,1)S(1)}, bf16[16,2176]{1,0:T(8,128)(2,1)S(1)}, u32[]{:S(2)}, u32[]{:S(2)}) collective-permute-start(bf16[16,2176]{1,0:T(8,128)(2,1)S(1)} %get-tuple-element.18), channel_id=1, source_target_pairs={{0,4},{4,0},{8,12},{12,8},{16,20},{20,16},{24,28},{28,24},{1,5},{5... | collective-permute-start | bytes 208904 | tf_op jit(solution)/shard_map/ppermute | solution.py:20
  8.0 0.0 collective-permute-done.refs_1_
  8.0 0.1 collective-permute-start.4
  8.1 1.5 %collective-permute-done.1.refs_2_ = bf16[16,2176]{1,0:T(8,128)(2,1)S(1)} collective-permute-done((bf16[16,2176]{1,0:T(8,128)(2,1)S(1)}, bf16[16,2176]{1,0:T(8,128)(2,1)S(1)}, u32[]{:S(2)}, u32[]{:S(2)}) %collective-permute-start.1) | collective-permute-done | bytes 69664 | tf_op jit(solution)/shard_map/ppermute | solution.py:20
  9.6 0.1 collective-permute-start.5
  9.7 0.0 collective-permute-done.2.refs_3_
  9.7 0.4 %collective-permute-start.6 = (bf16[16,2176]{1,0:T(8,128)(2,1)S(1)}, bf16[16,2176]{1,0:T(8,128)(2,1)S(1)}, u32[]{:S(2)}, u32[]{:S(2)}) collective-permute-start(bf16[16,2176]{1,0:T(8,128)(2,1)S(1)} %collective-permute-done.2.refs_3_), channel_id=1, source_target_pairs={{0,4},{4,0},{8,12},{12,8},{16,20},{20,16},{24,28},{28,24},{1,5},{5... | collective-permute-start | bytes 208904 | tf_op jit(solution)/shard_map/ppermute | solution.py:20
  10.1 0.0 collective-permute-done.3.refs_4_
  10.1 0.0 collective-permute-done.4.refs_5_
  10.1 0.7 %collective-permute-done.5.refs_6_ = bf16[16,2176]{1,0:T(8,128)(2,1)S(1)} collective-permute-done((bf16[16,2176]{1,0:T(8,128)(2,1)S(1)}, bf16[16,2176]{1,0:T(8,128)(2,1)S(1)}, u32[]{:S(2)}, u32[]{:S(2)}) %collective-permute-start.5) | collective-permute-done | bytes 69664 | tf_op jit(solution)/shard_map/ppermute | solution.py:20
  10.9 0.2 collective-permute-done.6.refs_7_
  11.0 0.0 collective-permute-done.7.refs_9_.refs_3_
  11.0 2.4 %merge.1 = (bf16[1152,1024]{1,0:T(8,128)(2,1)S(1)}, bf16[384,1152]{1,0:T(8,128)(2,1)S(1)}, bf16[128,1024]{1,0:T(8,128)(2,1)S(1)}) custom-call(bf16[16,2176]{1,0:T(8,128)(2,1)S(1)} %get-tuple-element.14.block_ref.refs_0_, bf16[16,2176]{1,0:T(8,128)(2,1)S(1)} %collective-permute-done.refs_1_, bf16[16,2176]{1,0:T(8,128)(2,1)S(1)} %collective-permute-done.1.refs_2_, ...), custom_call_target="tpu_custom_call" | custom-call | tf_op jit(solution)/shard_map/merge/pallas_call | solution.py:334
  13.5 1.1 %collective-permute-start.9 = (bf16[128,1024]{1,0:T(8,128)(2,1)S(1)}, bf16[128,1024]{1,0:T(8,128)(2,1)S(1)}, u32[]{:S(2)}, u32[]{:S(2)}) collective-permute-start(bf16[128,1024]{1,0:T(8,128)(2,1)S(1)} %get-tuple-element.22), channel_id=1, source_target_pairs={{0,20},{4,8},{8,28},{12,0},{16,4},{20,24},{24,12},{28,16},{1,21},{... | collective-permute-start | bytes 786440 | tf_op jit(solution)/shard_map/ppermute | solution.py:371
  14.6 1.8 %branch.4 = bf16[128,1024]{1,0:T(8,128)(2,1)S(1)} custom-call(bf16[1152,1024]{1,0:T(8,128)(2,1)S(1)} %get-tuple-element.20.refs_0_, bf16[384,1152]{1,0:T(8,128)(2,1)S(1)} %get-tuple-element.21.refs_1_, bf16[12,128,1024]{2,1,0:T(8,128)(2,1)S(1)} %get-tuple-element.19.refs_8_.refs_2_, bf16[12,128,1024]{2,1,0:T(8,128)(2,1)S(1)} %collective-permute-done.7.refs_9_.refs_3_), custom_call_target="tpu_custom_call" | custom-call | tf_op jit(solution)/shard_map/branch/pallas_call | solution.py:359
  16.4 0.6 %collective-permute-start.8 = (bf16[128,1024]{1,0:T(8,128)(2,1)S(1)}, bf16[128,1024]{1,0:T(8,128)(2,1)S(1)}, u32[]{:S(2)}, u32[]{:S(2)}) collective-permute-start(bf16[128,1024]{1,0:T(8,128)(2,1)S(1)} %branch.4), channel_id=1, source_target_pairs={{0,16},{4,12},{8,24},{12,4},{16,0},{20,28},{24,8},{28,20},{1,17},{... | collective-permute-start | bytes 786440 | tf_op jit(solution)/shard_map/ppermute | solution.py:372
  17.0 1.8 %branch.5 = f32[128,1024]{1,0:T(8,128)S(1)} custom-call(bf16[1152,1024]{1,0:T(8,128)(2,1)S(1)} %get-tuple-element.20.refs_0_, bf16[384,1152]{1,0:T(8,128)(2,1)S(1)} %get-tuple-element.21.refs_1_, bf16[12,128,1024]{2,1,0:T(8,128)(2,1)S(1)} %get-tuple-element.19.refs_8_.refs_2_, bf16[12,128,1024]{2,1,0:T(8,128)(2,1)S(1)} %collective-permute-done.7.refs_9_.refs_3_), custom_call_target="tpu_custom_call" | custom-call | tf_op jit(solution)/shard_map/branch/pallas_call | solution.py:359
  18.7 0.6 %collective-permute-done.9 = bf16[128,1024]{1,0:T(8,128)(2,1)S(1)} collective-permute-done((bf16[128,1024]{1,0:T(8,128)(2,1)S(1)}, bf16[128,1024]{1,0:T(8,128)(2,1)S(1)}, u32[]{:S(2)}, u32[]{:S(2)}) %collective-permute-start.9) | collective-permute-done | bytes 262176 | tf_op jit(solution)/shard_map/ppermute | solution.py:371
  19.3 0.1 add_convert_fusion
  19.4 0.0 copy-start
  19.4 1.1 %collective-permute-start.10 = (bf16[128,1024]{1,0:T(8,128)(2,1)S(1)}, bf16[128,1024]{1,0:T(8,128)(2,1)S(1)}, u32[]{:S(2)}, u32[]{:S(2)}) collective-permute-start(bf16[128,1024]{1,0:T(8,128)(2,1)S(1)} %add_convert_fusion), channel_id=1, source_target_pairs={{0,20},{4,8},{8,28},{12,0},{16,4},{20,24},{24,12},{28,16},{1,21},{... | collective-permute-start | bytes 786440 | tf_op jit(solution)/shard_map/ppermute | solution.py:374
  20.5 1.4 %branch.3.own_ref = f32[128,1024]{1,0:T(8,128)S(1)} custom-call(bf16[1152,1024]{1,0:T(8,128)(2,1)S(1)} %get-tuple-element.20.refs_0_, bf16[384,1152]{1,0:T(8,128)(2,1)S(1)} %get-tuple-element.21.refs_1_, bf16[12,128,1024]{2,1,0:T(8,128)(2,1)S(1)} %get-tuple-element.19.refs_8_.refs_2_, bf16[12,128,1024]{2,1,0:T(8,128)(2,1)S(1)} %collective-permute-done.7.refs_9_.refs_3_), custom_call_target="tpu_custom_call" | custom-call | tf_op jit(solution)/shard_map/branch/pallas_call | solution.py:359
  21.9 0.9 %collective-permute-done.8.early_ref = bf16[128,1024]{1,0:T(8,128)(2,1)S(1)} collective-permute-done((bf16[128,1024]{1,0:T(8,128)(2,1)S(1)}, bf16[128,1024]{1,0:T(8,128)(2,1)S(1)}, u32[]{:S(2)}, u32[]{:S(2)}) %collective-permute-start.8) | collective-permute-done | bytes 262176 | tf_op jit(solution)/shard_map/ppermute | solution.py:372
  22.8 2.4 %collective-permute-done.10.late_ref = bf16[128,1024]{1,0:T(8,128)(2,1)S(1)} collective-permute-done((bf16[128,1024]{1,0:T(8,128)(2,1)S(1)}, bf16[128,1024]{1,0:T(8,128)(2,1)S(1)}, u32[]{:S(2)}, u32[]{:S(2)}) %collective-permute-start.10) | collective-permute-done | bytes 262176 | tf_op jit(solution)/shard_map/ppermute | solution.py:374
  25.2 0.0 copy-done
  25.2 0.8 %finish.1 = bf16[128,1024]{1,0:T(8,128)(2,1)} custom-call(bf16[128,1024]{1,0:T(8,128)(2,1)S(1)} %copy-done, f32[128,1024]{1,0:T(8,128)S(1)} %branch.3.own_ref, bf16[128,1024]{1,0:T(8,128)(2,1)S(1)} %collective-permute-done.8.early_ref, bf16[128,1024]{1,0:T(8,128)(2,1)S(1)} %collective-permute-done.10.late_ref), custom_call_target="tpu_custom_call" | custom-call | tf_op jit(solution)/shard_map/finish/pallas_call | solution.py:375
Async XLA Ops:
  0.0 11.0 %collective-permute-start.7 = (bf16[12,128,1024]{2,1,0:T(8,128)(2,1)}, bf16[12,128,1024]{2,1,0:T(8,128)(2,1)S(1)}, u32[]{:S(2)}, u32[]{:S(2)}) collective-permute-start(bf16[12,128,1024]{2,1,0:T(8,128)(2,1)} %mix_hbm.1), channel_id=1, source_target_pairs={{0,4},{4,0},{8,12},{12,8},{16,20},{20,16},{24,28},{28,24},{1,5},{5... | collective-permute-start | bytes 9437192 | tf_op jit(solution)/shard_map/ppermute | solution.py:20
  1.7 6.4 %collective-permute-start = (bf16[16,2176]{1,0:T(8,128)(2,1)S(1)}, bf16[16,2176]{1,0:T(8,128)(2,1)S(1)}, u32[]{:S(2)}, u32[]{:S(2)}) collective-permute-start(bf16[16,2176]{1,0:T(8,128)(2,1)S(1)} %get-tuple-element.15), channel_id=1, source_target_pairs={{0,28},{4,24},{8,20},{12,16},{16,12},{20,8},{24,4},{28,0},{1,29},{... | collective-permute-start | bytes 208904 | tf_op jit(solution)/shard_map/ppermute | solution.py:20
  5.3 4.3 %collective-permute-start.1 = (bf16[16,2176]{1,0:T(8,128)(2,1)S(1)}, bf16[16,2176]{1,0:T(8,128)(2,1)S(1)}, u32[]{:S(2)}, u32[]{:S(2)}) collective-permute-start(bf16[16,2176]{1,0:T(8,128)(2,1)S(1)} %get-tuple-element.16), channel_id=1, source_target_pairs={{0,20},{4,16},{8,28},{12,24},{16,4},{20,0},{24,12},{28,8},{1,21},{... | collective-permute-start | bytes 208904 | tf_op jit(solution)/shard_map/ppermute | solution.py:20
  5.4 4.3 %collective-permute-start.2 = (bf16[16,2176]{1,0:T(8,128)(2,1)S(1)}, bf16[16,2176]{1,0:T(8,128)(2,1)S(1)}, u32[]{:S(2)}, u32[]{:S(2)}) collective-permute-start(bf16[16,2176]{1,0:T(8,128)(2,1)S(1)} %get-tuple-element.17), channel_id=1, source_target_pairs={{0,12},{4,8},{8,4},{12,0},{16,28},{20,24},{24,20},{28,16},{1,13},{... | collective-permute-start | bytes 208904 | tf_op jit(solution)/shard_map/ppermute | solution.py:20
  7.5 2.7 %collective-permute-start.3 = (bf16[16,2176]{1,0:T(8,128)(2,1)S(1)}, bf16[16,2176]{1,0:T(8,128)(2,1)S(1)}, u32[]{:S(2)}, u32[]{:S(2)}) collective-permute-start(bf16[16,2176]{1,0:T(8,128)(2,1)S(1)} %get-tuple-element.18), channel_id=1, source_target_pairs={{0,4},{4,0},{8,12},{12,8},{16,20},{20,16},{24,28},{28,24},{1,5},{5... | collective-permute-start | bytes 208904 | tf_op jit(solution)/shard_map/ppermute | solution.py:20
  8.0 2.1 %collective-permute-start.4 = (bf16[16,2176]{1,0:T(8,128)(2,1)S(1)}, bf16[16,2176]{1,0:T(8,128)(2,1)S(1)}, u32[]{:S(2)}, u32[]{:S(2)}) collective-permute-start(bf16[16,2176]{1,0:T(8,128)(2,1)S(1)} %collective-permute-done.refs_1_), channel_id=1, source_target_pairs={{0,4},{4,0},{8,12},{12,8},{16,20},{20,16},{24,28},{28,24},{1,5},{5... | collective-permute-start | bytes 208904 | tf_op jit(solution)/shard_map/ppermute | solution.py:20
  9.6 1.3 %collective-permute-start.5 = (bf16[16,2176]{1,0:T(8,128)(2,1)S(1)}, bf16[16,2176]{1,0:T(8,128)(2,1)S(1)}, u32[]{:S(2)}, u32[]{:S(2)}) collective-permute-start(bf16[16,2176]{1,0:T(8,128)(2,1)S(1)} %collective-permute-done.1.refs_2_), channel_id=1, source_target_pairs={{0,4},{4,0},{8,12},{12,8},{16,20},{20,16},{24,28},{28,24},{1,5},{5... | collective-permute-start | bytes 208904 | tf_op jit(solution)/shard_map/ppermute | solution.py:20
  9.7 1.3 %collective-permute-start.6 = (bf16[16,2176]{1,0:T(8,128)(2,1)S(1)}, bf16[16,2176]{1,0:T(8,128)(2,1)S(1)}, u32[]{:S(2)}, u32[]{:S(2)}) collective-permute-start(bf16[16,2176]{1,0:T(8,128)(2,1)S(1)} %collective-permute-done.2.refs_3_), channel_id=1, source_target_pairs={{0,4},{4,0},{8,12},{12,8},{16,20},{20,16},{24,28},{28,24},{1,5},{5... | collective-permute-start | bytes 208904 | tf_op jit(solution)/shard_map/ppermute | solution.py:20
  13.5 5.8 %collective-permute-start.9 = (bf16[128,1024]{1,0:T(8,128)(2,1)S(1)}, bf16[128,1024]{1,0:T(8,128)(2,1)S(1)}, u32[]{:S(2)}, u32[]{:S(2)}) collective-permute-start(bf16[128,1024]{1,0:T(8,128)(2,1)S(1)} %get-tuple-element.22), channel_id=1, source_target_pairs={{0,20},{4,8},{8,28},{12,0},{16,4},{20,24},{24,12},{28,16},{1,21},{... | collective-permute-start | bytes 786440 | tf_op jit(solution)/shard_map/ppermute | solution.py:371
  16.4 6.4 %collective-permute-start.8 = (bf16[128,1024]{1,0:T(8,128)(2,1)S(1)}, bf16[128,1024]{1,0:T(8,128)(2,1)S(1)}, u32[]{:S(2)}, u32[]{:S(2)}) collective-permute-start(bf16[128,1024]{1,0:T(8,128)(2,1)S(1)} %branch.4), channel_id=1, source_target_pairs={{0,16},{4,12},{8,24},{12,4},{16,0},{20,28},{24,8},{28,20},{1,17},{... | collective-permute-start | bytes 786440 | tf_op jit(solution)/shard_map/ppermute | solution.py:372
  19.4 5.9 %copy-start = (bf16[128,1024]{1,0:T(8,128)(2,1)S(1)}, bf16[128,1024]{1,0:T(8,128)(2,1)}, u32[]{:S(2)}) copy-start(bf16[128,1024]{1,0:T(8,128)(2,1)} %tokens_ref.1) | copy-start | bytes 786436
  19.4 5.8 %collective-permute-start.10 = (bf16[128,1024]{1,0:T(8,128)(2,1)S(1)}, bf16[128,1024]{1,0:T(8,128)(2,1)S(1)}, u32[]{:S(2)}, u32[]{:S(2)}) collective-permute-start(bf16[128,1024]{1,0:T(8,128)(2,1)S(1)} %add_convert_fusion), channel_id=1, source_target_pairs={{0,20},{4,8},{8,28},{12,0},{16,4},{20,24},{24,12},{28,16},{1,21},{... | collective-permute-start | bytes 786440 | tf_op jit(solution)/shard_map/ppermute | solution.py:374

commit v9 on v8

--- a/solution.py
+++ b/solution.py
@@ -86,14 +86,12 @@
     copy.wait()
 
 
-def finish_kernel(tokens_ref, own_ref, early_ref, late_ref, out_hbm, held, sems):
+def finish_kernel(own_ref, late_ref, out_hbm, held, sems):
     chunk = held.shape[0] // PARTS
     copies = []
     for i in range(PARTS):
         cut = pl.ds(i * chunk, chunk)
-        total = tokens_ref[cut, :].astype(jnp.float32) + own_ref[cut, :]
-        total = total + early_ref[cut, :].astype(jnp.float32)
-        held[cut, :] = (total + late_ref[cut, :].astype(jnp.float32)).astype(held.dtype)
+        held[cut, :] = (own_ref[cut, :] + late_ref[cut, :].astype(jnp.float32)).astype(held.dtype)
         copies.append(pltpu.make_async_copy(held.at[cut], out_hbm.at[cut], sems.at[i]))
         copies[-1].start()
     for copy in copies:
@@ -237,7 +235,7 @@
 
 
 def branch_kernel(chips, rows, fine, kind, *refs):
-    signal, strip, mix_ref, pair_mix_ref, out_ref, feats = refs
+    signal, strip, mix_ref, pair_mix_ref, *more, out_ref, feats = refs
     index = lax.axis_index("seq")
     other, part = aim(index // 2, index % 2, kind)
     devices = 2 * chips
@@ -254,6 +252,8 @@
     for steps in range(1, chips + 1):
         pl.when(other == steps - 1)(functools.partial(convolve, steps))
     total = project(feats, mix_ref, pair_mix_ref)
+    for ref in more:
+        total = total + ref[...].astype(jnp.float32)
     out_ref[...] = total.astype(out_ref.dtype)
 
 
@@ -355,15 +355,15 @@
     fixed = [signal, strip, near_mixing, pair_mixing]
     if relay:
 
-        def branch(kind, dtype):
+        def branch(kind, dtype, *more):
             return kernel_call(
                 functools.partial(branch_kernel, chips, rows, fine, kind),
                 "branch",
                 jax.ShapeDtypeStruct((rows, width), dtype),
-                [VMEM] * 4,
+                [VMEM] * (4 + len(more)),
                 24 * MIB,
                 [pltpu.VMEM((rows, num * count), jnp.bfloat16)],
-            )(*fixed)
+            )(*fixed, *more)
 
         pairs = [(c, q) for c in range(chips) for q in range(2)]
         across = [(2 * c + q, 2 * (c ^ (2 - q)) + 1 - q) for c, q in pairs]
@@ -375,7 +375,7 @@
         return pl.pallas_call(
             finish_kernel,
             out_shape=jax.ShapeDtypeStruct((rows, width), tokens.dtype),
-            in_specs=[VMEM] * 4,
+            in_specs=[VMEM] * 2,
             out_specs=HBM,
             scratch_shapes=[
                 pltpu.VMEM((rows, width), tokens.dtype),
@@ -383,7 +383,7 @@
             ],
             compiler_params=pltpu.CompilerParams(vmem_limit_bytes=8 * MIB),
             name="finish",
-        )(tokens, branch("own", jnp.float32), early, late)
+        )(branch("own", jnp.float32, tokens, early), late)
     else:
 
         def branch(shift):

time: 26.2 us -> 26.2 us (level)
    ppermute x1, waiting for transfers between devices: 2.45 us -> 1.03 us  [local(): late = lax.ppermute(late, 'seq', across)]
    ppermute x1, waiting for transfers between devices: 0.93 us -> 2.33 us  [local(): early = lax.ppermute(branch('early', jnp.bfloat16), 'seq', along)]
where the time goes in v9:
time: 26.2 us; the launch traced here: 26 us
  Pallas kernels  11.2 us (43%)
  starting transfers between devices  8.28 us (32%)
  waiting for transfers between devices  6.32 us (24%)
    ppermute x8, starting transfers between devices, swap(): return lax.ppermute(value, 'seq', [(i, i ^ bits) for i in range(size)])  5.49 us
    pallas_call x3, Pallas kernels, branch(): kernel_call(functools.partial(branch_kernel, chips, rows, fine, kind), 'b...  4.94 us
    pallas_call x1, Pallas kernels, local(): kernel_call(functools.partial(merge_kernel, chips, shifts, rows, num, fin...  2.44 us
    ppermute x8, waiting for transfers between devices, swap(): return lax.ppermute(value, 'seq', [(i, i ^ bits) for i in range(size)])  2.39 us
    ppermute x1, waiting for transfers between devices, local(): early = lax.ppermute(branch('early', jnp.bfloat16), 'seq', along)  2.33 us
    pallas_call x1, Pallas kernels, local(): kernel_call(stage_kernel, 'stage', [jax.ShapeDtypeStruct(mixing.shape, mi...  1.9 us
    pallas_call x1, Pallas kernels, local(): kernel_call(norm_kernel, 'norm', [jax.ShapeDtypeStruct(flat, jnp.bfloat16...  1.22 us
    ppermute x1, starting transfers between devices, local(): far = lax.ppermute(far, 'seq', across)  1.1 us
  transfers between devices with their start and end apart: 11, of which 6 were waited for; matrix products, arithmetic and copies ran while one was open for 0% of the time, Pallas kernels for 31%

profile of v9, /device:TPU:0, one launch (start us, length us, event | category | flops | bytes accessed | tf_op | source)
XLA Modules:
  0.0 26.0 jit_solution(6736347905136004285)
XLA Ops:
  0.0 0.5 %collective-permute-start.7 = (bf16[12,128,1024]{2,1,0:T(8,128)(2,1)}, bf16[12,128,1024]{2,1,0:T(8,128)(2,1)S(1)}, u32[]{:S(2)}, u32[]{:S(2)}) collective-permute-start(bf16[12,128,1024]{2,1,0:T(8,128)(2,1)} %mix_hbm.1), channel_id=1, source_target_pairs={{0,4},{4,0},{8,12},{12,8},{16,20},{20,16},{24,28},{28,24},{1,5},{5... | collective-permute-start | bytes 9437192 | tf_op jit(solution)/shard_map/ppermute | solution.py:20
  0.5 1.2 %norm.1 = (bf16[16,2176]{1,0:T(8,128)(2,1)S(1)}, bf16[16,2176]{1,0:T(8,128)(2,1)S(1)}, bf16[16,2176]{1,0:T(8,128)(2,1)S(1)}, bf16[16,2176]{1,0:T(8,128)(2,1)S(1)}) custom-call(bf16[128,1024]{1,0:T(8,128)(2,1)} %refs_4_.1, f32[1,1024]{1,0:T(1,128)} %bitcast.1, f32[12,128]{1,0:T(8,128)} %filters_hbm.1), custom_call_target="tpu_custom_call" | custom-call | tf_op jit(solution)/shard_map/norm/pallas_call | solution.py:297
  1.7 3.6 %collective-permute-start = (bf16[16,2176]{1,0:T(8,128)(2,1)S(1)}, bf16[16,2176]{1,0:T(8,128)(2,1)S(1)}, u32[]{:S(2)}, u32[]{:S(2)}) collective-permute-start(bf16[16,2176]{1,0:T(8,128)(2,1)S(1)} %get-tuple-element.15), channel_id=1, source_target_pairs={{0,28},{4,24},{8,20},{12,16},{16,12},{20,8},{24,4},{28,0},{1,29},{... | collective-permute-start | bytes 208904 | tf_op jit(solution)/shard_map/ppermute | solution.py:20
  5.3 0.1 collective-permute-start.1
  5.4 0.1 collective-permute-start.2
  5.6 1.9 %stage.1 = (bf16[12,128,1024]{2,1,0:T(8,128)(2,1)S(1)}, bf16[16,2176]{1,0:T(8,128)(2,1)S(1)}) custom-call(bf16[12,128,1024]{2,1,0:T(8,128)(2,1)} %mix_hbm.1, bf16[16,2176]{1,0:T(8,128)(2,1)S(1)} %get-tuple-element.14.block_ref.refs_0_), custom_call_target="tpu_custom_call" | custom-call | tf_op jit(solution)/shard_map/stage/pallas_call | solution.py:310
  7.5 0.6 %collective-permute-start.3 = (bf16[16,2176]{1,0:T(8,128)(2,1)S(1)}, bf16[16,2176]{1,0:T(8,128)(2,1)S(1)}, u32[]{:S(2)}, u32[]{:S(2)}) collective-permute-start(bf16[16,2176]{1,0:T(8,128)(2,1)S(1)} %get-tuple-element.18), channel_id=1, source_target_pairs={{0,4},{4,0},{8,12},{12,8},{16,20},{20,16},{24,28},{28,24},{1,5},{5... | collective-permute-start | bytes 208904 | tf_op jit(solution)/shard_map/ppermute | solution.py:20
  8.0 0.0 collective-permute-done.refs_1_
  8.0 0.1 collective-permute-start.4
  8.1 1.5 %collective-permute-done.1.refs_2_ = bf16[16,2176]{1,0:T(8,128)(2,1)S(1)} collective-permute-done((bf16[16,2176]{1,0:T(8,128)(2,1)S(1)}, bf16[16,2176]{1,0:T(8,128)(2,1)S(1)}, u32[]{:S(2)}, u32[]{:S(2)}) %collective-permute-start.1) | collective-permute-done | bytes 69664 | tf_op jit(solution)/shard_map/ppermute | solution.py:20
  9.6 0.1 collective-permute-start.5
  9.7 0.0 collective-permute-done.2.refs_3_
  9.7 0.4 %collective-permute-start.6 = (bf16[16,2176]{1,0:T(8,128)(2,1)S(1)}, bf16[16,2176]{1,0:T(8,128)(2,1)S(1)}, u32[]{:S(2)}, u32[]{:S(2)}) collective-permute-start(bf16[16,2176]{1,0:T(8,128)(2,1)S(1)} %collective-permute-done.2.refs_3_), channel_id=1, source_target_pairs={{0,4},{4,0},{8,12},{12,8},{16,20},{20,16},{24,28},{28,24},{1,5},{5... | collective-permute-start | bytes 208904 | tf_op jit(solution)/shard_map/ppermute | solution.py:20
  10.1 0.0 collective-permute-done.3.refs_4_
  10.1 0.0 collective-permute-done.4.refs_5_
  10.1 0.7 %collective-permute-done.5.refs_6_ = bf16[16,2176]{1,0:T(8,128)(2,1)S(1)} collective-permute-done((bf16[16,2176]{1,0:T(8,128)(2,1)S(1)}, bf16[16,2176]{1,0:T(8,128)(2,1)S(1)}, u32[]{:S(2)}, u32[]{:S(2)}) %collective-permute-start.5) | collective-permute-done | bytes 69664 | tf_op jit(solution)/shard_map/ppermute | solution.py:20
  10.9 0.2 collective-permute-done.6.refs_7_
  11.0 0.0 collective-permute-done.7.refs_9_.refs_3_
  11.0 2.4 %merge.1 = (bf16[1152,1024]{1,0:T(8,128)(2,1)S(1)}, bf16[384,1152]{1,0:T(8,128)(2,1)S(1)}, bf16[128,1024]{1,0:T(8,128)(2,1)S(1)}) custom-call(bf16[16,2176]{1,0:T(8,128)(2,1)S(1)} %get-tuple-element.14.block_ref.refs_0_, bf16[16,2176]{1,0:T(8,128)(2,1)S(1)} %collective-permute-done.refs_1_, bf16[16,2176]{1,0:T(8,128)(2,1)S(1)} %collective-permute-done.1.refs_2_, ...), custom_call_target="tpu_custom_call" | custom-call | tf_op jit(solution)/shard_map/merge/pallas_call | solution.py:334
  13.5 1.1 %collective-permute-start.9 = (bf16[128,1024]{1,0:T(8,128)(2,1)S(1)}, bf16[128,1024]{1,0:T(8,128)(2,1)S(1)}, u32[]{:S(2)}, u32[]{:S(2)}) collective-permute-start(bf16[128,1024]{1,0:T(8,128)(2,1)S(1)} %get-tuple-element.22), channel_id=1, source_target_pairs={{0,20},{4,8},{8,28},{12,0},{16,4},{20,24},{24,12},{28,16},{1,21},{... | collective-permute-start | bytes 786440 | tf_op jit(solution)/shard_map/ppermute | solution.py:371
  14.6 1.8 %branch.3 = bf16[128,1024]{1,0:T(8,128)(2,1)S(1)} custom-call(bf16[1152,1024]{1,0:T(8,128)(2,1)S(1)} %get-tuple-element.20.refs_0_, bf16[384,1152]{1,0:T(8,128)(2,1)S(1)} %get-tuple-element.21.refs_1_, bf16[12,128,1024]{2,1,0:T(8,128)(2,1)S(1)} %get-tuple-element.19.refs_8_.refs_2_, bf16[12,128,1024]{2,1,0:T(8,128)(2,1)S(1)} %collective-permute-done.7.refs_9_.refs_3_), custom_call_target="tpu_custom_call" | custom-call | tf_op jit(solution)/shard_map/branch/pallas_call | solution.py:359
  16.4 0.0 copy-start
  16.4 0.6 %collective-permute-start.8 = (bf16[128,1024]{1,0:T(8,128)(2,1)S(1)}, bf16[128,1024]{1,0:T(8,128)(2,1)S(1)}, u32[]{:S(2)}, u32[]{:S(2)}) collective-permute-start(bf16[128,1024]{1,0:T(8,128)(2,1)S(1)} %branch.3), channel_id=1, source_target_pairs={{0,16},{4,12},{8,24},{12,4},{16,0},{20,28},{24,8},{28,20},{1,17},{... | collective-permute-start | bytes 786440 | tf_op jit(solution)/shard_map/ppermute | solution.py:372
  17.0 1.8 %branch.5 = f32[128,1024]{1,0:T(8,128)S(1)} custom-call(bf16[1152,1024]{1,0:T(8,128)(2,1)S(1)} %get-tuple-element.20.refs_0_, bf16[384,1152]{1,0:T(8,128)(2,1)S(1)} %get-tuple-element.21.refs_1_, bf16[12,128,1024]{2,1,0:T(8,128)(2,1)S(1)} %get-tuple-element.19.refs_8_.refs_2_, bf16[12,128,1024]{2,1,0:T(8,128)(2,1)S(1)} %collective-permute-done.7.refs_9_.refs_3_), custom_call_target="tpu_custom_call" | custom-call | tf_op jit(solution)/shard_map/branch/pallas_call | solution.py:359
  18.7 0.6 %collective-permute-done.9 = bf16[128,1024]{1,0:T(8,128)(2,1)S(1)} collective-permute-done((bf16[128,1024]{1,0:T(8,128)(2,1)S(1)}, bf16[128,1024]{1,0:T(8,128)(2,1)S(1)}, u32[]{:S(2)}, u32[]{:S(2)}) %collective-permute-start.9) | collective-permute-done | bytes 262176 | tf_op jit(solution)/shard_map/ppermute | solution.py:371
  19.3 0.1 add_convert_fusion
  19.4 1.1 %collective-permute-start.10 = (bf16[128,1024]{1,0:T(8,128)(2,1)S(1)}, bf16[128,1024]{1,0:T(8,128)(2,1)S(1)}, u32[]{:S(2)}, u32[]{:S(2)}) collective-permute-start(bf16[128,1024]{1,0:T(8,128)(2,1)S(1)} %add_convert_fusion), channel_id=1, source_target_pairs={{0,20},{4,8},{8,28},{12,0},{16,4},{20,24},{24,12},{28,16},{1,21},{... | collective-permute-start | bytes 786440 | tf_op jit(solution)/shard_map/ppermute | solution.py:374
  20.5 2.3 %collective-permute-done.8.refs_5_ = bf16[128,1024]{1,0:T(8,128)(2,1)S(1)} collective-permute-done((bf16[128,1024]{1,0:T(8,128)(2,1)S(1)}, bf16[128,1024]{1,0:T(8,128)(2,1)S(1)}, u32[]{:S(2)}, u32[]{:S(2)}) %collective-permute-start.8) | collective-permute-done | bytes 262176 | tf_op jit(solution)/shard_map/ppermute | solution.py:372
  22.8 0.0 copy-done
  22.8 1.4 %branch.4.own_ref = f32[128,1024]{1,0:T(8,128)S(1)} custom-call(bf16[1152,1024]{1,0:T(8,128)(2,1)S(1)} %get-tuple-element.20.refs_0_, bf16[384,1152]{1,0:T(8,128)(2,1)S(1)} %get-tuple-element.21.refs_1_, bf16[12,128,1024]{2,1,0:T(8,128)(2,1)S(1)} %get-tuple-element.19.refs_8_.refs_2_, bf16[12,128,1024]{2,1,0:T(8,128)(2,1)S(1)} %collective-permute-done.7.refs_9_.refs_3_, ...), custom_call_target="tpu_custom_call" | custom-call | tf_op jit(solution)/shard_map/branch/pallas_call | solution.py:359
  24.2 1.0 %collective-permute-done.10.late_ref = bf16[128,1024]{1,0:T(8,128)(2,1)S(1)} collective-permute-done((bf16[128,1024]{1,0:T(8,128)(2,1)S(1)}, bf16[128,1024]{1,0:T(8,128)(2,1)S(1)}, u32[]{:S(2)}, u32[]{:S(2)}) %collective-permute-start.10) | collective-permute-done | bytes 262176 | tf_op jit(solution)/shard_map/ppermute | solution.py:374
  25.2 0.7 %finish.1 = bf16[128,1024]{1,0:T(8,128)(2,1)} custom-call(f32[128,1024]{1,0:T(8,128)S(1)} %branch.4.own_ref, bf16[128,1024]{1,0:T(8,128)(2,1)S(1)} %collective-permute-done.10.late_ref), custom_call_target="tpu_custom_call" | custom-call | tf_op jit(solution)/shard_map/finish/pallas_call | solution.py:375
Async XLA Ops:
  0.0 11.0 %collective-permute-start.7 = (bf16[12,128,1024]{2,1,0:T(8,128)(2,1)}, bf16[12,128,1024]{2,1,0:T(8,128)(2,1)S(1)}, u32[]{:S(2)}, u32[]{:S(2)}) collective-permute-start(bf16[12,128,1024]{2,1,0:T(8,128)(2,1)} %mix_hbm.1), channel_id=1, source_target_pairs={{0,4},{4,0},{8,12},{12,8},{16,20},{20,16},{24,28},{28,24},{1,5},{5... | collective-permute-start | bytes 9437192 | tf_op jit(solution)/shard_map/ppermute | solution.py:20
  1.7 6.4 %collective-permute-start = (bf16[16,2176]{1,0:T(8,128)(2,1)S(1)}, bf16[16,2176]{1,0:T(8,128)(2,1)S(1)}, u32[]{:S(2)}, u32[]{:S(2)}) collective-permute-start(bf16[16,2176]{1,0:T(8,128)(2,1)S(1)} %get-tuple-element.15), channel_id=1, source_target_pairs={{0,28},{4,24},{8,20},{12,16},{16,12},{20,8},{24,4},{28,0},{1,29},{... | collective-permute-start | bytes 208904 | tf_op jit(solution)/shard_map/ppermute | solution.py:20
  5.3 4.3 %collective-permute-start.1 = (bf16[16,2176]{1,0:T(8,128)(2,1)S(1)}, bf16[16,2176]{1,0:T(8,128)(2,1)S(1)}, u32[]{:S(2)}, u32[]{:S(2)}) collective-permute-start(bf16[16,2176]{1,0:T(8,128)(2,1)S(1)} %get-tuple-element.16), channel_id=1, source_target_pairs={{0,20},{4,16},{8,28},{12,24},{16,4},{20,0},{24,12},{28,8},{1,21},{... | collective-permute-start | bytes 208904 | tf_op jit(solution)/shard_map/ppermute | solution.py:20
  5.4 4.3 %collective-permute-start.2 = (bf16[16,2176]{1,0:T(8,128)(2,1)S(1)}, bf16[16,2176]{1,0:T(8,128)(2,1)S(1)}, u32[]{:S(2)}, u32[]{:S(2)}) collective-permute-start(bf16[16,2176]{1,0:T(8,128)(2,1)S(1)} %get-tuple-element.17), channel_id=1, source_target_pairs={{0,12},{4,8},{8,4},{12,0},{16,28},{20,24},{24,20},{28,16},{1,13},{... | collective-permute-start | bytes 208904 | tf_op jit(solution)/shard_map/ppermute | solution.py:20
  7.5 2.7 %collective-permute-start.3 = (bf16[16,2176]{1,0:T(8,128)(2,1)S(1)}, bf16[16,2176]{1,0:T(8,128)(2,1)S(1)}, u32[]{:S(2)}, u32[]{:S(2)}) collective-permute-start(bf16[16,2176]{1,0:T(8,128)(2,1)S(1)} %get-tuple-element.18), channel_id=1, source_target_pairs={{0,4},{4,0},{8,12},{12,8},{16,20},{20,16},{24,28},{28,24},{1,5},{5... | collective-permute-start | bytes 208904 | tf_op jit(solution)/shard_map/ppermute | solution.py:20
  8.0 2.1 %collective-permute-start.4 = (bf16[16,2176]{1,0:T(8,128)(2,1)S(1)}, bf16[16,2176]{1,0:T(8,128)(2,1)S(1)}, u32[]{:S(2)}, u32[]{:S(2)}) collective-permute-start(bf16[16,2176]{1,0:T(8,128)(2,1)S(1)} %collective-permute-done.refs_1_), channel_id=1, source_target_pairs={{0,4},{4,0},{8,12},{12,8},{16,20},{20,16},{24,28},{28,24},{1,5},{5... | collective-permute-start | bytes 208904 | tf_op jit(solution)/shard_map/ppermute | solution.py:20
  9.6 1.3 %collective-permute-start.5 = (bf16[16,2176]{1,0:T(8,128)(2,1)S(1)}, bf16[16,2176]{1,0:T(8,128)(2,1)S(1)}, u32[]{:S(2)}, u32[]{:S(2)}) collective-permute-start(bf16[16,2176]{1,0:T(8,128)(2,1)S(1)} %collective-permute-done.1.refs_2_), channel_id=1, source_target_pairs={{0,4},{4,0},{8,12},{12,8},{16,20},{20,16},{24,28},{28,24},{1,5},{5... | collective-permute-start | bytes 208904 | tf_op jit(solution)/shard_map/ppermute | solution.py:20
  9.7 1.3 %collective-permute-start.6 = (bf16[16,2176]{1,0:T(8,128)(2,1)S(1)}, bf16[16,2176]{1,0:T(8,128)(2,1)S(1)}, u32[]{:S(2)}, u32[]{:S(2)}) collective-permute-start(bf16[16,2176]{1,0:T(8,128)(2,1)S(1)} %collective-permute-done.2.refs_3_), channel_id=1, source_target_pairs={{0,4},{4,0},{8,12},{12,8},{16,20},{20,16},{24,28},{28,24},{1,5},{5... | collective-permute-start | bytes 208904 | tf_op jit(solution)/shard_map/ppermute | solution.py:20
  13.5 5.8 %collective-permute-start.9 = (bf16[128,1024]{1,0:T(8,128)(2,1)S(1)}, bf16[128,1024]{1,0:T(8,128)(2,1)S(1)}, u32[]{:S(2)}, u32[]{:S(2)}) collective-permute-start(bf16[128,1024]{1,0:T(8,128)(2,1)S(1)} %get-tuple-element.22), channel_id=1, source_target_pairs={{0,20},{4,8},{8,28},{12,0},{16,4},{20,24},{24,12},{28,16},{1,21},{... | collective-permute-start | bytes 786440 | tf_op jit(solution)/shard_map/ppermute | solution.py:371
  16.4 6.5 %copy-start = (bf16[128,1024]{1,0:T(8,128)(2,1)S(1)}, bf16[128,1024]{1,0:T(8,128)(2,1)}, u32[]{:S(2)}) copy-start(bf16[128,1024]{1,0:T(8,128)(2,1)} %refs_4_.1) | copy-start | bytes 786436
  16.4 6.4 %collective-permute-start.8 = (bf16[128,1024]{1,0:T(8,128)(2,1)S(1)}, bf16[128,1024]{1,0:T(8,128)(2,1)S(1)}, u32[]{:S(2)}, u32[]{:S(2)}) collective-permute-start(bf16[128,1024]{1,0:T(8,128)(2,1)S(1)} %branch.3), channel_id=1, source_target_pairs={{0,16},{4,12},{8,24},{12,4},{16,0},{20,28},{24,8},{28,20},{1,17},{... | collective-permute-start | bytes 786440 | tf_op jit(solution)/shard_map/ppermute | solution.py:372
  19.4 5.8 %collective-permute-start.10 = (bf16[128,1024]{1,0:T(8,128)(2,1)S(1)}, bf16[128,1024]{1,0:T(8,128)(2,1)S(1)}, u32[]{:S(2)}, u32[]{:S(2)}) collective-permute-start(bf16[128,1024]{1,0:T(8,128)(2,1)S(1)} %add_convert_fusion), channel_id=1, source_target_pairs={{0,20},{4,8},{8,28},{12,0},{16,4},{20,24},{24,12},{28,16},{1,21},{... | collective-permute-start | bytes 786440 | tf_op jit(solution)/shard_map/ppermute | solution.py:374
